TPU v7x, 32 devices: a whole 2x2x4 slice. The times are simulated.
32 devices in a mesh: dp: 8 (over z, x), expert: 4 (over y, core).
Axes of the slice: x: 2, y: 2, z: 4, core: 2. Of those that a mesh axis runs over, the one named last changes fastest.
Arguments:
- tokens: bfloat16 [10240, 1536], P(('dp', 'expert')), may hold values from -6 to 6
- w_query: bfloat16 [1536, 1536], P(('dp', 'expert')), may hold values from -0.15625 to 0.15625
- w_key: bfloat16 [1536, 512], P(('dp', 'expert')), may hold values from -0.15625 to 0.15625
- w_value: bfloat16 [1536, 512], P(('dp', 'expert')), may hold values from -0.15625 to 0.15625
- w_out: bfloat16 [1536, 1536], P(('dp', 'expert')), may hold values from -0.625 to 0.625
- w_router: bfloat16 [1536, 40], P(('dp', 'expert')), may hold values from -0.078125 to 0.078125
- gain_attn: bfloat16 [1536], P(('dp', 'expert')), may hold values from 0.099609375 to 1.8984375
- gain_moe: bfloat16 [1536], P(('dp', 'expert')), may hold values from 0.099609375 to 1.8984375
- w_gate: bfloat16 [40, 1536, 512], P('expert'), may hold values from -0.15625 to 0.15625
- w_up: bfloat16 [40, 1536, 512], P('expert'), may hold values from -0.15625 to 0.15625
- w_down: bfloat16 [40, 512, 1536], P('expert'), may hold values from -0.75 to 0.75
- segments: int32 [10240], P('dp'), may hold values from 0 to 1279, as said below
- routes: int32 [10240, 8], P(('dp', 'expert')), may hold values from 0 to 39, all different within a row
- priority: int32 [10240, 8], P(('dp', 'expert')), may hold values from 0 to 7, each once within a row
- cotangent: bfloat16 [10240, 1536], P(('dp', 'expert')), may hold values from -6 to 6
Outputs:
- outputs: bfloat16 [10240, 1536], P(('dp', 'expert'))
- grad_tokens: float32 [10240, 1536], P(('dp', 'expert'))
- grad_query: float32 [1536, 1536], P(('dp', 'expert'))
- grad_key: float32 [1536, 512], P(('dp', 'expert'))
- grad_value: float32 [1536, 512], P(('dp', 'expert'))
- grad_out: float32 [1536, 1536], P(('dp', 'expert'))
- grad_router: float32 [1536, 40], P(('dp', 'expert'))
- grad_gain_attn: float32 [1536], P(('dp', 'expert'))
- grad_gain_moe: float32 [1536], P(('dp', 'expert'))
- grad_gate: float32 [40, 1536, 512], P('expert', 'dp')
- grad_up: float32 [40, 1536, 512], P('expert', 'dp')
- grad_down: float32 [40, 512, 1536], P('expert', 'dp')
Inputs may be any that keep to these rules, and one draw needn't show every extreme that they name: `segments`: within each sequence of 1280 tokens, a token's segment number is the position in that sequence of its segment's first token; the last position of a sequence starts a segment. `routes`: each token names 8 different experts; every expert is named by some token. `priority`: each token's row holds every rank once.
All inputs are finite; a program needn't handle non-finite values.
Results may differ from a plain program's by a relative error of at most 0.017.
Values may be sent and summed in bfloat16 or wider, within the bound.
A program may use at most 320 MiB of HBM per device.

v0:
```python
import jax
import jax.numpy as jnp
from jax import lax
from jax.sharding import PartitionSpec as P

HD = 64


epsilon = 1e-06
rope_base = 10000.0
masked_score = -1e30


def norm_parts(values, gain_row):
    scaling = lax.rsqrt(jnp.mean(values * values, axis=-1, keepdims=True) + epsilon)
    normed = values * scaling
    return (normed * gain_row, normed, scaling)


def norm_back(grad_rows, normed, scaling, gain_row):
    grad_normed = grad_rows * gain_row
    grad_gain = jnp.sum(grad_rows * normed, axis=0)
    inner_sum = jnp.mean(grad_normed * normed, axis=-1, keepdims=True)
    return (scaling * (grad_normed - normed * inner_sum), grad_gain)


def rope_tables(positions, head_size):
    frequency = rope_base ** (-2.0 * jnp.arange(head_size // 2, dtype=jnp.float32) / head_size)
    angles = positions.astype(jnp.float32)[:, None] * frequency[None, :]
    return (jnp.cos(angles), jnp.sin(angles))


def rotate(vectors, cosine, sine_part):
    halfway = vectors.shape[-1] // 2
    first_half = vectors[..., :halfway]
    second_half = vectors[..., halfway:]
    cos_rows = cosine[:, None, :]
    sin_rows = sine_part[:, None, :]
    return jnp.concatenate(
        [
            first_half * cos_rows - second_half * sin_rows,
            second_half * cos_rows + first_half * sin_rows,
        ],
        axis=-1,
    )


def slot_table(routes, priority, experts, capacity):
    top_count = routes.shape[1]
    expert_hot = (routes[:, :, None] == jnp.arange(experts, dtype=jnp.int32)[None, None, :]).astype(
        jnp.int32
    )
    rank_hot = (
        priority[:, :, None] == jnp.arange(top_count, dtype=jnp.int32)[None, None, :]
    ).astype(jnp.int32)
    per_rank = jnp.einsum("tkr,tke->rte", rank_hot, expert_hot)
    flat_hot = per_rank.reshape(top_count * routes.shape[0], experts)
    earlier = (jnp.cumsum(flat_hot, axis=0, dtype=jnp.int32) - flat_hot).reshape(per_rank.shape)
    slot_ids = jnp.einsum("tkr,tke,rte->tk", rank_hot, expert_hot, earlier)
    return (slot_ids, slot_ids < capacity)


def slot_values(routes, slot_ids, kept_pairs, values, fill_value, experts, capacity):
    target = jnp.where(kept_pairs, routes * capacity + slot_ids, experts * capacity)
    blank_slots = jnp.full((experts * capacity,), fill_value, dtype=values.dtype)
    return blank_slots.at[target.reshape(-1)].set(values.reshape(-1), mode="drop")


def attend_group(pieces, allowed):
    query_group, key_group, value_group = pieces
    factor = query_group.shape[-1] ** (-0.5)
    scores = (
        jnp.einsum("tgd,sd->gts", query_group, key_group, preferred_element_type=jnp.float32)
        * factor
    )
    masked = jnp.where(allowed[None], scores, masked_score)
    largest = jnp.max(masked, axis=-1, keepdims=True)
    powers = jnp.exp(masked - largest)
    totals = jnp.sum(powers, axis=-1, keepdims=True)
    softmax_rows = (powers / totals).astype(jnp.bfloat16)
    attended = jnp.einsum(
        "gts,sd->tgd", softmax_rows, value_group, preferred_element_type=jnp.float32
    )
    return (attended, largest[..., 0] + jnp.log(totals[..., 0]))


def attend_back(pieces, allowed):
    query_group, key_group, value_group, grad_group, log_total = pieces
    factor = query_group.shape[-1] ** (-0.5)
    scores = (
        jnp.einsum("tgd,sd->gts", query_group, key_group, preferred_element_type=jnp.float32)
        * factor
    )
    softmax_rows = jnp.where(allowed[None], jnp.exp(scores - log_total[..., None]), 0.0)
    grad_soft = jnp.einsum(
        "tgd,sd->gts", grad_group, value_group, preferred_element_type=jnp.float32
    )
    inner_sum = jnp.sum(softmax_rows * grad_soft, axis=-1, keepdims=True)
    grad_scores = (softmax_rows * (grad_soft - inner_sum)).astype(jnp.bfloat16)
    grad_query = (
        jnp.einsum("gts,sd->tgd", grad_scores, key_group, preferred_element_type=jnp.float32)
        * factor
    )
    grad_key = (
        jnp.einsum("gts,tgd->sd", grad_scores, query_group, preferred_element_type=jnp.float32)
        * factor
    )
    grad_value = jnp.einsum(
        "gts,tgd->sd",
        softmax_rows.astype(jnp.bfloat16),
        grad_group,
        preferred_element_type=jnp.float32,
    )
    return (grad_query, grad_key, grad_value)


def expert_apply(received, w_gate, w_up, w_down):
    gate_pre = jnp.einsum("nesd,edf->nesf", received, w_gate, preferred_element_type=jnp.float32)
    up_pre = jnp.einsum("nesd,edf->nesf", received, w_up, preferred_element_type=jnp.float32)
    hidden = (jax.nn.silu(gate_pre) * up_pre).astype(jnp.bfloat16)
    return jnp.einsum("nesf,efd->nesd", hidden, w_down, preferred_element_type=jnp.float32).astype(
        jnp.bfloat16
    )


def shards(
    tokens,
    w_query,
    w_key,
    w_value,
    w_out,
    w_router,
    gain_attn,
    gain_moe,
    w_gate,
    w_up,
    w_down,
    segments,
    routes,
    priority,
    cotangent,
):
    rows_here = tokens.shape[0]
    model_width = tokens.shape[1]
    expert_devices = lax.axis_size("expert")
    device_place = lax.axis_index("expert")
    local_experts = w_gate.shape[0]
    experts = local_experts * expert_devices
    top_count = routes.shape[1]
    capacity = rows_here * top_count // experts
    seq_length = rows_here * expert_devices
    head_size = HD
    gathered = (
        lax.all_gather(w_query, ("dp", "expert"), axis=0, tiled=True),
        lax.all_gather(w_key, ("dp", "expert"), axis=0, tiled=True),
        lax.all_gather(w_value, ("dp", "expert"), axis=0, tiled=True),
        lax.all_gather(w_out, ("dp", "expert"), axis=0, tiled=True),
        lax.all_gather(w_router, ("dp", "expert"), axis=0, tiled=True),
        lax.all_gather(gain_attn, ("dp", "expert"), axis=0, tiled=True),
        lax.all_gather(gain_moe, ("dp", "expert"), axis=0, tiled=True),
    )
    query_full, key_full, value_full, out_full, router_full, attn_gain_full, moe_gain_full = (
        gathered
    )
    head_count = query_full.shape[1] // head_size
    kv_heads = key_full.shape[1] // head_size
    group_size = head_count // kv_heads
    inputs = tokens.astype(jnp.float32)
    normed_attn, unit_attn, scale_attn = norm_parts(inputs, attn_gain_full.astype(jnp.float32))
    normed_attn = normed_attn.astype(jnp.bfloat16)
    positions = device_place * rows_here + jnp.arange(rows_here, dtype=jnp.int32)
    cosine, sine_part = rope_tables(positions, head_size)
    query_pre = jnp.dot(normed_attn, query_full, preferred_element_type=jnp.float32).reshape(
        rows_here, head_count, head_size
    )
    key_pre = jnp.dot(normed_attn, key_full, preferred_element_type=jnp.float32).reshape(
        rows_here, kv_heads, head_size
    )
    query_rot = rotate(query_pre, cosine, sine_part).astype(jnp.bfloat16)
    key_flat = (
        rotate(key_pre, cosine, sine_part)
        .astype(jnp.bfloat16)
        .reshape(rows_here, kv_heads * head_size)
    )
    value_rows = jnp.dot(normed_attn, value_full, preferred_element_type=jnp.float32).astype(
        jnp.bfloat16
    )
    key_all, value_all = (
        lax.all_gather(key_flat, "expert", axis=0, tiled=True),
        lax.all_gather(value_rows, "expert", axis=0, tiled=True),
    )
    query_segments = lax.dynamic_slice_in_dim(segments, device_place * rows_here, rows_here)
    key_positions = jnp.arange(seq_length, dtype=jnp.int32)
    allowed = (key_positions[None, :] <= positions[:, None]) & (
        segments[None, :] == query_segments[:, None]
    )

    def forward_group(pieces):
        return attend_group(pieces, allowed)

    def backward_group(pieces):
        return attend_back(pieces, allowed)

    query_groups = jnp.transpose(
        query_rot.reshape(rows_here, kv_heads, group_size, head_size), (1, 0, 2, 3)
    )
    key_groups = jnp.transpose(key_all.reshape(seq_length, kv_heads, head_size), (1, 0, 2))
    value_groups = jnp.transpose(value_all.reshape(seq_length, kv_heads, head_size), (1, 0, 2))
    attended, log_total = lax.map(forward_group, (query_groups, key_groups, value_groups))
    mixed_heads = (
        jnp.transpose(attended, (1, 0, 2, 3))
        .reshape(rows_here, head_count * head_size)
        .astype(jnp.bfloat16)
    )
    middle = inputs + jnp.dot(mixed_heads, out_full, preferred_element_type=jnp.float32)
    moe_gain_f = moe_gain_full.astype(jnp.float32)
    normed_moe, unit_moe, scale_moe = norm_parts(middle, moe_gain_f)
    normed_moe = normed_moe.astype(jnp.bfloat16)
    logits = jnp.dot(normed_moe, router_full, preferred_element_type=jnp.float32)
    expert_hot = (routes[:, :, None] == jnp.arange(experts, dtype=jnp.int32)[None, None, :]).astype(
        jnp.float32
    )
    chosen = jnp.sum(expert_hot * logits[:, None, :], axis=-1)
    gate_probs = jax.nn.softmax(chosen, axis=-1)
    slot_ids, kept_pairs = slot_table(routes, priority, experts, capacity)
    token_ids = jnp.broadcast_to(jnp.arange(rows_here, dtype=jnp.int32)[:, None], routes.shape)
    slot_owner = slot_values(routes, slot_ids, kept_pairs, token_ids, rows_here, experts, capacity)
    padded = jnp.concatenate([normed_moe, jnp.zeros((1, model_width), jnp.bfloat16)], axis=0)
    outgoing = jnp.take(padded, slot_owner, axis=0).reshape(
        expert_devices, local_experts, capacity, model_width
    )
    outcome = expert_apply(
        lax.all_to_all(outgoing, "expert", split_axis=0, concat_axis=0, tiled=True),
        w_gate,
        w_up,
        w_down,
    )
    returned = lax.all_to_all(outcome, "expert", split_axis=0, concat_axis=0, tiled=True).reshape(
        experts * capacity, model_width
    )
    combine_index = routes * capacity + jnp.minimum(slot_ids, capacity - 1)
    picked = jnp.take(returned, combine_index.reshape(-1), axis=0).reshape(
        rows_here, top_count, model_width
    )
    kept_float = kept_pairs.astype(jnp.float32)
    weighting = gate_probs * kept_float
    branch = jnp.einsum("tk,tkd->td", weighting, picked, preferred_element_type=jnp.float32)
    outputs = (middle + branch).astype(jnp.bfloat16)
    grad_branch = cotangent.astype(jnp.float32)
    grad_weighting = (
        jnp.einsum("td,tkd->tk", grad_branch, picked, preferred_element_type=jnp.float32)
        * kept_float
    )
    grad_chosen = gate_probs * (
        grad_weighting - jnp.sum(gate_probs * grad_weighting, axis=-1, keepdims=True)
    )
    grad_logits = jnp.sum(expert_hot * grad_chosen[:, :, None], axis=1).astype(jnp.bfloat16)
    grad_router = jnp.einsum(
        "td,te->de", normed_moe, grad_logits, preferred_element_type=jnp.float32
    )
    grad_normed_moe = jnp.einsum(
        "te,de->td", grad_logits, router_full, preferred_element_type=jnp.float32
    )
    slot_weight = slot_values(routes, slot_ids, kept_pairs, weighting, 0.0, experts, capacity)
    grad_padded = jnp.concatenate([grad_branch, jnp.zeros((1, model_width), jnp.float32)], axis=0)
    grad_results = (jnp.take(grad_padded, slot_owner, axis=0) * slot_weight[:, None]).astype(
        jnp.bfloat16
    )
    grad_results = grad_results.reshape(expert_devices, local_experts, capacity, model_width)
    grad_arrived, arrived = (
        lax.all_to_all(grad_results, "expert", split_axis=0, concat_axis=0, tiled=True),
        lax.all_to_all(outgoing, "expert", split_axis=0, concat_axis=0, tiled=True),
    )
    gate_pre = jnp.einsum("nesd,edf->nesf", arrived, w_gate, preferred_element_type=jnp.float32)
    up_pre = jnp.einsum("nesd,edf->nesf", arrived, w_up, preferred_element_type=jnp.float32)
    sigmoid_gate = jax.nn.sigmoid(gate_pre)
    silu_gate = gate_pre * sigmoid_gate
    hidden = (silu_gate * up_pre).astype(jnp.bfloat16)
    grad_hidden = jnp.einsum(
        "nesd,efd->nesf", grad_arrived, w_down, preferred_element_type=jnp.float32
    )
    grad_down = jnp.einsum(
        "nesf,nesd->efd", hidden, grad_arrived, preferred_element_type=jnp.float32
    )
    grad_gate_pre = (
        grad_hidden * up_pre * sigmoid_gate * (1.0 + gate_pre * (1.0 - sigmoid_gate))
    ).astype(jnp.bfloat16)
    grad_up_pre = (grad_hidden * silu_gate).astype(jnp.bfloat16)
    grad_gate = jnp.einsum(
        "nesd,nesf->edf", arrived, grad_gate_pre, preferred_element_type=jnp.float32
    )
    grad_up = jnp.einsum("nesd,nesf->edf", arrived, grad_up_pre, preferred_element_type=jnp.float32)
    grad_rows = jnp.einsum(
        "nesf,edf->nesd", grad_gate_pre, w_gate, preferred_element_type=jnp.float32
    )
    grad_rows = (
        grad_rows
        + jnp.einsum("nesf,edf->nesd", grad_up_pre, w_up, preferred_element_type=jnp.float32)
    ).astype(jnp.bfloat16)
    grad_back = lax.all_to_all(
        grad_rows, "expert", split_axis=0, concat_axis=0, tiled=True
    ).reshape(experts * capacity, model_width)
    scattered = (
        jnp.zeros((rows_here + 1, model_width), jnp.float32)
        .at[slot_owner]
        .add(grad_back.astype(jnp.float32))
    )
    grad_normed_moe = grad_normed_moe + scattered[:rows_here]
    gate_share, up_share, down_share = (
        lax.psum_scatter(
            grad_gate.astype(jnp.bfloat16), "dp", scatter_dimension=1, tiled=True
        ).astype(jnp.float32),
        lax.psum_scatter(
            grad_up.astype(jnp.bfloat16), "dp", scatter_dimension=1, tiled=True
        ).astype(jnp.float32),
        lax.psum_scatter(
            grad_down.astype(jnp.bfloat16), "dp", scatter_dimension=1, tiled=True
        ).astype(jnp.float32),
    )
    grad_middle_add, grad_moe_gain = norm_back(grad_normed_moe, unit_moe, scale_moe, moe_gain_f)
    grad_middle = grad_branch + grad_middle_add
    grad_attn_out = grad_middle.astype(jnp.bfloat16)
    grad_out_w = jnp.einsum(
        "tc,td->cd", mixed_heads, grad_attn_out, preferred_element_type=jnp.float32
    )
    grad_mixed = jnp.einsum(
        "td,cd->tc", grad_attn_out, out_full, preferred_element_type=jnp.float32
    ).astype(jnp.bfloat16)
    grad_groups = jnp.transpose(
        grad_mixed.reshape(rows_here, kv_heads, group_size, head_size), (1, 0, 2, 3)
    )
    grad_query_g, grad_key_g, grad_value_g = lax.map(
        backward_group, (query_groups, key_groups, value_groups, grad_groups, log_total)
    )
    grad_key_all = jnp.transpose(grad_key_g, (1, 0, 2)).reshape(seq_length, kv_heads * head_size)
    grad_value_all = jnp.transpose(grad_value_g, (1, 0, 2)).reshape(
        seq_length, kv_heads * head_size
    )
    grad_key_rot, grad_value_sum = (
        lax.psum_scatter(grad_key_all, "expert", scatter_dimension=0, tiled=True),
        lax.psum_scatter(grad_value_all, "expert", scatter_dimension=0, tiled=True),
    )
    grad_query_rot = jnp.transpose(grad_query_g, (1, 0, 2, 3)).reshape(
        rows_here, head_count, head_size
    )
    grad_query_pre = (
        rotate(grad_query_rot, cosine, -sine_part)
        .astype(jnp.bfloat16)
        .reshape(rows_here, head_count * head_size)
    )
    grad_key_pre = (
        rotate(grad_key_rot.reshape(rows_here, kv_heads, head_size), cosine, -sine_part)
        .astype(jnp.bfloat16)
        .reshape(rows_here, kv_heads * head_size)
    )
    grad_value_rows = grad_value_sum.astype(jnp.bfloat16)
    grad_query_w = jnp.einsum(
        "tc,tq->cq", normed_attn, grad_query_pre, preferred_element_type=jnp.float32
    )
    grad_key_w = jnp.einsum(
        "tc,tq->cq", normed_attn, grad_key_pre, preferred_element_type=jnp.float32
    )
    grad_value_w = jnp.einsum(
        "tc,tq->cq", normed_attn, grad_value_rows, preferred_element_type=jnp.float32
    )
    grad_normed_attn = jnp.einsum(
        "tq,cq->tc", grad_query_pre, query_full, preferred_element_type=jnp.float32
    )
    grad_normed_attn = grad_normed_attn + jnp.einsum(
        "tq,cq->tc", grad_key_pre, key_full, preferred_element_type=jnp.float32
    )
    grad_normed_attn = grad_normed_attn + jnp.einsum(
        "tq,cq->tc", grad_value_rows, value_full, preferred_element_type=jnp.float32
    )
    grad_input_add, grad_attn_gain = norm_back(
        grad_normed_attn, unit_attn, scale_attn, attn_gain_full.astype(jnp.float32)
    )
    grad_tokens = grad_middle + grad_input_add
    dense_sums = (
        lax.psum_scatter(grad_query_w, ("dp", "expert"), scatter_dimension=0, tiled=True),
        lax.psum_scatter(grad_key_w, ("dp", "expert"), scatter_dimension=0, tiled=True),
        lax.psum_scatter(grad_value_w, ("dp", "expert"), scatter_dimension=0, tiled=True),
        lax.psum_scatter(grad_out_w, ("dp", "expert"), scatter_dimension=0, tiled=True),
        lax.psum_scatter(grad_router, ("dp", "expert"), scatter_dimension=0, tiled=True),
        lax.psum_scatter(grad_attn_gain, ("dp", "expert"), scatter_dimension=0, tiled=True),
        lax.psum_scatter(grad_moe_gain, ("dp", "expert"), scatter_dimension=0, tiled=True),
    )
    return (
        outputs,
        grad_tokens,
        dense_sums[0],
        dense_sums[1],
        dense_sums[2],
        dense_sums[3],
        dense_sums[4],
        dense_sums[5],
        dense_sums[6],
        gate_share,
        up_share,
        down_share,
    )


def solution(mesh):
    return jax.shard_map(
        shards,
        mesh=mesh,
        in_specs=(
            P(("dp", "expert"), None),
            P(("dp", "expert"), None),
            P(("dp", "expert"), None),
            P(("dp", "expert"), None),
            P(("dp", "expert"), None),
            P(("dp", "expert"), None),
            P(("dp", "expert")),
            P(("dp", "expert")),
            P("expert", None, None),
            P("expert", None, None),
            P("expert", None, None),
            P("dp"),
            P(("dp", "expert"), None),
            P(("dp", "expert"), None),
            P(("dp", "expert"), None),
        ),
        out_specs=(
            P(("dp", "expert"), None),
            P(("dp", "expert"), None),
            P(("dp", "expert"), None),
            P(("dp", "expert"), None),
            P(("dp", "expert"), None),
            P(("dp", "expert"), None),
            P(("dp", "expert"), None),
            P(("dp", "expert")),
            P(("dp", "expert")),
            P("expert", "dp", None),
            P("expert", "dp", None),
            P("expert", "dp", None),
        ),
        check_vma=False,
    )
```

profile of v0, /device:TPU:0, one launch (start us, length us, event | category | flops | bytes accessed | tf_op | source)
XLA Modules:
  0.0 2370.2 jit_solution(4897735139913734611)
XLA Ops:
  10.4 42.1 %all-reduce.7 = (bf16[1536]{0:T(1024)(128)(2,1)S(1)}, bf16[1536]{0:T(1024)(128)(2,1)}) all-reduce(bf16[1536]{0:T(1024)(128)(2,1)S(1)} %dynamic-update-slice, bf16[1536]{0:T(1024)(128)(2,1)S(1)} %dynamic-update-slice.1), channel_id=1, replica_groups=mesh['dp'=8,'expert'=4] {'dp','expert'}, use_global_device_ids=true, to_apply=%add.2 | all-reduce | flops 3072 | bytes 12288
  54.0 14.6 all-gather.8.cloned.1.call-done
  72.8 52.7 %all-gather.12.cloned.1.call-done = bf16[1536,512]{1,0:T(8,128)(2,1)} async-done(((bf16[48,512]{1,0:T(8,128)(2,1)}), bf16[1536,512]{1,0:T(8,128)(2,1)}) %all-gather.12.cloned.1.call-update) | async-done | bytes 1572880 | tf_op jit(solution)/shard_map/all_gather | solution.py:155
  136.1 11.5 reduce-window.6
  156.3 10.4 scatter_custom_fusion
  172.2 59.2 %all-gather.16.cloned.1.call-done = bf16[1536,1536]{1,0:T(8,128)(2,1)} async-done(((bf16[48,1536]{1,0:T(8,128)(2,1)}), bf16[1536,1536]{1,0:T(8,128)(2,1)}) %all-gather.16.cloned.1.call-update) | async-done | bytes 4718608 | tf_op jit(solution)/shard_map/all_gather | solution.py:154
  237.6 49.9 %while.30 = (s32[]{:T(128)}, bf16[8,320,3,64]{1,3,2,0:T(8,128)(2,1)S(1)}, f32[8,3,320]{2,1,0:T(4,128)}, bf16[8,1280,64]{1,2,0:T(8,128)(2,1)}, bf16[8,1280,64]{1,...) while((s32[]{:T(128)}, ...), condition=%wide.region_4.5_spmd.clone.clone, body=%wide.region_1.4_spmd.clone.sunk.clone | while | flops 325631040 | bytes 16382313 | solution.py:209
  287.5 9.1 all-gather.18.cloned.1.call-done
  302.8 9.5 gather_fusion
  312.3 7.1 broadcast_select_fusion
  319.5 5.5 all-to-all-start
  326.5 10.4 gather_fusion.2
  336.9 108.1 %all-gather = bf16[32,48,40]{1,2,0:T(8,128)(2,1)S(1)} all-gather(bf16[1,48,40]{1,2,0:T(8,128)(2,1)S(1)} %bitcast.373), channel_id=1, replica_groups=mesh['dp'=8,'expert'=4] {'dp','expert'}, dimensions={0}, use_global_device_ids=true | all-gather | bytes 126720 | tf_op jit(solution)/shard_map/all_gather | solution.py:158
  447.4 10.1 scatter_custom_fusion.1
  457.6 8.9 multiply_convert_fusion
  466.4 5.7 all-to-all-start.2
  472.1 14.2 fusion.60
  486.4 14.2 fusion.64
  500.6 59.1 %all-to-all-done.2 = bf16[4,10,64,1536]{3,2,1,0:T(8,128)(2,1)} async-done(((bf16[4,10,64,1536]{3,2,1,0:T(8,128)(2,1)}), bf16[4,10,64,1536]{3,2,1,0:T(8,128)(2,1)}, u32[]{:S(2)}, u32[]{:S(2)}) %all-to-all-start.2) | async-done | bytes 7864352 | tf_op jit(solution)/shard_map/all_to_all | solution.py:271
  559.7 16.8 fusion.83
  576.5 11.8 fusion.58
  588.3 12.6 fusion.70
  605.0 5.8 all-to-all-start.3
  610.8 10.5 convert_bitcast_fusion
  625.3 73.0 %all-to-all-done.3 = bf16[4,10,64,1536]{3,2,1,0:T(8,128)(2,1)} async-done(((bf16[4,10,64,1536]{3,2,1,0:T(8,128)(2,1)}), bf16[4,10,64,1536]{3,2,1,0:T(8,128)(2,1)}, u32[]{:S(2)}, u32[]{:S(2)}) %all-to-all-start.3) | async-done | bytes 7864352 | tf_op jit(solution)/shard_map/all_to_all | solution.py:300
  698.3 5.5 all-to-all-start.1
  705.3 28.6 %scatter_custom_fusion.2 = f32[321,1536]{1,0:T(8,128)} fusion(s32[2560]{0:T(1024)} %copy-done.54, bf16[2560,1536]{1,0:T(8,128)(2,1)} %bitcast.90, f32[]{:T(128)} %constant.88.clone.1), kind=kCustom, calls=%fused_computation.71 | custom fusion | flops 7864320 | bytes 9837056 | tf_op jit(solution)/shard_map/scatter-add | solution.py:306
  733.9 57.5 %all-to-all-done.1 = bf16[4,10,64,1536]{3,2,1,0:T(8,128)(2,1)} async-done(((bf16[4,10,64,1536]{3,2,1,0:T(8,128)(2,1)}), bf16[4,10,64,1536]{3,2,1,0:T(8,128)(2,1)}, u32[]{:S(2)}, u32[]{:S(2)}) %all-to-all-start.1) | async-done | bytes 7864352 | tf_op jit(solution)/shard_map/all_to_all | solution.py:238
  791.4 20.7 gather_fusion.1
  812.1 9.1 fusion.77
  827.5 5.6 fusion.78
  840.4 90.9 %while.31 = (s32[]{:T(128)}, f32[8,320,3,64]{1,3,2,0:T(8,128)S(1)}, f32[8,1280,64]{1,2,0:T(8,128)}, f32[8,1280,64]{1,2,0:T(8,128)}, bf16[8,1280,64]{1,2,0:T(8,12...) while((s32[]{:T(128)}, f32[8,320,3,64]{1,3,2,0:T(8,128)S(1)}, ...), condition=%wide.region_19.20_spmd.clone.clone, body=%wide.region_17.19_spmd.clone.sunk.clone | while | flops 798862400 | bytes 39746944 | solution.py:332
  942.7 10.6 bitcast_convert_fusion.2
  955.0 10.0 bitcast_convert_fusion.1
  966.7 11.8 bitcast_convert_fusion
  983.2 21.6 reduce-scatter.33.cloned.1.call-done
  1012.2 5.3 fusion.138
  1019.1 6.6 fusion.113
  1025.7 6.2 fusion.147
  1031.9 73.5 %reduce-scatter.35.cloned.1.call-done = f32[48,40]{1,0:T(8,128)} async-done(((f32[1536,40]{1,0:T(8,128)}), f32[48,40]{1,0:T(8,128)}) %reduce-scatter.35.cloned.1.call-update) | async-done | bytes 7696
  1112.5 44.4 %all-reduce.6 = (f32[1536]{0:T(1024)S(1)}, f32[1536]{0:T(1024)S(1)}) all-reduce(f32[1536]{0:T(1024)S(1)} %get-tuple-element.163, f32[1536]{0:T(1024)S(1)} %copy-done.58), channel_id=9, replica_groups=mesh['dp'=8,'expert'=4] {'dp','expert'}, use_global_device_ids=true, to_apply=%region_29.30.clone | all-reduce | flops 3072 | bytes 24576
  1161.4 198.7 %reduce-scatter.25.cloned.1.call-done = bf16[10,192,512]{2,1,0:T(8,128)(2,1)} async-done(((bf16[10,1536,512]{2,1,0:T(8,128)(2,1)}), bf16[10,192,512]{2,1,0:T(8,128)(2,1)}) %reduce-scatter.25.cloned.1.call-update) | async-done | bytes 1966096 | tf_op jit(solution)/shard_map/reduce_scatter | solution.py:310
  1364.1 249.8 %reduce-scatter.27.cloned.1.call-done = bf16[10,192,512]{2,1,0:T(8,128)(2,1)} async-done(((bf16[10,1536,512]{2,1,0:T(8,128)(2,1)}), bf16[10,192,512]{2,1,0:T(8,128)(2,1)}) %reduce-scatter.27.cloned.1.call-update) | async-done | bytes 1966096 | tf_op jit(solution)/shard_map/reduce_scatter | solution.py:313
  1617.9 249.7 %reduce-scatter.29.cloned.1.call-done = bf16[10,64,1536]{2,1,0:T(8,128)(2,1)} async-done(((bf16[10,512,1536]{2,1,0:T(8,128)(2,1)}), bf16[10,64,1536]{2,1,0:T(8,128)(2,1)}) %reduce-scatter.29.cloned.1.call-update) | async-done | bytes 1966096 | tf_op jit(solution)/shard_map/reduce_scatter | solution.py:316
  1871.6 102.6 %reduce-scatter.19.cloned.1.call-done = f32[48,512]{1,0:T(8,128)} async-done(((f32[1536,512]{1,0:T(8,128)}), f32[48,512]{1,0:T(8,128)}) %reduce-scatter.19.cloned.1.call-update) | async-done | bytes 98320 | tf_op jit(solution)/shard_map/reduce_scatter | solution.py:381
  1974.2 106.4 %reduce-scatter.21.cloned.1.call-done = f32[48,512]{1,0:T(8,128)} async-done(((f32[1536,512]{1,0:T(8,128)}), f32[48,512]{1,0:T(8,128)}) %reduce-scatter.21.cloned.1.call-update) | async-done | bytes 98320 | tf_op jit(solution)/shard_map/reduce_scatter | solution.py:382
  2080.6 140.9 %reduce-scatter.17.cloned.1.call-done = f32[48,1536]{1,0:T(8,128)} async-done(((f32[1536,1536]{1,0:T(8,128)}), f32[48,1536]{1,0:T(8,128)}) %reduce-scatter.17.cloned.1.call-update) | async-done | bytes 294928 | tf_op jit(solution)/shard_map/reduce_scatter | solution.py:380
  2221.5 141.9 %reduce-scatter.23.cloned.1.call-done = f32[48,1536]{1,0:T(8,128)} async-done(((f32[1536,1536]{1,0:T(8,128)}), f32[48,1536]{1,0:T(8,128)}) %reduce-scatter.23.cloned.1.call-update) | async-done | bytes 294928 | tf_op jit(solution)/shard_map/reduce_scatter | solution.py:383
  (384 shorter events, 264.4 us)
Async XLA Ops:
  7.2 61.5 %all-gather.8.cloned.1.call-start = ((), (), s32[]{:S(2)}) async-start(), calls=%async_computation.14 | async-start | bytes 1622016 | tf_op jit(solution)/shard_map/all_gather | solution.py:156
  7.9 117.6 %all-gather.12.cloned.1.call-start = ((), (), s32[]{:S(2)}) async-start(), calls=%async_computation.16 | async-start | bytes 1622016 | tf_op jit(solution)/shard_map/all_gather | solution.py:155
  8.7 159.5 %all-gather.10.cloned.1.call-start = ((), (), s32[]{:S(2)}) async-start(), calls=%async_computation.15 | async-start | bytes 1638400 | tf_op jit(solution)/shard_map/all_gather | solution.py:190
  52.5 73.0 %copy-start.33 = (f32[1536]{0:T(1024)}, f32[1536]{0:T(1024)S(1)}, u32[]{:S(2)}) copy-start(f32[1536]{0:T(1024)S(1)} %convert_element_type.134) | copy-start | bytes 18436
  54.0 71.5 %copy-start.50 = (f32[320]{0:T(512)}, f32[320]{0:T(512)S(1)}, u32[]{:S(2)}) copy-start(f32[320]{0:T(512)S(1)} %add_rsqrt_fusion.1) | copy-start | bytes 3844
  54.0 71.5 %copy-start = (bf16[320,1536]{1,0:T(8,128)(2,1)S(1)}, bf16[320,1536]{1,0:T(8,128)(2,1)}, u32[]{:S(2)}) copy-start(bf16[320,1536]{1,0:T(8,128)(2,1)} %param.19) | copy-start | bytes 2949124
  71.9 98.7 %all-gather.14.cloned.1.call-start = ((), (), s32[]{:S(2)}) async-start(), calls=%async_computation.17 | async-start | bytes 1638400 | tf_op jit(solution)/shard_map/all_gather | solution.py:189
  72.8 55.3 %copy-start.23 = (f32[320,32]{0,1:T(8,128)}, f32[320,32]{0,1:T(8,128)S(1)}, u32[]{:S(2)}) copy-start(f32[320,32]{0,1:T(8,128)S(1)} %get-tuple-element.234) | copy-start | bytes 122884
  72.8 55.3 %copy-start.31 = (f32[320,32]{0,1:T(8,128)}, f32[320,32]{0,1:T(8,128)S(1)}, u32[]{:S(2)}) copy-start(f32[320,32]{0,1:T(8,128)S(1)} %get-tuple-element.233) | copy-start | bytes 122884
  129.1 102.2 %all-gather.16.cloned.1.call-start = ((), (), s32[]{:S(2)}) async-start(), calls=%async_computation.18 | async-start | bytes 4866048 | tf_op jit(solution)/shard_map/all_gather | solution.py:154
  129.7 166.9 %all-gather.18.cloned.1.call-start = ((), (), s32[]{:S(2)}) async-start(), calls=%async_computation.19 | async-start | bytes 4866048 | tf_op jit(solution)/shard_map/all_gather | solution.py:157
  150.1 16.6 copy-start.64
  150.1 17.9 copy-start.26
  155.2 15.4 copy-start.48
  156.1 14.5 copy-start.61
  166.7 134.1 %copy-start.42 = (f32[1536]{0:T(1024)}, f32[1536]{0:T(1024)S(1)}, u32[]{:S(2)}) copy-start(f32[1536]{0:T(1024)S(1)} %convert_element_type.142) | copy-start | bytes 18436
  168.1 63.3 %copy-start.34 = (f32[1536]{0:T(1024)S(1)}, f32[1536]{0:T(1024)}, u32[]{:S(2)}) copy-start(f32[1536]{0:T(1024)} %copy-done.33) | copy-start | bytes 18436
  168.1 63.3 %copy-start.51 = (f32[320]{0:T(512)S(1)}, f32[320]{0:T(512)}, u32[]{:S(2)}) copy-start(f32[320]{0:T(512)} %copy-done.50) | copy-start | bytes 3844
  172.2 63.8 %copy-start.24 = (f32[320,32]{0,1:T(8,128)S(1)}, f32[320,32]{0,1:T(8,128)}, u32[]{:S(2)}) copy-start(f32[320,32]{0,1:T(8,128)} %copy-done.23) | copy-start | bytes 122884
  287.5 13.3 copy-start.6
  287.5 13.3 copy-start.9
  287.5 13.3 copy-start.38
  302.3 143.0 %copy-start.7 = (bf16[320,1536]{1,0:T(8,128)(2,1)}, bf16[320,1536]{1,0:T(8,128)(2,1)S(1)}, u32[]{:S(2)}) copy-start(bf16[320,1536]{1,0:T(8,128)(2,1)S(1)} %multiply_convert_fusion.1) | copy-start | bytes 2949124
  302.8 9.5 copy-start.53
  319.5 147.0 %all-to-all-start = ((bf16[4,10,64,1536]{3,2,1,0:T(8,128)(2,1)}), bf16[4,10,64,1536]{3,2,1,0:T(8,128)(2,1)}, u32[]{:S(2)}, u32[]{:S(2)}) async-start(bf16[4,10,64,1536]{3,2,1,0:T(8,128)(2,1)} %broadcast_select_fusion), calls=%async_computation | async-start | bytes 15728640 | tf_op jit(solution)/shard_map/all_to_all | solution.py:233
  326.5 10.4 copy-start.63
  336.8 108.9 %copy-start.22 = (s32[320,8]{1,0:T(8,128)S(1)}, s32[320,8]{1,0:T(8,128)}, u32[]{:S(2)}) copy-start(s32[320,8]{1,0:T(8,128)} %copy-done.21) | copy-start | bytes 30724
  336.8 110.3 %copy-start.55 = (pred[320,8]{0,1:T(8,128)(4,1)S(1)}, pred[320,8]{0,1:T(8,128)(4,1)}, u32[]{:S(2)}) copy-start(pred[320,8]{0,1:T(8,128)(4,1)} %get-tuple-element.214) | copy-start | bytes 7684
  466.4 93.2 %all-to-all-start.2 = ((bf16[4,10,64,1536]{3,2,1,0:T(8,128)(2,1)}), bf16[4,10,64,1536]{3,2,1,0:T(8,128)(2,1)}, u32[]{:S(2)}, u32[]{:S(2)}) async-start(bf16[4,10,64,1536]{3,2,1,0:T(8,128)(2,1)} %multiply_convert_fusion), calls=%async_computation.2 | async-start | bytes 15728640 | tf_op jit(solution)/shard_map/all_to_all | solution.py:271
  576.5 11.9 copy-start.15
  605.0 93.3 %all-to-all-start.3 = ((bf16[4,10,64,1536]{3,2,1,0:T(8,128)(2,1)}), bf16[4,10,64,1536]{3,2,1,0:T(8,128)(2,1)}, u32[]{:S(2)}, u32[]{:S(2)}) async-start(bf16[4,10,64,1536]{3,2,1,0:T(8,128)(2,1)} %copy.136), calls=%async_computation.3 | async-start | bytes 15728640 | tf_op jit(solution)/shard_map/all_to_all | solution.py:300
  625.3 78.7 %copy-start.47 = (s32[320,8]{0,1:T(8,128)S(1)}, s32[320,8]{0,1:T(8,128)}, u32[]{:S(2)}) copy-start(s32[320,8]{0,1:T(8,128)} %param.31) | copy-start | bytes 30724
  625.3 78.7 %copy-start.49 = (s32[320,8]{0,1:T(8,128)S(1)}, s32[320,8]{0,1:T(8,128)}, u32[]{:S(2)}) copy-start(s32[320,8]{0,1:T(8,128)} %copy-done.48) | copy-start | bytes 30724
  698.3 93.1 %all-to-all-start.1 = ((bf16[4,10,64,1536]{3,2,1,0:T(8,128)(2,1)}), bf16[4,10,64,1536]{3,2,1,0:T(8,128)(2,1)}, u32[]{:S(2)}, u32[]{:S(2)}) async-start(bf16[4,10,64,1536]{3,2,1,0:T(8,128)(2,1)} %copy.131), calls=%async_computation.1 | async-start | bytes 15728640 | tf_op jit(solution)/shard_map/all_to_all | solution.py:238
  703.8 274.8 %reduce-scatter.31.cloned.1.call-start = ((), (), s32[]{:S(2)}) async-start(), calls=%async_computation.27 | async-start | bytes 3276800
  704.4 107.7 %copy-start.56 = (pred[320,8]{1,0:T(8,128)(4,1)}, pred[320,8]{1,0:T(8,128)(4,1)S(1)}, u32[]{:S(2)}) copy-start(pred[320,8]{1,0:T(8,128)(4,1)S(1)} %copy.127) | copy-start | bytes 7684
  791.4 20.7 copy-start.11
  812.1 12.2 copy-start.3
  824.4 11.6 slice-start
  935.9 68.9 %reduce-scatter.33.cloned.1.call-start = ((), (), s32[]{:S(2)}) async-start(), calls=%async_computation.28 | async-start | bytes 3276800
  939.8 165.6 %reduce-scatter.35.cloned.1.call-start = ((), (), s32[]{:S(2)}) async-start(), calls=%async_computation.29 | async-start | bytes 811008
  942.6 417.5 %reduce-scatter.25.cloned.1.call-start = ((), (), s32[]{:S(2)}) async-start(), calls=%async_computation.24 | async-start | bytes 17694720 | tf_op jit(solution)/shard_map/reduce_scatter | solution.py:310
  953.3 660.6 %reduce-scatter.27.cloned.1.call-start = ((), (), s32[]{:S(2)}) async-start(), calls=%async_computation.25 | async-start | bytes 17694720 | tf_op jit(solution)/shard_map/reduce_scatter | solution.py:313
  965.0 902.6 %reduce-scatter.29.cloned.1.call-start = ((), (), s32[]{:S(2)}) async-start(), calls=%async_computation.26 | async-start | bytes 17694720 | tf_op jit(solution)/shard_map/reduce_scatter | solution.py:316
  978.6 995.7 %reduce-scatter.19.cloned.1.call-start = ((), (), s32[]{:S(2)}) async-start(), calls=%async_computation.21 | async-start | bytes 3244032 | tf_op jit(solution)/shard_map/reduce_scatter | solution.py:381
  983.2 1097.4 %reduce-scatter.21.cloned.1.call-start = ((), (), s32[]{:S(2)}) async-start(), calls=%async_computation.22 | async-start | bytes 3244032 | tf_op jit(solution)/shard_map/reduce_scatter | solution.py:382
  1009.0 1212.5 %reduce-scatter.17.cloned.1.call-start = ((), (), s32[]{:S(2)}) async-start(), calls=%async_computation.20 | async-start | bytes 9732096 | tf_op jit(solution)/shard_map/reduce_scatter | solution.py:380
  1017.6 1345.8 %reduce-scatter.23.cloned.1.call-start = ((), (), s32[]{:S(2)}) async-start(), calls=%async_computation.23 | async-start | bytes 9732096 | tf_op jit(solution)/shard_map/reduce_scatter | solution.py:383
  (39 other events, 103.8 us)
Sparse Core Ops, SparseCore 0:
  10.9 57.7 all-gather.7
  71.6 53.9 all-gather.11
  127.7 17.0 all-gather.9
  146.8 18.1 all-gather.13
  167.7 63.5 all-gather.15
  234.1 62.4 all-gather.17
  936.0 30.7 reduce-scatter.30
  970.1 34.6 reduce-scatter.32
  1009.9 95.5 reduce-scatter.34
  1108.9 251.1 reduce-scatter.24
  1363.7 250.2 reduce-scatter.26
  1617.4 250.2 reduce-scatter.28
  1873.6 100.5 reduce-scatter.18
  1980.1 100.4 reduce-scatter.20
  2086.9 134.5 reduce-scatter.16
  2228.9 134.4 reduce-scatter.22
where the time goes:
time: 2380 us; the launch traced here: 2370 us
  waiting for transfers between devices  1610 us (68%)
  matrix products  295 us (12%)
  blocking collectives  195 us (8%)
  local copies, waits for them, and re-layouts  119 us (5%)
  other arithmetic  109 us (5%)
    reduce_scatter x1, waiting for transfers between devices, shards(): lax.psum_scatter(grad_up.astype(jnp.bfloat16), 'dp', scatter_dimension=1,...  250 us
    reduce_scatter x1, waiting for transfers between devices, shards(): lax.psum_scatter(grad_down.astype(jnp.bfloat16), 'dp', scatter_dimension=...  250 us
    reduce_scatter x1, waiting for transfers between devices, shards(): lax.psum_scatter(grad_gate.astype(jnp.bfloat16), 'dp', scatter_dimension=...  199 us
    reduce_scatter x1, waiting for transfers between devices, shards(): lax.psum_scatter(grad_out_w, ('dp', 'expert'), scatter_dimension=0, tiled...  142 us
    reduce_scatter x1, waiting for transfers between devices, shards(): lax.psum_scatter(grad_query_w, ('dp', 'expert'), scatter_dimension=0, til...  141 us
    all_gather x1, blocking collectives, shards(): lax.all_gather(w_router, ('dp', 'expert'), axis=0, tiled=True)  108 us
    reduce_scatter x1, waiting for transfers between devices, shards(): lax.psum_scatter(grad_value_w, ('dp', 'expert'), scatter_dimension=0, til...  106 us
    reduce_scatter x1, waiting for transfers between devices, shards(): lax.psum_scatter(grad_key_w, ('dp', 'expert'), scatter_dimension=0, tiled...  103 us
  transfers between devices with their start and end apart: 20, of which 16 were waited for; matrix products, arithmetic and copies ran while one was open for 13% of the time, Pallas kernels for 0%

commit v1 on v0

v1 whole, which is shorter than its diff:
```python
import functools

import jax
import jax.numpy as jnp
from jax import lax
from jax.experimental import pallas as pl
from jax.experimental.pallas import tpu as pltpu
from jax.sharding import Mesh
from jax.sharding import PartitionSpec as P

HD = 64
QUAD = 4
F32 = jnp.float32
BF16 = jnp.bfloat16

epsilon = 1e-06
rope_base = 10000.0
masked_score = -1e30


def dot32(spec, a, b):
    return jnp.einsum(spec, a, b, preferred_element_type=F32)


def norm_parts(values, gain_row):
    scaling = lax.rsqrt(jnp.mean(values * values, axis=-1, keepdims=True) + epsilon)
    normed = values * scaling
    return (normed * gain_row, normed, scaling)


def norm_back(grad_rows, normed, scaling, gain_row):
    grad_normed = grad_rows * gain_row
    grad_gain = jnp.sum(grad_rows * normed, axis=0)
    inner_sum = jnp.mean(grad_normed * normed, axis=-1, keepdims=True)
    return (scaling * (grad_normed - normed * inner_sum), grad_gain)


def rope_tables(positions, head_size):
    frequency = rope_base ** (-2.0 * jnp.arange(head_size // 2, dtype=F32) / head_size)
    angles = positions.astype(F32)[:, None] * frequency[None, :]
    return (jnp.cos(angles), jnp.sin(angles))


def slot_dense(routes, priority, experts, capacity):
    rows, top_count = routes.shape
    hot = routes[:, :, None] == jnp.arange(experts, dtype=jnp.int32)
    rank = jnp.sum(jnp.where(hot, priority[:, :, None] + 1, 0), axis=1) - 1
    per_rank = rank[None] == jnp.arange(top_count, dtype=jnp.int32)[:, None, None]
    flat = jnp.transpose(per_rank.astype(BF16), (1, 0, 2)).reshape(rows, top_count * experts)
    index = jnp.arange(rows, dtype=jnp.int32)
    before = (index[None, :] < index[:, None]).astype(BF16)
    within = jnp.dot(before, flat, preferred_element_type=F32).reshape(rows, top_count, experts)
    totals = jnp.sum(per_rank.astype(F32), axis=1)
    base = jnp.cumsum(totals, axis=0) - totals
    slot = jnp.sum(
        jnp.where(jnp.transpose(per_rank, (1, 0, 2)), within + base[None], 0.0), axis=1
    )
    named = rank >= 0
    return named, jnp.where(named & (slot < capacity), slot, -1.0)


NT=(((1,),(1,)),((),()))
NN=(((1,),(0,)),((),()))
TN=(((0,),(0,)),((),()))

def mm(a,b,dims=NN):
    return lax.dot_general(a,b,dims,preferred_element_type=F32)

def swap_halves(x):
    lane=lax.broadcasted_iota(jnp.int32,(x.shape[0],128),1)
    low=(lane%HD)<HD//2
    parts=[]
    for c in range(x.shape[1]//128):
        g=x[:,c*128:(c+1)*128]
        parts.append(jnp.where(low,pltpu.roll(g,128-HD//2,1),pltpu.roll(g,HD//2,1)))
    return jnp.concatenate(parts,axis=1)

def bias_block(seg_row, keys, first):
    n=seg_row.shape[1]
    s=lax.broadcasted_iota(jnp.int32,(keys,n),0)
    t=lax.broadcasted_iota(jnp.int32,(keys,n),1)+first
    return jnp.where((s<=t)&(s>=seg_row),0.0,masked_score)

def forward_kernel(heads, kv_heads, block, x_ref, gain_ref, w_ref, cos_ref, sin_ref, seg_ref,
                   h1_ref, q_ref, k_ref, v_ref, o_ref, lse_ref, vt_ref):
    length=x_ref.shape[0]
    group=heads//kv_heads
    nq=heads*HD; nk=kv_heads*HD
    for i in range(length//block):
        rows=pl.ds(i*block,block)
        x=x_ref[rows,:].astype(F32)
        r=lax.rsqrt(jnp.mean(x*x,axis=1,keepdims=True)+epsilon)
        h1=(x*r*gain_ref[...]).astype(BF16)
        h1_ref[rows,:]=h1
        qkv=mm(h1,w_ref[...])
        qk=qkv[:,:nq+nk]
        c=jnp.concatenate([cos_ref[rows,:]]*((nq+nk)//128),axis=1)
        s=jnp.concatenate([sin_ref[rows,:]]*((nq+nk)//128),axis=1)
        qk=(qk*c+swap_halves(qk)*s).astype(BF16)
        v=qkv[:,nq+nk:].astype(BF16)
        for h in range(heads):
            q_ref[h,rows,:]=qk[:,h*HD:(h+1)*HD]
        vt=v.astype(F32).T.astype(BF16)
        for h in range(kv_heads):
            k_ref[h,rows,:]=qk[:,nq+h*HD:nq+(h+1)*HD]
            v_ref[h,rows,:]=v[:,h*HD:(h+1)*HD]
            vt_ref[h,:,rows]=vt[h*HD:(h+1)*HD,:]
        keys=(i+1)*block
        bias=bias_block(seg_ref[:,rows],keys,i*block)
        outs=[]
        for h in range(heads):
            g=h//group
            st=mm(k_ref[g,pl.ds(0,keys),:],q_ref[h,rows,:]*BF16(HD**-0.5),NT)+bias
            top=jnp.max(st,axis=0,keepdims=True)
            p=jnp.exp(st-top)
            total=jnp.sum(p,axis=0,keepdims=True)
            ot=mm(vt_ref[g,:,pl.ds(0,keys)],p.astype(BF16))
            outs.append(ot/total)
            lse_ref[pl.ds(h,1),rows]=top+jnp.log(total)
        o_ref[rows,:]=jnp.concatenate(outs,axis=0).T.astype(BF16)

def attention_forward(x_all,gain,w_qkv,cosine,sine,segments,heads,kv_heads,block=256):
    length,width=x_all.shape
    V=pl.BlockSpec(memory_space=pltpu.VMEM)
    nq=heads*HD
    pad=-(-heads//8)*8
    return pl.pallas_call(functools.partial(forward_kernel,heads,kv_heads,block),
        out_shape=(jax.ShapeDtypeStruct((length,width),BF16),
          jax.ShapeDtypeStruct((heads,length,HD),BF16),jax.ShapeDtypeStruct((kv_heads,length,HD),BF16),
          jax.ShapeDtypeStruct((kv_heads,length,HD),BF16),jax.ShapeDtypeStruct((length,nq),BF16),
          jax.ShapeDtypeStruct((pad,length),F32)),
        in_specs=[V]*6,out_specs=(V,)*6,
        scratch_shapes=[pltpu.VMEM((kv_heads,HD,length),BF16)],
        compiler_params=pltpu.CompilerParams(vmem_limit_bytes=56<<20),
        cost_estimate=pl.CostEstimate(flops=2*length*width*w_qkv.shape[1]+2*heads*length*length*256,bytes_accessed=14<<20,transcendentals=heads*length*length//2),
        name="attention_forward")(x_all,gain.reshape(1,-1),w_qkv,cosine,sine,segments.reshape(1,-1))

def backward_kernel(heads, kv_heads, block, q_ref, k_ref, v_ref, do_ref, lse_ref, cos_ref, sin_ref, seg_ref,
                    dqkv_ref, kt_ref, dk_ref, dv_ref):
    length=q_ref.shape[1]
    group=heads//kv_heads
    nq=heads*HD; nk=kv_heads*HD
    factor=HD**-0.5
    dk_ref[...]=jnp.zeros_like(dk_ref)
    dv_ref[...]=jnp.zeros_like(dv_ref)
    for g in range(kv_heads):
        kt_ref[g]=k_ref[g].astype(F32).T.astype(BF16)
    for i in range(length//block):
        rows=pl.ds(i*block,block)
        keys=(i+1)*block
        span=pl.ds(0,keys)
        bias=bias_block(seg_ref[:,rows],keys,i*block)
        dqs=[]
        for h in range(heads):
            g=h//group
            q=q_ref[h,rows,:]
            do=do_ref[rows,h*HD:(h+1)*HD]
            st=mm(k_ref[g,span,:],q*BF16(factor),NT)+bias
            p=jnp.exp(st-lse_ref[pl.ds(h,1),rows])
            dpt=mm(v_ref[g,span,:],do,NT)
            inner=jnp.sum(p*dpt,axis=0,keepdims=True)
            ds=(p*(dpt-inner)).astype(BF16)
            dv_ref[g,span,:]+=mm(p.astype(BF16),do)
            dk_ref[g,span,:]+=mm(ds,q)
            dqs.append(mm(kt_ref[g,:,span],ds))
        dq=jnp.concatenate(dqs,axis=0).T*factor
        c=jnp.concatenate([cos_ref[rows,:]]*(nq//128),axis=1)
        s=jnp.concatenate([sin_ref[rows,:]]*(nq//128),axis=1)
        dqkv_ref[rows,:nq]=(dq*c-swap_halves(dq)*s).astype(BF16)
    dk=jnp.concatenate([dk_ref[g] for g in range(kv_heads)],axis=1)*factor
    c=jnp.concatenate([cos_ref[...]]*(nk//128),axis=1)
    s=jnp.concatenate([sin_ref[...]]*(nk//128),axis=1)
    dqkv_ref[:,nq:nq+nk]=(dk*c-swap_halves(dk)*s).astype(BF16)
    dqkv_ref[:,nq+nk:]=jnp.concatenate([dv_ref[g] for g in range(kv_heads)],axis=1).astype(BF16)

def attention_backward(q,k,v,do,lse,cosine,sine,segments,block=256):
    heads,length,_=q.shape; kv_heads=k.shape[0]
    V=pl.BlockSpec(memory_space=pltpu.VMEM)
    return pl.pallas_call(functools.partial(backward_kernel,heads,kv_heads,block),
        out_shape=jax.ShapeDtypeStruct((length,(heads+2*kv_heads)*HD),BF16),
        in_specs=[V]*8,out_specs=V,
        scratch_shapes=[pltpu.VMEM((kv_heads,HD,length),BF16),pltpu.VMEM((kv_heads,length,HD),F32),pltpu.VMEM((kv_heads,length,HD),F32)],
        compiler_params=pltpu.CompilerParams(vmem_limit_bytes=56<<20),
        cost_estimate=pl.CostEstimate(flops=5*heads*length*length*256,bytes_accessed=10<<20,transcendentals=heads*length*length//2),
        name="attention_backward")(q,k,v,do,lse,cosine,sine,segments.reshape(1,-1))


ALL = ("q", "r", "expert")
DP = ("q", "r")
GROUP = ("r", "expert")


def shards(
    tokens, w_query, w_key, w_value, w_out, w_router, gain_attn, gain_moe,
    w_gate, w_up, w_down, segments, routes, priority, cotangent,
):
    rows_here, width = tokens.shape
    E = lax.axis_size("expert")
    R = lax.axis_size("r")
    Q = lax.axis_size("q")
    e = lax.axis_index("expert")
    r = lax.axis_index("r")
    shard_rows = w_query.shape[0]
    local = w_gate.shape[0]
    experts = local * E
    ffn = w_gate.shape[2]
    capacity = rows_here * routes.shape[1] // experts
    length = rows_here * E
    sources = R * E
    q_cols = w_query.shape[1] // E
    k_cols = w_key.shape[1] // E
    pieces = jnp.concatenate(
        [w.reshape(shard_rows, E, -1) for w in (w_query, w_key, w_value)], axis=2
    )
    mine = lax.all_to_all(pieces, "expert", split_axis=1, concat_axis=0, tiled=True)
    mine = mine.reshape(shard_rows * E, -1)
    w_qkv = lax.all_gather(mine, DP, axis=0, tiled=True)
    x_all = lax.all_gather(tokens, "expert", axis=0, tiled=True)
    small = jnp.concatenate([w_router, gain_attn[:, None], gain_moe[:, None]], axis=1)
    small = lax.all_gather(small, ALL, axis=0, tiled=True)
    router_full = small[:, :experts]
    attn_gain = small[:, experts].astype(F32)
    moe_gain = small[:, experts + 1].astype(F32)
    out_full = lax.all_gather(w_out, ALL, axis=0, tiled=True)
    dm_all = lax.all_gather(cotangent, GROUP, axis=0, tiled=True).reshape(
        sources, rows_here, width
    )
    named, slots = slot_dense(routes, priority, experts, capacity)

    positions = jnp.arange(length, dtype=jnp.int32)
    cosine, sine = rope_tables(positions, HD)
    cosine = jnp.tile(cosine, (1, 4))
    sine = jnp.tile(jnp.concatenate([-sine, sine], axis=1), (1, 2))
    kv_heads = k_cols // HD
    h1_all, query, key, value, mixed, log_total = attention_forward(
        x_all, attn_gain, w_qkv, cosine, sine, segments, q_cols // HD, kv_heads
    )
    mixed_own = lax.all_to_all(mixed, "expert", split_axis=0, concat_axis=1, tiled=True)
    inputs = tokens.astype(F32)
    middle = inputs + jnp.dot(mixed_own, out_full, preferred_element_type=F32)
    h2, unit_moe, scale_moe = norm_parts(middle, moe_gain)
    h2 = h2.astype(BF16)
    logits = jnp.dot(h2, router_full, preferred_element_type=F32)
    probs = jax.nn.softmax(jnp.where(named, logits, masked_score), axis=-1)
    probs = jnp.where(named, probs, 0.0)
    h2_all = lax.all_gather(h2, GROUP, axis=0, tiled=True).reshape(sources, rows_here, width)
    table = lax.all_gather(jnp.concatenate([slots, probs], axis=1), GROUP, axis=0, tiled=True)
    table = table.reshape(sources, rows_here, 2 * experts)
    slot_all, prob_all = table[..., :experts], table[..., experts:]

    count = -(-local // R)
    first = (r * local + R // 2) // R
    last = ((r + 1) * local + R // 2) // R
    y_part = jnp.zeros((sources, rows_here, width), F32)
    dr_part = jnp.zeros((sources, rows_here, width), F32)
    dg_part = jnp.zeros((sources, rows_here, experts), F32)
    gate_list, up_list, down_list = [], [], []
    for i in range(count):
        live = first + i < last
        place = jnp.minimum(first + i, local - 1)
        column = e * local + place
        wg = lax.dynamic_index_in_dim(w_gate, place, 0, False)
        wu = lax.dynamic_index_in_dim(w_up, place, 0, False)
        wd = lax.dynamic_index_in_dim(w_down, place, 0, False)
        slot_e = lax.dynamic_index_in_dim(slot_all, column, 2, False)
        prob_e = lax.dynamic_index_in_dim(prob_all, column, 2, False)
        hot = (slot_e[:, None, :] == jnp.arange(capacity, dtype=F32)[None, :, None]) & live
        hotb = hot.astype(BF16)
        weight = jnp.sum(jnp.where(hot, prob_e[:, None, :], 0.0), axis=-1).reshape(-1, 1)
        rows = dot32("sct,std->scd", hotb, h2_all).astype(BF16).reshape(-1, width)
        dm_rows = dot32("sct,std->scd", hotb, dm_all).astype(BF16).reshape(-1, width)
        ga = jnp.dot(rows, wg, preferred_element_type=F32)
        ua = jnp.dot(rows, wu, preferred_element_type=F32)
        sig = jax.nn.sigmoid(ga)
        silu = ga * sig
        m = silu * ua
        mg = (m * weight).astype(BF16)
        y_rows = jnp.dot(mg, wd, preferred_element_type=F32).astype(BF16)
        u = dot32("nd,fd->nf", dm_rows, wd)
        dg = jnp.sum(m * u, axis=-1)
        dmh = u * weight
        da = (dmh * ua * sig * (1.0 + ga * (1.0 - sig))).astype(BF16)
        du = (dmh * silu).astype(BF16)
        gate_list.append(dot32("nd,nf->df", rows, da).astype(BF16))
        up_list.append(dot32("nd,nf->df", rows, du).astype(BF16))
        down_list.append(dot32("nf,nd->fd", mg, dm_rows).astype(BF16))
        dr_rows = (dot32("nf,df->nd", da, wg) + dot32("nf,df->nd", du, wu)).astype(BF16)
        shape = (sources, capacity, width)
        y_part = y_part + dot32("sct,scd->std", hotb, y_rows.reshape(shape))
        dr_part = dr_part + dot32("sct,scd->std", hotb, dr_rows.reshape(shape))
        back = jnp.sum(jnp.where(hot, dg.reshape(sources, capacity, 1), 0.0), axis=1)
        dg_part = dg_part + back[:, :, None] * (
            jnp.arange(experts, dtype=jnp.int32) == column
        ).astype(F32)
    dr_sum = lax.psum_scatter(
        dr_part.astype(BF16).reshape(-1, width), GROUP, scatter_dimension=0, tiled=True
    ).astype(F32)
    dg = lax.psum_scatter(dg_part.reshape(-1, experts), GROUP, scatter_dimension=0, tiled=True)
    y_sum = lax.psum_scatter(
        y_part.astype(BF16).reshape(-1, width), GROUP, scatter_dimension=0, tiled=True
    ).astype(F32)
    outputs = (middle + y_sum).astype(BF16)

    dp = Q * R
    share_d, share_f = width // dp, ffn // dp

    def spread(parts, rows):
        stack = jnp.stack(parts).reshape(count, dp, rows, -1)
        stack = jnp.transpose(stack, (1, 0, 2, 3))
        got = lax.all_to_all(stack, DP, split_axis=0, concat_axis=0, tiled=True)
        got = jnp.sum(got.reshape((Q, R) + got.shape[1:]).astype(F32), axis=0)
        keep = []
        for place in range(R):
            lo = (place * local + R // 2) // R
            hi = ((place + 1) * local + R // 2) // R
            keep.append(got[place, : hi - lo])
        return jnp.concatenate(keep, axis=0)

    gate_share = spread(gate_list, share_d)
    up_share = spread(up_list, share_d)
    down_share = spread(down_list, share_f)

    inner = jnp.sum(probs * dg, axis=-1, keepdims=True)
    dz = (probs * (dg - inner)).astype(BF16)
    grad_router = dot32("td,te->de", h2, dz)
    dh2 = dr_sum + dot32("te,de->td", dz, router_full)
    add, grad_moe_gain = norm_back(dh2, unit_moe, scale_moe, moe_gain)
    dx1 = cotangent.astype(F32) + add
    dat = dx1.astype(BF16)
    dat_all = lax.all_gather(dat, "expert", axis=0, tiled=True)
    do_own = dot32("td,cd->tc", dat, out_full).astype(BF16)
    do = lax.all_to_all(do_own, "expert", split_axis=1, concat_axis=0, tiled=True)
    grad_out = dot32("tc,td->cd", mixed, dat_all)
    dqkv = attention_backward(query, key, value, do, log_total, cosine, sine, segments)
    grad_qkv = dot32("tc,tq->cq", h1_all, dqkv)
    dh1 = lax.psum_scatter(
        dot32("tq,cq->tc", dqkv, w_qkv).astype(BF16), "expert", scatter_dimension=0, tiled=True
    ).astype(F32)
    _, unit_attn, scale_attn = norm_parts(inputs, attn_gain)
    add, grad_attn_gain = norm_back(dh1, unit_attn, scale_attn, attn_gain)
    grad_tokens = dx1 + add

    qkv_sum = lax.psum_scatter(grad_qkv.astype(BF16), DP, scatter_dimension=0, tiled=True)
    qkv_own = lax.all_to_all(
        qkv_sum.reshape(E, shard_rows, -1), "expert", split_axis=0, concat_axis=0, tiled=True
    )
    qkv_own = jnp.transpose(qkv_own, (1, 0, 2)).astype(F32)
    grad_query = qkv_own[:, :, :q_cols].reshape(shard_rows, -1)
    grad_key = qkv_own[:, :, q_cols : q_cols + k_cols].reshape(shard_rows, -1)
    grad_value = qkv_own[:, :, q_cols + k_cols :].reshape(shard_rows, -1)
    out_sum = lax.psum_scatter(grad_out.astype(BF16), DP, scatter_dimension=0, tiled=True)
    perm = [(p * E + x, dp * x + p) for p in range(dp) for x in range(E)]
    out_own = lax.ppermute(out_sum, ALL, perm).astype(F32)
    small_grad = jnp.concatenate(
        [grad_router, grad_attn_gain[:, None], grad_moe_gain[:, None]], axis=1
    )
    small_own = lax.psum_scatter(small_grad, ALL, scatter_dimension=0, tiled=True)
    return (
        outputs,
        grad_tokens,
        grad_query,
        grad_key,
        grad_value,
        out_own,
        small_own[:, :experts],
        small_own[:, experts],
        small_own[:, experts + 1],
        gate_share,
        up_share,
        down_share,
    )


def solution(mesh):
    dp, ex = mesh.devices.shape
    fine = Mesh(mesh.devices.reshape(dp // QUAD, QUAD, ex), ALL)
    row, flat = P(ALL, None), P(ALL)
    bank = P("expert", None, None)
    spread = P("expert", DP, None)
    return jax.shard_map(
        shards,
        mesh=fine,
        in_specs=(row,) * 6 + (flat,) * 2 + (bank,) * 3 + (P(DP),) + (row,) * 3,
        out_specs=(row,) * 7 + (flat,) * 2 + (spread,) * 3,
        check_vma=False,
    )
```

time: 2380 us -> 1410 us (0.59)
  waiting for transfers between devices: 1610 us -> 866 us
  blocking collectives: 195 us -> 84.2 us
  local copies, waits for them, and re-layouts: 119 us -> 29.8 us
  other arithmetic: 109 us -> 53.6 us
  Pallas kernels: 0 us -> 49.4 us
    reduce_scatter x7 -> x5, waiting for transfers between devices: 1190 us -> 166 us  [the longest x1 162 us: shards(): lax.psum_scatter(dr_part.astype(BF16).reshape(-1, width), GROUP, scatter_...]
    all_to_all x4 -> x5, waiting for transfers between devices: 190 us -> 316 us  [the longest x3 290 us: spread(): got = lax.all_to_all(stack, DP, split_axis=0, concat_axis=0, tiled=True)]
    all_gather x6 -> x7, waiting for transfers between devices: 136 us -> 234 us  [the longest x1 82.9 us: shards(): lax.all_gather(cotangent, GROUP, axis=0, tiled=True)]
    unnamed x2 -> x0, blocking collectives: 86.5 us -> none
    all_gather x1, blocking collectives: 108 us -> 43.4 us  [shards(): small = lax.all_gather(small, ALL, axis=0, tiled=True)]
    unnamed x19 -> x16, waiting for transfers between devices: 97.8 us -> 149 us
    pallas_call x0 -> x2, Pallas kernels: none -> 49.4 us  [the longest x1 24.7 us: attention_forward(): pl.pallas_call(functools.partial(forward_kernel, heads, kv_heads, block),...]
    all_to_all x0 -> x2, blocking collectives: none -> 40.8 us  [the longest x1 30.8 us: shards(): lax.all_to_all(do_own, 'expert', split_axis=1, concat_axis=0, tiled=True)]
  transfers between devices with their start and end apart: 20 -> 20, of which waited for: 16 -> 14; matrix products, arithmetic and copies ran while one was open for 13% -> 15% of each run, Pallas kernels for 0% -> 4%
where the time goes in v1:
time: 1410 us; the launch traced here: 1400 us
  waiting for transfers between devices  866 us (61%)
  matrix products  274 us (19%)
  blocking collectives  84.2 us (6%)
  other arithmetic  53.6 us (4%)
  Pallas kernels  49.4 us (4%)
  local copies, waits for them, and re-layouts  29.8 us (2%)
  starting transfers between devices  24.1 us (2%)
  between operations  15.4 us (1%)
    all_to_all x3, waiting for transfers between devices, spread(): got = lax.all_to_all(stack, DP, split_axis=0, concat_axis=0, tiled=True)  290 us
    dot_general x36, matrix products, dot32(): return jnp.einsum(spec, a, b, preferred_element_type=F32)  229 us
    reduce_scatter x1, waiting for transfers between devices, shards(): lax.psum_scatter(dr_part.astype(BF16).reshape(-1, width), GROUP, scatter_...  162 us
    unnamed x16, waiting for transfers between devices  149 us
    all_gather x1, waiting for transfers between devices, shards(): lax.all_gather(cotangent, GROUP, axis=0, tiled=True)  82.9 us
    all_gather x1, waiting for transfers between devices, shards(): lax.all_gather(h2, GROUP, axis=0, tiled=True)  66.2 us
    all_gather x1, blocking collectives, shards(): small = lax.all_gather(small, ALL, axis=0, tiled=True)  43.4 us
    all_gather x1, waiting for transfers between devices, shards(): x_all = lax.all_gather(tokens, 'expert', axis=0, tiled=True)  32.7 us
  transfers between devices with their start and end apart: 20, of which 14 were waited for; matrix products, arithmetic and copies ran while one was open for 15% of the time, Pallas kernels for 4%

profile of v1, /device:TPU:0, one launch (start us, length us, event | category | flops | bytes accessed | tf_op | source)
XLA Modules:
  0.0 1396.6 jit_solution(12792839661962039169)
XLA Ops:
  9.0 10.0 all_to_all.73
  22.9 43.4 %all_gather.25 = bf16[1536,42]{1,0:T(8,128)(2,1)S(1)} all-gather(bf16[48,42]{1,0:T(8,128)(2,1)S(1)} %pad_maximum_fusion.6), channel_id=1, replica_groups=mesh['q'=2,'r'=4,'expert'=4] {'q','r','expert'}, dimensions={0}, use_global_device_ids=true | all-gather | bytes 133056 | tf_op jit(solution)/shard_map/all_gather | solution.py:220
  69.2 32.7 %all-gather.9.cloned.1.call-done.x_ref = bf16[1280,1536]{1,0:T(8,128)(2,1)} async-done(((bf16[320,1536]{1,0:T(8,128)(2,1)}), bf16[1280,1536]{1,0:T(8,128)(2,1)}) %all-gather.9.cloned.1.call-update) | async-done | bytes 3932176 | tf_op jit(solution)/shard_map/all_gather | solution.py:218
  101.9 24.7 %attention_forward.1 = (bf16[1280,1536]{1,0:T(8,128)(2,1)}, bf16[6,1280,64]{2,1,0:T(8,128)(2,1)}, bf16[2,1280,64]{2,1,0:T(8,128)(2,1)}, bf16[2,1280,64]{2,1,0:T(...) custom-call(bf16[1280,1536]{1,0:T(8,128)(2,1)} %all-gather.9.cloned.1.call-done.x_ref, ...), custom_call_target="tpu_custom_call" | custom-call | flops 7549747200 | bytes 14680064 | tf_op jit(solution)/shard_map/attention_forward/pallas_call | solution.py:127
  131.1 13.9 all-to-all-done.1
  145.1 23.6 %all-gather.13.cloned.1.call-done = bf16[1536,1536]{1,0:T(8,128)(2,1)} async-done(((bf16[48,1536]{1,0:T(8,128)(2,1)}), bf16[1536,1536]{1,0:T(8,128)(2,1)}) %all-gather.13.cloned.1.call-update) | async-done | bytes 4718608 | tf_op jit(solution)/shard_map/all_gather | solution.py:224
  177.9 28.4 %all-gather.21.cloned.1.call-done = f32[16,320,80]{1,2,0:T(8,128)} async-done(((f32[1,320,80]{1,2,0:T(8,128)}), f32[16,320,80]{1,2,0:T(8,128)}) %all-gather.21.cloned.1.call-update) | async-done | bytes 1638416 | tf_op jit(solution)/shard_map/all_gather | solution.py:247
  208.2 82.9 %all-gather.17.cloned.1.call-done = bf16[5120,1536]{1,0:T(8,128)(2,1)} async-done(((bf16[320,1536]{1,0:T(8,128)(2,1)}), bf16[5120,1536]{1,0:T(8,128)(2,1)}) %all-gather.17.cloned.1.call-update) | async-done | bytes 15728656 | tf_op jit(solution)/shard_map/all_gather | solution.py:225
  291.2 10.4 convolution_convert_fusion.1
  302.9 4.4 convolution_convert_fusion.2
  310.6 66.2 %all-gather.15.cloned.1.call-done = bf16[5120,1536]{1,0:T(8,128)(2,1)} async-done(((bf16[320,1536]{1,0:T(8,128)(2,1)}), bf16[5120,1536]{1,0:T(8,128)(2,1)}) %all-gather.15.cloned.1.call-update) | async-done | bytes 15728656 | tf_op jit(solution)/shard_map/all_gather | solution.py:246
  376.8 8.7 convolution_convert_fusion.5
  390.2 5.7 fusion.20
  395.9 4.6 fusion.16
  400.5 4.6 fusion.30
  405.1 4.5 fusion.26
  413.2 5.8 fusion.36
  418.9 4.7 fusion.40
  423.7 4.7 multiply_reduce_fusion
  429.3 6.9 multiply_reduce_fusion.1
  437.2 6.0 multiply_reduce_fusion.2
  444.1 5.2 multiply_convert_fusion
  449.4 7.1 fusion.18
  466.3 12.6 fusion.50
  488.8 12.4 fusion.43
  503.8 5.1 add_convert_fusion.2
  508.9 26.9 %add_convert_fusion = bf16[16,320,1536]{2,1,0:T(8,128)(2,1)} fusion(f32[16,320,1536]{2,1,0:T(8,128)} %fusion.43, f32[16,320,1536]{2,1,0:T(8,128)} %fusion.50, bf16[16,64,1536]{2,1,0:T(8,128)(2,1)S(1)} %bitcast.321, f32[16,320]{1,0:T(8,128)S(1)} %bitcast.347, pred[]{:T(512)S(6)} %lt.70), kind=kOutput, calls=%fused_computation | convolution fusion | flops 1030881280 | bytes 81809408 | tf_op jit(solution)/shard_map/sct,scd->std/dot_general | solution.py:22
  535.9 27.8 %reduce-scatter.22.cloned.1.call-done = f32[320,40]{1,0:T(8,128)} async-done(((f32[5120,40]{1,0:T(8,128)}), f32[320,40]{1,0:T(8,128)}) %reduce-scatter.22.cloned.1.call-update) | async-done | bytes 51216
  564.8 162.0 %reduce-scatter.14.cloned.1.call-done = bf16[320,1536]{1,0:T(8,128)(2,1)} async-done(((bf16[5120,1536]{1,0:T(8,128)(2,1)}), bf16[320,1536]{1,0:T(8,128)(2,1)}) %reduce-scatter.14.cloned.1.call-update) | async-done | bytes 983056 | tf_op jit(solution)/shard_map/reduce_scatter | solution.py:295
  732.4 4.4 convolution_convert_fusion.21
  736.9 30.8 %all_to_all.74 = bf16[320,4,384]{2,0,1:T(8,128)(2,1)} all-to-all(bf16[320,4,384]{2,0,1:T(8,128)(2,1)S(1)} %bitcast.360), channel_id=1, replica_groups=mesh['q'=2,'r'=4,'expert'=4] {'expert'}, dimensions={1} | all-to-all | bytes 1966080 | tf_op jit(solution)/shard_map/all_to_all | solution.py:332
  767.8 24.7 %attention_backward.1 = bf16[1280,640]{1,0:T(8,128)(2,1)} custom-call(bf16[6,1280,64]{2,1,0:T(8,128)(2,1)} %get-tuple-element.19.q_ref, bf16[2,1280,64]{2,1,0:T(8,128)(2,1)} %get-tuple-element.20.k_ref, bf16[2,1280,64]{2,1,0:T(8,128)(2,1)} %get-tuple-element.21.v_ref, bf16[1280,384]{1,0:T(8,128)(2,1)} %bitcast.373, f32[8,1280]{1,0:T(8,128)} %get-tuple-element.22.lse_ref, ...), custom_call_target="tpu_custom_call" | custom-call | flops 12582912000 | bytes 10485760 | tf_op jit(solution)/shard_map/attention_backward/pallas_call | solution.py:179
  792.5 6.0 convolution_convert_fusion.10
  798.6 5.0 convolution_convert_fusion.20
  803.6 6.4 convolution_convert_fusion
  821.3 12.6 fusion.53
  833.9 12.6 fusion.46
  846.5 26.9 %add_convert_fusion.1 = bf16[16,320,1536]{2,1,0:T(8,128)(2,1)} fusion(f32[16,320,1536]{2,1,0:T(8,128)} %fusion.46, f32[16,320,1536]{2,1,0:T(8,128)} %fusion.53, bf16[16,64,1536]{2,1,0:T(8,128)(2,1)S(1)} %bitcast.320, f32[16,320]{1,0:T(8,128)S(1)} %bitcast.348, pred[]{:T(512)S(6)} %lt.70), kind=kOutput, calls=%fused_computation.1 | convolution fusion | flops 1030881280 | bytes 81809408 | tf_op jit(solution)/shard_map/sct,scd->std/dot_general | solution.py:22
  873.4 4.3 convolution_convert_fusion.15
  884.2 4.8 all-to-all-start.5
  899.8 100.6 %all-to-all-done.5 = bf16[8,3,192,512]{3,2,1,0:T(8,128)(2,1)} async-done(((bf16[8,3,192,512]{3,2,1,0:T(8,128)(2,1)}), bf16[8,3,192,512]{3,2,1,0:T(8,128)(2,1)}, u32[]{:S(2)}, u32[]{:S(2)}) %all-to-all-start.5) | async-done | bytes 4718624 | tf_op jit(solution)/shard_map/all_to_all | solution.py:310
  1000.4 4.6 all-to-all-start.4
  1015.5 93.7 %all-to-all-done.4 = bf16[8,3,192,512]{3,2,1,0:T(8,128)(2,1)} async-done(((bf16[8,3,192,512]{3,2,1,0:T(8,128)(2,1)}), bf16[8,3,192,512]{3,2,1,0:T(8,128)(2,1)}, u32[]{:S(2)}, u32[]{:S(2)}) %all-to-all-start.4) | async-done | bytes 4718624 | tf_op jit(solution)/shard_map/all_to_all | solution.py:310
  1109.2 4.8 all-to-all-start.6
  1128.0 95.6 %all-to-all-done.6 = bf16[8,3,64,1536]{3,2,1,0:T(8,128)(2,1)} async-done(((bf16[8,3,64,1536]{3,2,1,0:T(8,128)(2,1)}), bf16[8,3,64,1536]{3,2,1,0:T(8,128)(2,1)}, u32[]{:S(2)}, u32[]{:S(2)}) %all-to-all-start.6) | async-done | bytes 4718624 | tf_op jit(solution)/shard_map/all_to_all | solution.py:310
  1237.8 12.5 all-to-all-done.3
  1262.3 5.1 fusion.8
  1267.4 119.0 %reduce-scatter.24.cloned.1.call-done = f32[48,42]{1,0:T(8,128)} async-done(((f32[1536,42]{1,0:T(8,128)}), f32[48,42]{1,0:T(8,128)}) %reduce-scatter.24.cloned.1.call-update) | async-done | bytes 8080
  (306 shorter events, 150.8 us)
Async XLA Ops:
  7.2 62.0 %all-gather.11.cloned.1.call-start = ((), (), s32[]{:S(2)}) async-start(), calls=%async_computation.15 | async-start | bytes 2211840 | tf_op jit(solution)/shard_map/all_gather | solution.py:217
  19.1 82.8 %all-gather.9.cloned.1.call-start = ((), (), s32[]{:S(2)}) async-start(), calls=%async_computation.14 | async-start | bytes 4915200 | tf_op jit(solution)/shard_map/all_gather | solution.py:218
  19.9 148.9 %all-gather.13.cloned.1.call-start = ((), (), s32[]{:S(2)}) async-start(), calls=%async_computation.16 | async-start | bytes 4866048 | tf_op jit(solution)/shard_map/all_gather | solution.py:224
  21.4 47.2 %copy-start.67 = (s32[1280]{0:T(1024)S(1)}, s32[1280]{0:T(1024)}, u32[]{:S(2)}) copy-start(s32[1280]{0:T(1024)} %param.26) | copy-start | bytes 15364
  21.4 47.8 %copy-start.64 = (s32[320,8]{0,1:T(8,128)S(1)}, s32[320,8]{0,1:T(8,128)}, u32[]{:S(2)}) copy-start(s32[320,8]{0,1:T(8,128)} %param.28) | copy-start | bytes 30724
  66.3 108.1 %copy-start.12 = (bf16[1536,42]{1,0:T(8,128)(2,1)}, bf16[1536,42]{1,0:T(8,128)(2,1)S(1)}, u32[]{:S(2)}) copy-start(bf16[1536,42]{1,0:T(8,128)(2,1)S(1)} %all_gather.25) | copy-start | bytes 387076
  66.8 59.8 %copy-start.57 = (f32[1536]{0:T(1024)}, f32[1536]{0:T(1024)S(1)}, u32[]{:S(2)}) copy-start(f32[1536]{0:T(1024)S(1)} %get-tuple-element.29) | copy-start | bytes 18436
  66.8 106.1 %copy-start.54 = (f32[1536]{0:T(1024)}, f32[1536]{0:T(1024)S(1)}, u32[]{:S(2)}) copy-start(f32[1536]{0:T(1024)S(1)} %get-tuple-element.28) | copy-start | bytes 18436
  69.2 61.1 %copy-start.65 = (s32[320,8]{0,1:T(8,128)S(1)}, s32[320,8]{0,1:T(8,128)}, u32[]{:S(2)}) copy-start(s32[320,8]{0,1:T(8,128)} %param.27) | copy-start | bytes 30724
  126.7 18.3 %all-to-all-start.1 = ((bf16[4,320,384]{2,1,0:T(8,128)(2,1)}), bf16[4,320,384]{2,1,0:T(8,128)(2,1)S(1)}, u32[]{:S(2)}, u32[]{:S(2)}) async-start(bf16[4,320,384]{2,1,0:T(8,128)(2,1)} %bitcast.372), calls=%async_computation.1 | async-start | bytes 1966080 | tf_op jit(solution)/shard_map/all_to_all | solution.py:238
  130.2 38.6 %copy-start.8 = (bf16[320,1536]{1,0:T(8,128)(2,1)S(1)}, bf16[320,1536]{1,0:T(8,128)(2,1)}, u32[]{:S(2)}) copy-start(bf16[320,1536]{1,0:T(8,128)(2,1)} %param.15) | copy-start | bytes 2949124
  130.2 76.2 %all-gather.21.cloned.1.call-start = ((), (), s32[]{:S(2)}) async-start(), calls=%async_computation.25 | async-start | bytes 2088960 | tf_op jit(solution)/shard_map/all_gather | solution.py:247
  176.2 114.9 %all-gather.17.cloned.1.call-start = ((), (), s32[]{:S(2)}) async-start(), calls=%async_computation.19 | async-start | bytes 16711680 | tf_op jit(solution)/shard_map/all_gather | solution.py:225
  176.8 199.9 %all-gather.15.cloned.1.call-start = ((), (), s32[]{:S(2)}) async-start(), calls=%async_computation.17 | async-start | bytes 16711680 | tf_op jit(solution)/shard_map/all_gather | solution.py:246
  177.4 386.2 %reduce-scatter.22.cloned.1.call-start = ((), (), s32[]{:S(2)}) async-start(), calls=%async_computation.26 | async-start | bytes 2785280
  310.6 126.6 %copy-start.15 = (bf16[16,64,1536]{2,1,0:T(8,128)(2,1)}, bf16[16,64,1536]{2,1,0:T(8,128)(2,1)S(1)}, u32[]{:S(2)}) copy-start(bf16[16,64,1536]{2,1,0:T(8,128)(2,1)S(1)} %convolution_convert_fusion.3) | copy-start | bytes 9437188
  390.2 14.9 %copy-start.25 = (bf16[16,64,1536]{2,1,0:T(8,128)(2,1)}, bf16[16,64,1536]{2,1,0:T(8,128)(2,1)S(1)}, u32[]{:S(2)}) copy-start(bf16[16,64,1536]{2,1,0:T(8,128)(2,1)S(1)} %convolution_convert_fusion.7) | copy-start | bytes 9437188
  449.3 54.4 %copy-start.42 = (bf16[1024,512]{0,1:T(8,128)(2,1)}, bf16[1024,512]{0,1:T(8,128)(2,1)S(1)}, u32[]{:S(2)}) copy-start(bf16[1024,512]{0,1:T(8,128)(2,1)S(1)} %get-tuple-element.50) | copy-start | bytes 3145732
  466.3 12.7 copy-start.26
  466.3 12.7 copy-start.27
  466.3 12.7 copy-start.32
  503.7 223.1 %reduce-scatter.14.cloned.1.call-start = ((), (), s32[]{:S(2)}) async-start(), calls=%async_computation.20 | async-start | bytes 16711680 | tf_op jit(solution)/shard_map/reduce_scatter | solution.py:295
  535.8 28.9 %copy-start.51 = (f32[320,40]{0,1:T(8,128)S(1)}, f32[320,40]{0,1:T(8,128)}, u32[]{:S(2)}) copy-start(f32[320,40]{0,1:T(8,128)} %copy-done.50) | copy-start | bytes 153604
  535.8 191.0 %copy-start.5 = (f32[320,1536]{1,0:T(8,128)S(1)}, f32[320,1536]{1,0:T(8,128)}, u32[]{:S(2)}) copy-start(f32[320,1536]{1,0:T(8,128)} %copy-done.4) | copy-start | bytes 5898244
  535.8 191.0 %copy-start.13 = (bf16[1536,42]{1,0:T(8,128)(2,1)S(1)}, bf16[1536,42]{1,0:T(8,128)(2,1)}, u32[]{:S(2)}) copy-start(bf16[1536,42]{1,0:T(8,128)(2,1)} %copy-done.12) | copy-start | bytes 387076
  535.8 191.0 %copy-start.55 = (f32[1536]{0:T(1024)S(1)}, f32[1536]{0:T(1024)}, u32[]{:S(2)}) copy-start(f32[1536]{0:T(1024)} %copy-done.54) | copy-start | bytes 18436
  535.8 191.0 %copy-start.60 = (f32[320]{0:T(512)S(1)}, f32[320]{0:T(512)}, u32[]{:S(2)}) copy-start(f32[320]{0:T(512)} %copy-done.59) | copy-start | bytes 3844
  535.8 262.8 %all-gather.19.cloned.1.call-start = ((), (), s32[]{:S(2)}) async-start(), calls=%async_computation.23 | async-start | bytes 4915200 | tf_op jit(solution)/shard_map/all_gather | solution.py:330
  564.7 164.7 %copy-start.52 = (bf16[320,40]{0,1:T(8,128)(2,1)}, bf16[320,40]{0,1:T(8,128)(2,1)S(1)}, u32[]{:S(2)}) copy-start(bf16[320,40]{0,1:T(8,128)(2,1)S(1)} %multiply_convert_fusion.10) | copy-start | bytes 76804
  564.7 166.1 %copy-start.14 = (bf16[320,1536]{1,0:T(8,128)(2,1)S(1)}, bf16[320,1536]{1,0:T(8,128)(2,1)}, u32[]{:S(2)}) copy-start(bf16[320,1536]{1,0:T(8,128)(2,1)} %param.29) | copy-start | bytes 2949124
  732.4 497.8 %reduce-scatter.18.cloned.1.call-start = ((), (), s32[]{:S(2)}) async-start(), calls=%async_computation.22 | async-start | bytes 2211840 | tf_op jit(solution)/shard_map/reduce_scatter | solution.py:343
  767.8 24.7 %copy-start.71 = (bf16[1280,1536]{1,0:T(8,128)(2,1)S(1)}, bf16[1280,1536]{1,0:T(8,128)(2,1)}, u32[]{:S(2)}) copy-start(bf16[1280,1536]{1,0:T(8,128)(2,1)} %get-tuple-element.23) | copy-start | bytes 11796484
  798.5 452.6 %reduce-scatter.20.cloned.1.call-start = ((), (), s32[]{:S(2)}) async-start(), calls=%async_computation.24 | async-start | bytes 1327104 | tf_op jit(solution)/shard_map/reduce_scatter | solution.py:351
  803.6 451.1 %reduce-scatter.16.cloned.1.call-start = ((), (), s32[]{:S(2)}) async-start(), calls=%async_computation.21 | async-start | bytes 4915200 | tf_op jit(solution)/shard_map/reduce_scatter | solution.py:336
  810.1 452.2 %reduce-scatter.12.cloned.1.call-start = ((), (), s32[]{:S(2)}) async-start(), calls=%async_computation.18 | async-start | bytes 16711680 | tf_op jit(solution)/shard_map/reduce_scatter | solution.py:299
  884.2 116.1 %all-to-all-start.5 = ((bf16[8,3,192,512]{3,2,1,0:T(8,128)(2,1)}), bf16[8,3,192,512]{3,2,1,0:T(8,128)(2,1)}, u32[]{:S(2)}, u32[]{:S(2)}) async-start(bf16[8,3,192,512]{3,2,1,0:T(8,128)(2,1)} %maximum_bitcast_fusion.1), calls=%async_computation.10 | async-start | bytes 9437184 | tf_op jit(solution)/shard_map/all_to_all | solution.py:310
  899.8 105.2 %copy-start.19 = (bf16[16,64,1536]{2,1,0:T(8,128)(2,1)S(1)}, bf16[16,64,1536]{2,1,0:T(8,128)(2,1)}, u32[]{:S(2)}) copy-start(bf16[16,64,1536]{2,1,0:T(8,128)(2,1)} %convolution_convert_fusion.1) | copy-start | bytes 9437188
  1000.4 108.8 %all-to-all-start.4 = ((bf16[8,3,192,512]{3,2,1,0:T(8,128)(2,1)}), bf16[8,3,192,512]{3,2,1,0:T(8,128)(2,1)}, u32[]{:S(2)}, u32[]{:S(2)}) async-start(bf16[8,3,192,512]{3,2,1,0:T(8,128)(2,1)} %maximum_bitcast_fusion), calls=%async_computation.9 | async-start | bytes 9437184 | tf_op jit(solution)/shard_map/all_to_all | solution.py:310
  1015.5 98.6 %copy-start.9 = (bf16[320,1536]{1,0:T(8,128)(2,1)S(1)}, bf16[320,1536]{1,0:T(8,128)(2,1)}, u32[]{:S(2)}) copy-start(bf16[320,1536]{1,0:T(8,128)(2,1)} %param.15) | copy-start | bytes 2949124
  1015.5 98.9 %copy-start.11 = (bf16[320,1536]{1,0:T(8,128)(2,1)S(1)}, bf16[320,1536]{1,0:T(8,128)(2,1)}, u32[]{:S(2)}) copy-start(bf16[320,1536]{1,0:T(8,128)(2,1)} %copy-done.10) | copy-start | bytes 2949124
  1015.5 98.9 %copy-start.53 = (bf16[320,40]{0,1:T(8,128)(2,1)S(1)}, bf16[320,40]{0,1:T(8,128)(2,1)}, u32[]{:S(2)}) copy-start(bf16[320,40]{0,1:T(8,128)(2,1)} %copy-done.52) | copy-start | bytes 76804
  1109.2 114.4 %all-to-all-start.6 = ((bf16[8,3,64,1536]{3,2,1,0:T(8,128)(2,1)}), bf16[8,3,64,1536]{3,2,1,0:T(8,128)(2,1)}, u32[]{:S(2)}, u32[]{:S(2)}) async-start(bf16[8,3,64,1536]{3,2,1,0:T(8,128)(2,1)} %maximum_bitcast_fusion.2), calls=%async_computation.11 | async-start | bytes 9437184 | tf_op jit(solution)/shard_map/all_to_all | solution.py:310
  1114.4 140.3 %copy-start.63 = (f32[320]{0:T(512)}, f32[320]{0:T(512)S(1)}, u32[]{:S(2)}) copy-start(f32[320]{0:T(512)S(1)} %add_rsqrt_fusion) | copy-start | bytes 3844
  1230.2 20.1 %all-to-all-start.3 = ((bf16[4,48,640]{2,1,0:T(8,128)(2,1)}), bf16[4,48,640]{2,1,0:T(8,128)(2,1)S(1)}, u32[]{:S(2)}, u32[]{:S(2)}) async-start(bf16[4,48,640]{2,1,0:T(8,128)(2,1)} %bitcast.379), calls=%async_computation.7 | async-start | bytes 491520 | tf_op jit(solution)/shard_map/all_to_all | solution.py:344
  1233.6 152.8 %reduce-scatter.24.cloned.1.call-start = ((), (), s32[]{:S(2)}) async-start(), calls=%async_computation.27 | async-start | bytes 811008
  1237.8 17.0 %copy-start.58 = (f32[1536]{0:T(1024)S(1)}, f32[1536]{0:T(1024)}, u32[]{:S(2)}) copy-start(f32[1536]{0:T(1024)} %copy-done.57) | copy-start | bytes 18436
  1251.1 2.9 collective-permute-start
  1262.3 127.5 %copy-start.1 = (bf16[48,512]{1,0:T(8,128)(2,1)S(1)}, bf16[48,512]{1,0:T(8,128)(2,1)}, u32[]{:S(2)}) copy-start(bf16[48,512]{1,0:T(8,128)(2,1)} %param.17) | copy-start | bytes 147460
  (44 other events, 189.4 us)
Sparse Core Ops, SparseCore 0:
  19.2 48.3 all-gather.10
  69.2 32.7 all-gather.8
  104.8 63.8 all-gather.12
  176.4 29.9 all-gather.20
  207.8 83.2 all-gather.16
  292.6 84.1 all-gather.14
  503.8 59.7 reduce-scatter.21
  566.0 160.7 reduce-scatter.13
  732.5 47.4 all-gather.18
  798.6 65.9 reduce-scatter.17
  868.3 124.5 reduce-scatter.19
  995.5 48.2 reduce-scatter.15
  1046.2 216.1 reduce-scatter.11
  1267.3 119.0 reduce-scatter.23

commit v2 on v1

--- a/solution.py
+++ b/solution.py
@@ -185,6 +185,319 @@
         name="attention_backward")(q,k,v,do,lse,cosine,sine,segments.reshape(1,-1))
 
 
+MESH=pl.DeviceIdType.MESH
+CORE=1
+ORDERS=((2,4,8),(4,8,2),(8,2,4))
+
+def flip(value, mask):
+    low, high = value % 2, value // 2
+    if mask & 1:
+        low = 1 - low
+    if mask & 2:
+        high = 1 - high
+    return high * 2 + low
+
+def group_device(mask):
+    q, r, e = lax.axis_index("q"), lax.axis_index("r"), lax.axis_index("expert")
+    return (q, flip(r, mask >> 2), flip(e, mask & 3))
+
+def group_member(mask):
+    return flip(lax.axis_index("r"), mask >> 2) * 4 + flip(lax.axis_index("expert"), mask & 3)
+
+def greet(masks):
+    barrier = pltpu.get_barrier_semaphore()
+    for mask in masks:
+        pl.semaphore_signal(barrier, inc=1, device_id=group_device(mask), device_id_type=MESH)
+    pl.semaphore_wait(barrier, len(masks))
+
+def last_hop(part, mask):
+    if mask & CORE:
+        return CORE
+    return [bit for bit in ORDERS[part] if mask & bit][-1]
+
+def gather_order():
+    free = {2: 0.0, 4: 0.0, 8: 0.0}
+    arrived, todo = {(p, 0): 0.0 for p in range(3)}, [(p, m) for p in range(3) for m in range(2, 16, 2)]
+    order = []
+    while todo:
+        best = None
+        for p, m in todo:
+            hop = last_hop(p, m)
+            if (p, m ^ hop) in arrived:
+                key = (max(free[hop], arrived[p, m ^ hop]), ORDERS[p].index(hop), p, m)
+                if best is None or key < best:
+                    best = key
+        start, _, p, m = best
+        hop = last_hop(p, m)
+        free[hop] = start + 1
+        arrived[p, m] = start + 1
+        todo.remove((p, m))
+        order.append((start + 1, p, m))
+    return [(p, m) for _, p, m in sorted(order)]
+
+def one_hot(table, capacity, slots):
+    place = lax.broadcasted_iota(jnp.int32, (capacity, table.shape[1]), 0).astype(F32)
+    return [table[k:k + 1, :] == place for k in range(slots)]
+
+def gather_kernel(slots, capacity, h2_ref, table_ref, dm_ref, rows_ref, dm_rows_ref, weight_ref, tables_ref,
+                  held, arrived, dm_held, send, recv, table_send, table_recv, dm_sem):
+    width = h2_ref.shape[1]
+    part_width = width // 3
+    greet(range(1, 16))
+    tables = []
+    for mask in range(1, 16):
+        copy = pltpu.make_async_remote_copy(table_ref.at[group_member(mask)], arrived.at[mask],
+            table_send.at[mask], table_recv.at[mask], device_id=group_device(mask), device_id_type=MESH)
+        copy.start()
+        tables.append(copy)
+    arrived[0] = table_ref[group_member(0)]
+    copies = {}
+    for p in range(3):
+        for mask in range(1, 16):
+            hop = last_hop(p, mask)
+            source = mask ^ hop
+            src = h2_ref.at[:, pl.ds(p * part_width, part_width)] if source == 0 else held.at[p, source]
+            copies[p, mask] = pltpu.make_async_remote_copy(src, held.at[p, mask], send.at[p, mask], recv.at[p, mask],
+                device_id=group_device(hop), device_id_type=MESH)
+    order = gather_order()
+    for p, mask in order + [(p, CORE) for p in range(3)]:
+        if mask ^ last_hop(p, mask) == 0:
+            copies[p, mask].start()
+    def dm_copy(mask):
+        return pltpu.make_async_copy(dm_ref.at[group_member(mask)], dm_held.at[mask % 2], dm_sem.at[mask % 2])
+    dm_copy(0).start()
+    for copy in tables:
+        copy.wait_recv()
+    def hots(mask):
+        return one_hot(arrived[mask], capacity, slots)
+    def place(target, mask, hot, block, columns):
+        got = mm(jnp.concatenate([h.astype(BF16) for h in hot], axis=0), block).astype(BF16)
+        for k in range(slots):
+            target[k, pl.ds(mask * capacity, capacity), columns] = got[k * capacity:(k + 1) * capacity]
+    def dm_step(mask):
+        if mask + 1 < 16:
+            dm_copy(mask + 1).start()
+        dm_copy(mask).wait()
+        hot = hots(mask)
+        place(dm_rows_ref, mask, hot, dm_held[mask % 2], slice(None))
+        if mask == 0:
+            place(rows_ref, 0, hot, h2_ref[...], slice(None))
+        table = arrived[mask]
+        for k in range(slots):
+            weight_ref[k, pl.ds(mask * capacity, capacity), :] = jnp.sum(
+                jnp.where(hot[k], table[4 + k:5 + k, :], 0.0), axis=1, keepdims=True)
+        tables_ref[mask] = table
+    todo = list(range(16))
+    dm_step(todo.pop(0))
+    dm_step(todo.pop(0))
+    def arrive(p, mask):
+        copies[p, mask].wait_recv()
+        for nxt in range(1, 16):
+            if nxt != mask and (nxt ^ last_hop(p, nxt)) == mask:
+                copies[p, nxt].start()
+        place(rows_ref, mask, hots(mask), held[p, mask], pl.ds(p * part_width, part_width))
+    for step, (p, mask) in enumerate(order):
+        arrive(p, mask)
+        if todo:
+            dm_step(todo.pop(0))
+    for p in range(3):
+        arrive(p, CORE)
+    for p, mask in order:
+        arrive(p, mask | CORE)
+    for copy in tables:
+        copy.wait_send()
+    for key in copies:
+        copies[key].wait_send()
+
+def gather_rows(h2, table, dm_all, slots, capacity, collective_id):
+    tokens, width = h2.shape
+    V = pl.BlockSpec(memory_space=pltpu.VMEM)
+    rows = jax.ShapeDtypeStruct((slots, 16 * capacity, width), BF16)
+    return pl.pallas_call(functools.partial(gather_kernel, slots, capacity),
+        out_shape=(rows, rows, jax.ShapeDtypeStruct((slots, 16 * capacity, 1), F32), jax.ShapeDtypeStruct(table.shape, F32)),
+        in_specs=[V, V, pl.BlockSpec(memory_space=pl.ANY)], out_specs=(V,) * 4,
+        scratch_shapes=[pltpu.VMEM((3, 16, tokens, width // 3), BF16), pltpu.VMEM(table.shape, F32),
+            pltpu.VMEM((2, tokens, width), BF16), pltpu.SemaphoreType.DMA((3, 16)), pltpu.SemaphoreType.DMA((3, 16)),
+            pltpu.SemaphoreType.DMA((16,)), pltpu.SemaphoreType.DMA((16,)), pltpu.SemaphoreType.DMA((2,))],
+        compiler_params=pltpu.CompilerParams(vmem_limit_bytes=58 << 20, collective_id=collective_id, has_side_effects=True),
+        cost_estimate=pl.CostEstimate(flops=4 * 16 * slots * capacity * tokens * width, bytes_accessed=60 << 20, transcendentals=0),
+        name="gather_rows")(h2, table, dm_all)
+
+def expert_kernel(chunks, dp, place_ref, x_ref, dm_ref, weight_ref, wg_ref, wu_ref, wd_ref,
+                  y_ref, dr_ref, dg_ref, gu_ref, down_ref, xs, dms, mgs, das):
+    i = pl.program_id(0)
+    ff = wg_ref.shape[2]
+    block = x_ref.shape[1]
+    @pl.when(i < chunks)
+    def _():
+        x, dmr, w = x_ref[0], dm_ref[0], weight_ref[0]
+        rows = pl.ds(pl.multiple_of(i * block, block), block)
+        xs[rows, :] = x
+        dms[rows, :] = dmr
+        ga = mm(x, wg_ref[0])
+        ua = mm(x, wu_ref[0])
+        u = mm(dmr, wd_ref[0], NT)
+        sig = 1.0 / (1.0 + jnp.exp(-ga))
+        silu = ga * sig
+        m = silu * ua
+        mg = (m * w).astype(BF16)
+        dg_ref[...] = jnp.sum(m * u, axis=1, keepdims=True)
+        dmh = u * w
+        da = (dmh * ua * (sig * (1.0 + ga * (1.0 - sig)))).astype(BF16)
+        du = (dmh * silu).astype(BF16)
+        mgs[rows, :] = mg
+        das[rows, :ff] = da
+        das[rows, ff:] = du
+        y_ref[...] = mm(mg, wd_ref[0]).astype(BF16)
+        dr_ref[...] = (mm(da, wg_ref[0], NT) + mm(du, wu_ref[0], NT)).astype(BF16)
+    @pl.when(i == chunks)
+    def _():
+        share = gu_ref.shape[1] // 2
+        for half in range(2):
+            grad = mm(xs[...], das[:, half * ff:(half + 1) * ff], TN).astype(BF16)
+            for d in range(dp):
+                gu_ref[d, half * share:(half + 1) * share, :] = grad[d * share:(d + 1) * share]
+        down_ref[...] = mm(mgs[...], dms[...], TN).astype(BF16)
+
+def expert_call(rows, dm_rows, weight, slot, w_gate, w_up, w_down, place, dp, block=512):
+    _, total, width = rows.shape
+    ff = w_gate.shape[2]
+    chunks = total // block
+    row_spec = pl.BlockSpec((1, block, width), lambda i, s: (slot, jnp.minimum(i, chunks - 1), 0))
+    out_row = pl.BlockSpec((block, width), lambda i, s: (jnp.minimum(i, chunks - 1), 0))
+    bank = lambda a: pl.BlockSpec((1,) + a.shape[1:], lambda i, s: (s[0], 0, 0))
+    share = width // dp
+    return pl.pallas_call(functools.partial(expert_kernel, chunks, dp),
+        grid_spec=pltpu.PrefetchScalarGridSpec(num_scalar_prefetch=1, grid=(chunks + 1,),
+            in_specs=[row_spec, row_spec, pl.BlockSpec((1, block, 1), lambda i, s: (slot, jnp.minimum(i, chunks - 1), 0)),
+                bank(w_gate), bank(w_up), bank(w_down)],
+            out_specs=(out_row, out_row, pl.BlockSpec((block, 1), lambda i, s: (jnp.minimum(i, chunks - 1), 0)),
+                pl.BlockSpec((dp, 2 * share, ff), lambda i, s: (0, 0, 0)), pl.BlockSpec((ff, width), lambda i, s: (0, 0))),
+            scratch_shapes=[pltpu.VMEM((total, width), BF16), pltpu.VMEM((total, width), BF16),
+                pltpu.VMEM((total, ff), BF16), pltpu.VMEM((total, 2 * ff), BF16)]),
+        out_shape=(jax.ShapeDtypeStruct((total, width), BF16), jax.ShapeDtypeStruct((total, width), BF16),
+            jax.ShapeDtypeStruct((total, 1), F32), jax.ShapeDtypeStruct((dp, 2 * share, ff), BF16),
+            jax.ShapeDtypeStruct((ff, width), BF16)),
+        compiler_params=pltpu.CompilerParams(vmem_limit_bytes=58 << 20, dimension_semantics=("arbitrary",)),
+        cost_estimate=pl.CostEstimate(flops=18 * total * width * ff, bytes_accessed=24 << 20, transcendentals=total * ff),
+        name="expert")(place.reshape(1), rows, dm_rows, weight, w_gate, w_up, w_down)
+
+def first_hop(part, mask):
+    return [bit for bit in ORDERS[part] if mask & bit][0]
+
+def combine_kernel(slots, capacity, with_dg, *refs):
+    rows = refs[:slots]
+    refs = refs[slots:]
+    tables_ref = refs[0]
+    refs = refs[1:]
+    if with_dg:
+        dg_refs, refs = refs[:slots], refs[slots:]
+        out_ref, dg_out = refs[:2]
+        refs = refs[2:]
+    else:
+        out_ref, refs = refs[0], refs[1:]
+    core_out, core_in, held, got, core_send, core_recv, send, recv = refs[:8]
+    if with_dg:
+        dg_hold, dg_in, dg_send, dg_recv = refs[8:]
+    width = out_ref.shape[1]
+    part_width = width // 3
+    greet(range(1, 16) if with_dg else (1, 2, 4, 8))
+    def hots(mask):
+        return one_hot(tables_ref[mask], capacity, slots)
+    def block_sum(mask, hot):
+        return mm(jnp.concatenate([h.astype(BF16) for h in hot], axis=0),
+            jnp.concatenate([rows[k][pl.ds(mask * capacity, capacity), :] for k in range(slots)], axis=0), TN)
+    dg_copies = []
+    def dg_step(mask, hot):
+        if not with_dg:
+            return
+        for k in range(slots):
+            col = dg_refs[k][pl.ds(mask * capacity, capacity), :]
+            dg_hold[mask, k:k + 1, :] = jnp.sum(jnp.where(hot[k], col, 0.0), axis=0, keepdims=True)
+        if mask == 0:
+            return
+        copy = pltpu.make_async_remote_copy(dg_hold.at[mask], dg_in.at[mask], dg_send.at[mask], dg_recv.at[mask],
+            device_id=group_device(mask), device_id_type=MESH)
+        copy.start()
+        dg_copies.append(copy)
+    listed = sorted(range(0, 16, 2), key=lambda m: (-bin(m).count("1"), m))
+    if with_dg:
+        dg_hold[...] = jnp.zeros_like(dg_hold)
+    core = {}
+    for mask in listed:
+        hot = hots(mask | CORE)
+        core_out[mask // 2] = block_sum(mask | CORE, hot).astype(BF16)
+        core[mask] = pltpu.make_async_remote_copy(core_out.at[mask // 2], core_in.at[mask // 2], core_send.at[mask // 2],
+            core_recv.at[mask // 2], device_id=group_device(CORE), device_id_type=MESH)
+        core[mask].start()
+        dg_step(mask | CORE, hot)
+    copies = {}
+    for p in range(3):
+        for mask in range(2, 16, 2):
+            copies[p, mask] = pltpu.make_async_remote_copy(held.at[p, mask // 2], got.at[p, mask // 2], send.at[p, mask // 2],
+                recv.at[p, mask // 2], device_id=group_device(first_hop(p, mask)), device_id_type=MESH)
+    for mask in listed:
+        hot = hots(mask)
+        own = block_sum(mask, hot)
+        core[mask].wait_recv()
+        own = (own + core_in[mask // 2].astype(F32)).astype(BF16)
+        for p in range(3):
+            held[p, mask // 2] = own[:, p * part_width:(p + 1) * part_width]
+            if mask & ORDERS[p][0]:
+                copies[p, mask].start()
+        dg_step(mask, hot)
+    def add(p, target, sources):
+        total = held[p, target // 2].astype(F32)
+        for source in sources:
+            copies[p, source].wait_recv()
+            total = total + got[p, source // 2].astype(F32)
+        return total
+    def forward(p, target, sources):
+        held[p, target // 2] = add(p, target, sources).astype(BF16)
+        copies[p, target].start()
+    for both in (True, False):
+        for p in range(3):
+            a, b, c = ORDERS[p]
+            target = b | c if both else b
+            forward(p, target, [target | a])
+    for p in range(3):
+        a, b, c = ORDERS[p]
+        forward(p, c, [c | a, c | b])
+    for p in range(3):
+        a, b, c = ORDERS[p]
+        out_ref[:, p * part_width:(p + 1) * part_width] = add(p, 0, [a, b, c])
+    if with_dg:
+        dg_out[0] = dg_hold[0]
+        for copy in dg_copies:
+            copy.wait_recv()
+        for mask in range(1, 16):
+            dg_out[mask] = dg_in[mask]
+        for copy in dg_copies:
+            copy.wait_send()
+    for mask in listed:
+        core[mask].wait_send()
+    for key in copies:
+        copies[key].wait_send()
+
+def combine_rows(rows, tables, dgs, capacity, collective_id):
+    slots = len(rows)
+    tokens, width = tables.shape[2], rows[0].shape[1]
+    V = pl.BlockSpec(memory_space=pltpu.VMEM)
+    with_dg = dgs is not None
+    out = jax.ShapeDtypeStruct((tokens, width), F32)
+    table = pltpu.VMEM(tables.shape, F32)
+    sem = pltpu.SemaphoreType.DMA
+    return pl.pallas_call(functools.partial(combine_kernel, slots, capacity, with_dg),
+        out_shape=(out, jax.ShapeDtypeStruct(tables.shape, F32)) if with_dg else out,
+        in_specs=[V] * (slots + 1 + (slots if with_dg else 0)), out_specs=(V, V) if with_dg else V,
+        scratch_shapes=[pltpu.VMEM((8, tokens, width), BF16), pltpu.VMEM((8, tokens, width), BF16),
+            pltpu.VMEM((3, 8, tokens, width // 3), BF16), pltpu.VMEM((3, 8, tokens, width // 3), BF16),
+            sem((8,)), sem((8,)), sem((3, 8)), sem((3, 8))] + ([table, table, sem((16,)), sem((16,))] if with_dg else []),
+        compiler_params=pltpu.CompilerParams(vmem_limit_bytes=58 << 20, collective_id=collective_id, has_side_effects=True),
+        cost_estimate=pl.CostEstimate(flops=2 * 16 * slots * capacity * tokens * width, bytes_accessed=40 << 20, transcendentals=0),
+        name="combine_with_dg" if with_dg else "combine_rows")(*rows, tables, *(dgs if with_dg else ()))
+
+
 ALL = ("q", "r", "expert")
 DP = ("q", "r")
 GROUP = ("r", "expert")
@@ -225,8 +538,24 @@
     dm_all = lax.all_gather(cotangent, GROUP, axis=0, tiled=True).reshape(
         sources, rows_here, width
     )
-    named, slots = slot_dense(routes, priority, experts, capacity)
-
+    named, slots_dense = slot_dense(routes, priority, experts, capacity)
+
+    pick_columns = None
+    shared_banks = None
+    if local % R:
+        ways = R // (local % R)
+        part = ffn // (Q * R * ways)
+        at = jnp.arange(ffn // ways, dtype=jnp.int32)
+        at = (at // part * ways)[None] * part + at % part + jnp.arange(ways, dtype=jnp.int32)[:, None] * part
+        pick_columns = (jnp.arange(ffn, dtype=jnp.int32)[None, :, None] == at[:, None, :]).astype(BF16)
+        mine = lax.dynamic_index_in_dim(pick_columns, r % ways, 0, False)
+        place = (local // R) * R + r // ways
+        shared = [lax.dynamic_index_in_dim(w, place, 0, False) for w in (w_gate, w_up, w_down)]
+        shared_banks = (
+            dot32("df,fc->dc", shared[0], mine).astype(BF16)[None],
+            dot32("df,fc->dc", shared[1], mine).astype(BF16)[None],
+            dot32("fd,fc->cd", shared[2], mine).astype(BF16)[None],
+        )
     positions = jnp.arange(length, dtype=jnp.int32)
     cosine, sine = rope_tables(positions, HD)
     cosine = jnp.tile(cosine, (1, 4))
@@ -243,82 +572,81 @@
     logits = jnp.dot(h2, router_full, preferred_element_type=F32)
     probs = jax.nn.softmax(jnp.where(named, logits, masked_score), axis=-1)
     probs = jnp.where(named, probs, 0.0)
-    h2_all = lax.all_gather(h2, GROUP, axis=0, tiled=True).reshape(sources, rows_here, width)
-    table = lax.all_gather(jnp.concatenate([slots, probs], axis=1), GROUP, axis=0, tiled=True)
-    table = table.reshape(sources, rows_here, 2 * experts)
-    slot_all, prob_all = table[..., :experts], table[..., experts:]
-
-    count = -(-local // R)
-    first = (r * local + R // 2) // R
-    last = ((r + 1) * local + R // 2) // R
-    y_part = jnp.zeros((sources, rows_here, width), F32)
-    dr_part = jnp.zeros((sources, rows_here, width), F32)
-    dg_part = jnp.zeros((sources, rows_here, experts), F32)
-    gate_list, up_list, down_list = [], [], []
-    for i in range(count):
-        live = first + i < last
-        place = jnp.minimum(first + i, local - 1)
-        column = e * local + place
-        wg = lax.dynamic_index_in_dim(w_gate, place, 0, False)
-        wu = lax.dynamic_index_in_dim(w_up, place, 0, False)
-        wd = lax.dynamic_index_in_dim(w_down, place, 0, False)
-        slot_e = lax.dynamic_index_in_dim(slot_all, column, 2, False)
-        prob_e = lax.dynamic_index_in_dim(prob_all, column, 2, False)
-        hot = (slot_e[:, None, :] == jnp.arange(capacity, dtype=F32)[None, :, None]) & live
-        hotb = hot.astype(BF16)
-        weight = jnp.sum(jnp.where(hot, prob_e[:, None, :], 0.0), axis=-1).reshape(-1, 1)
-        rows = dot32("sct,std->scd", hotb, h2_all).astype(BF16).reshape(-1, width)
-        dm_rows = dot32("sct,std->scd", hotb, dm_all).astype(BF16).reshape(-1, width)
-        ga = jnp.dot(rows, wg, preferred_element_type=F32)
-        ua = jnp.dot(rows, wu, preferred_element_type=F32)
-        sig = jax.nn.sigmoid(ga)
-        silu = ga * sig
-        m = silu * ua
-        mg = (m * weight).astype(BF16)
-        y_rows = jnp.dot(mg, wd, preferred_element_type=F32).astype(BF16)
-        u = dot32("nd,fd->nf", dm_rows, wd)
-        dg = jnp.sum(m * u, axis=-1)
-        dmh = u * weight
-        da = (dmh * ua * sig * (1.0 + ga * (1.0 - sig))).astype(BF16)
-        du = (dmh * silu).astype(BF16)
-        gate_list.append(dot32("nd,nf->df", rows, da).astype(BF16))
-        up_list.append(dot32("nd,nf->df", rows, du).astype(BF16))
-        down_list.append(dot32("nf,nd->fd", mg, dm_rows).astype(BF16))
-        dr_rows = (dot32("nf,df->nd", da, wg) + dot32("nf,df->nd", du, wu)).astype(BF16)
-        shape = (sources, capacity, width)
-        y_part = y_part + dot32("sct,scd->std", hotb, y_rows.reshape(shape))
-        dr_part = dr_part + dot32("sct,scd->std", hotb, dr_rows.reshape(shape))
-        back = jnp.sum(jnp.where(hot, dg.reshape(sources, capacity, 1), 0.0), axis=1)
-        dg_part = dg_part + back[:, :, None] * (
-            jnp.arange(experts, dtype=jnp.int32) == column
-        ).astype(F32)
-    dr_sum = lax.psum_scatter(
-        dr_part.astype(BF16).reshape(-1, width), GROUP, scatter_dimension=0, tiled=True
-    ).astype(F32)
-    dg = lax.psum_scatter(dg_part.reshape(-1, experts), GROUP, scatter_dimension=0, tiled=True)
-    y_sum = lax.psum_scatter(
-        y_part.astype(BF16).reshape(-1, width), GROUP, scatter_dimension=0, tiled=True
-    ).astype(F32)
+    dp = Q * R
+    whole = local // R
+    rest = local - whole * R
+    ways = R // rest if rest else 1
+    slots = whole + (1 if rest else 0)
+
+    def by_device(table):
+        table = table.T.reshape(E, local, rows_here)
+        picks = [
+            table[:, [r * whole + s for s in range(whole)] + ([R * whole + r // ways] if rest else [])]
+            for r in range(R)
+        ]
+        return jnp.stack(picks).reshape(sources, slots, rows_here)
+
+    table = jnp.concatenate(
+        [
+            by_device(slots_dense),
+            jnp.zeros((sources, 4 - slots, rows_here), F32),
+            by_device(probs),
+            jnp.zeros((sources, 4 - slots, rows_here), F32),
+        ],
+        axis=1,
+    )
+    rows, dm_rows, weight, tables = gather_rows(h2, table, dm_all, slots, capacity, 1)
+    y_rows, dr_rows, dg_rows, spread_in = [], [], [], []
+    for s in range(slots):
+        if s < whole:
+            banks, place = (w_gate, w_up, w_down), r * whole + s
+        else:
+            banks, place = shared_banks, jnp.int32(0)
+        y, dr, dg, grad_gu, grad_down = expert_call(
+            rows, dm_rows, weight, s, *banks, place.astype(jnp.int32), dp
+        )
+        y_rows.append(y)
+        dr_rows.append(dr)
+        dg_rows.append(dg)
+        spread_in.append((grad_gu, grad_down.reshape(dp, -1, width)))
+    moved = [
+        tuple(lax.all_to_all(a, DP, split_axis=0, concat_axis=0, tiled=True) for a in pair)
+        for pair in spread_in
+    ]
+    dr_sum, dg_back = combine_rows(dr_rows, tables, dg_rows, capacity, 2)
+    y_sum = combine_rows(y_rows, tables, None, capacity, 3)
     outputs = (middle + y_sum).astype(BF16)
-
-    dp = Q * R
+    me = r * E + e
+    dg_back = jnp.take(dg_back, me ^ jnp.arange(sources), axis=0)[:, :slots]
+    dg_back = dg_back.reshape(R, E, slots, rows_here)
+    pieces = [jnp.transpose(dg_back[:, :, :whole], (1, 0, 2, 3)).reshape(E, R * whole, rows_here)]
+    if rest:
+        pieces.append(
+            jnp.transpose(jnp.sum(dg_back[:, :, whole].reshape(rest, ways, E, rows_here), axis=1), (1, 0, 2))
+        )
+    dg = jnp.concatenate(pieces, axis=1).reshape(experts, rows_here).T
+
     share_d, share_f = width // dp, ffn // dp
-
-    def spread(parts, rows):
-        stack = jnp.stack(parts).reshape(count, dp, rows, -1)
-        stack = jnp.transpose(stack, (1, 0, 2, 3))
-        got = lax.all_to_all(stack, DP, split_axis=0, concat_axis=0, tiled=True)
-        got = jnp.sum(got.reshape((Q, R) + got.shape[1:]).astype(F32), axis=0)
-        keep = []
-        for place in range(R):
-            lo = (place * local + R // 2) // R
-            hi = ((place + 1) * local + R // 2) // R
-            keep.append(got[place, : hi - lo])
-        return jnp.concatenate(keep, axis=0)
-
-    gate_share = spread(gate_list, share_d)
-    up_share = spread(up_list, share_d)
-    down_share = spread(down_list, share_f)
+    sums = []
+    for s in range(whole):
+        gu, down = moved[s]
+        sums.append(
+            (
+                jnp.sum(gu.reshape(Q, R, 2, share_d, ffn).astype(F32), axis=0),
+                jnp.sum(down.reshape(Q, R, share_f, width).astype(F32), axis=0),
+            )
+        )
+    gate_share = jnp.stack([a[:, 0] for a, _ in sums], axis=1).reshape(-1, share_d, ffn)
+    up_share = jnp.stack([a[:, 1] for a, _ in sums], axis=1).reshape(-1, share_d, ffn)
+    down_share = jnp.stack([a for _, a in sums], axis=1).reshape(-1, share_f, width)
+    if rest:
+        gu, down = moved[whole]
+        gu = gu.reshape(Q, rest, ways, 2, share_d, ffn // ways)
+        gu = dot32("qxhgdc,hfc->xgdf", gu, pick_columns)
+        gate_share = jnp.concatenate([gate_share, gu[:, 0]], axis=0)
+        up_share = jnp.concatenate([up_share, gu[:, 1]], axis=0)
+        down = jnp.sum(down.reshape(Q, rest, share_f, width).astype(F32), axis=0)
+        down_share = jnp.concatenate([down_share, down], axis=0)
 
     inner = jnp.sum(probs * dg, axis=-1, keepdims=True)
     dz = (probs * (dg - inner)).astype(BF16)
@@ -333,28 +661,33 @@
     grad_out = dot32("tc,td->cd", mixed, dat_all)
     dqkv = attention_backward(query, key, value, do, log_total, cosine, sine, segments)
     grad_qkv = dot32("tc,tq->cq", h1_all, dqkv)
+    dh1_part = dot32("tq,cq->tc", dqkv, w_qkv)
+    unit_all = norm_parts(x_all.astype(F32), attn_gain)[1]
+    grad_attn_gain = jnp.sum(dh1_part * unit_all, axis=0)
     dh1 = lax.psum_scatter(
-        dot32("tq,cq->tc", dqkv, w_qkv).astype(BF16), "expert", scatter_dimension=0, tiled=True
+        dh1_part.astype(BF16), "expert", scatter_dimension=0, tiled=True
     ).astype(F32)
     _, unit_attn, scale_attn = norm_parts(inputs, attn_gain)
-    add, grad_attn_gain = norm_back(dh1, unit_attn, scale_attn, attn_gain)
+    add, _ = norm_back(dh1, unit_attn, scale_attn, attn_gain)
     grad_tokens = dx1 + add
 
-    qkv_sum = lax.psum_scatter(grad_qkv.astype(BF16), DP, scatter_dimension=0, tiled=True)
+    small_grad = jnp.concatenate(
+        [grad_router, grad_attn_gain[:, None], grad_moe_gain[:, None]], axis=1
+    )
+    small_grad = jnp.pad(small_grad, ((0, 0), (0, 128 - small_grad.shape[1])))
+    grad_all = jnp.concatenate([grad_qkv, small_grad], axis=1).astype(BF16)
+    qkv_sum = lax.psum_scatter(grad_all, DP, scatter_dimension=0, tiled=True)
     qkv_own = lax.all_to_all(
         qkv_sum.reshape(E, shard_rows, -1), "expert", split_axis=0, concat_axis=0, tiled=True
     )
     qkv_own = jnp.transpose(qkv_own, (1, 0, 2)).astype(F32)
+    small_own = jnp.sum(qkv_own[:, :, q_cols + 2 * k_cols :], axis=1)
     grad_query = qkv_own[:, :, :q_cols].reshape(shard_rows, -1)
     grad_key = qkv_own[:, :, q_cols : q_cols + k_cols].reshape(shard_rows, -1)
-    grad_value = qkv_own[:, :, q_cols + k_cols :].reshape(shard_rows, -1)
+    grad_value = qkv_own[:, :, q_cols + k_cols : q_cols + 2 * k_cols].reshape(shard_rows, -1)
     out_sum = lax.psum_scatter(grad_out.astype(BF16), DP, scatter_dimension=0, tiled=True)
     perm = [(p * E + x, dp * x + p) for p in range(dp) for x in range(E)]
     out_own = lax.ppermute(out_sum, ALL, perm).astype(F32)
-    small_grad = jnp.concatenate(
-        [grad_router, grad_attn_gain[:, None], grad_moe_gain[:, None]], axis=1
-    )
-    small_own = lax.psum_scatter(small_grad, ALL, scatter_dimension=0, tiled=True)
     return (
         outputs,
         grad_tokens,

time: 1410 us -> 923 us (0.65)
  waiting for transfers between devices: 866 us -> 281 us
  Pallas kernels: 49.4 us -> 366 us
  matrix products: 274 us -> 38.3 us
    pallas_call x0 -> x6, Pallas kernels: none -> 317 us  [the longest x2 183 us: combine_rows(): pl.pallas_call(functools.partial(combine_kernel, slots, capacity, with_dg...]
    dot_general x36 -> x10, matrix products: 229 us -> 33.1 us  [dot32(): return jnp.einsum(spec, a, b, preferred_element_type=F32)]
    reduce_scatter x4 -> x2, waiting for transfers between devices: 166 us -> 0.01 us  [the longest x1 0.01 us: shards(): qkv_sum = lax.psum_scatter(grad_all, DP, scatter_dimension=0, tiled=True)]
    unnamed x16 -> x8, waiting for transfers between devices: 149 us -> 2.96 us
    all_to_all x3 -> x5, waiting for transfers between devices: 290 us -> 152 us  [shards(): lax.all_to_all(a, DP, split_axis=0, concat_axis=0, tiled=True)]
    all_gather x2 -> x0, waiting for transfers between devices: 94.6 us -> none  [the longest x1 66.2 us: shards(): lax.all_gather(h2, GROUP, axis=0, tiled=True)]
    dot_general x9 -> x0, matrix products: 39.9 us -> none  [the longest x3 15.1 us: shards(): ga = jnp.dot(rows, wg, preferred_element_type=F32)]
    all_to_all x0 -> x1, blocking collectives: none -> 25 us  [shards(): lax.all_to_all(a, DP, split_axis=0, concat_axis=0, tiled=True)]
  transfers between devices with their start and end apart: 20 -> 16, of which waited for: 14 -> 8; matrix products, arithmetic and copies ran while one was open for 15% -> 10% of each run, Pallas kernels for 4% -> 18%
where the time goes in v2:
time: 923 us; the launch traced here: 907 us
  Pallas kernels  366 us (40%)
  waiting for transfers between devices  281 us (30%)
  blocking collectives  94.9 us (10%)
  other arithmetic  44.1 us (5%)
  matrix products  38.3 us (4%)
  local copies, waits for them, and re-layouts  34.5 us (4%)
  starting transfers between devices  32.8 us (4%)
  between operations  15.5 us (2%)
    pallas_call x2, Pallas kernels, combine_rows(): pl.pallas_call(functools.partial(combine_kernel, slots, capacity, with_dg...  183 us
    all_to_all x5, waiting for transfers between devices, shards(): lax.all_to_all(a, DP, split_axis=0, concat_axis=0, tiled=True)  152 us
    pallas_call x1, Pallas kernels, gather_rows(): pl.pallas_call(functools.partial(gather_kernel, slots, capacity), out_sha...  72.5 us
    all_gather x1, waiting for transfers between devices, shards(): lax.all_gather(cotangent, GROUP, axis=0, tiled=True)  70.3 us
    pallas_call x3, Pallas kernels, expert_call(): pl.pallas_call(functools.partial(expert_kernel, chunks, dp), grid_spec=pl...  61 us
    all_gather x1, blocking collectives, shards(): small = lax.all_gather(small, ALL, axis=0, tiled=True)  43 us
    dot_general x10, matrix products, dot32(): return jnp.einsum(spec, a, b, preferred_element_type=F32)  33.1 us
    all_gather x1, waiting for transfers between devices, shards(): x_all = lax.all_gather(tokens, 'expert', axis=0, tiled=True)  28.5 us
  transfers between devices with their start and end apart: 16, of which 8 were waited for; matrix products, arithmetic and copies ran while one was open for 10% of the time, Pallas kernels for 18%

profile of v2, /device:TPU:0, one launch (start us, length us, event | category | flops | bytes accessed | tf_op | source)
XLA Modules:
  0.0 907.1 jit_solution(8552450743864111979)
XLA Ops:
  9.1 10.0 %all_to_all.88 = bf16[48,4,640]{2,0,1:T(8,128)(2,1)} all-to-all(bf16[48,4,640]{2,0,1:T(8,128)(2,1)S(1)} %pad_maximum_fusion.8), channel_id=1, replica_groups=mesh['q'=2,'r'=4,'expert'=4] {'expert'}, dimensions={1} | all-to-all | bytes 491520 | tf_op jit(solution)/shard_map/all_to_all | solution.py:528
  26.3 43.0 %all_gather.19 = bf16[1536,42]{1,0:T(8,128)(2,1)S(1)} all-gather(bf16[48,42]{1,0:T(8,128)(2,1)S(1)} %pad_maximum_fusion.13), channel_id=1, replica_groups=mesh['q'=2,'r'=4,'expert'=4] {'q','r','expert'}, dimensions={0}, use_global_device_ids=true | all-gather | bytes 133056 | tf_op jit(solution)/shard_map/all_gather | solution.py:533
  73.6 28.5 %all-gather.6.cloned.1.call-done.x_ref = bf16[1280,1536]{1,0:T(8,128)(2,1)} async-done(((bf16[320,1536]{1,0:T(8,128)(2,1)}), bf16[1280,1536]{1,0:T(8,128)(2,1)}) %all-gather.6.cloned.1.call-update) | async-done | bytes 3932176 | tf_op jit(solution)/shard_map/all_gather | solution.py:531
  102.1 24.7 %attention_forward.1 = (bf16[1280,1536]{1,0:T(8,128)(2,1)}, bf16[6,1280,64]{2,1,0:T(8,128)(2,1)}, bf16[2,1280,64]{2,1,0:T(8,128)(2,1)}, bf16[2,1280,64]{2,1,0:T(...) custom-call(bf16[1280,1536]{1,0:T(8,128)(2,1)} %all-gather.6.cloned.1.call-done.x_ref, ...), custom_call_target="tpu_custom_call" | custom-call | flops 7549747200 | bytes 14680064 | tf_op jit(solution)/shard_map/attention_forward/pallas_call | solution.py:127
  126.8 3.9 all-to-all-start.1
  130.9 2.9 fusion.5.wd_ref
  133.9 2.9 fusion.4.wu_ref
  136.8 3.0 fusion.3.wg_ref
  140.3 4.8 all-to-all-done.1
  146.2 22.6 %all-gather.10.cloned.1.call-done = bf16[1536,1536]{1,0:T(8,128)(2,1)} async-done(((bf16[48,1536]{1,0:T(8,128)(2,1)}), bf16[1536,1536]{1,0:T(8,128)(2,1)}) %all-gather.10.cloned.1.call-update) | async-done | bytes 4718608 | tf_op jit(solution)/shard_map/all_gather | solution.py:537
  168.8 4.4 multiply_reduce_fusion.2
  183.0 70.3 %all-gather.12.cloned.1.call-done = bf16[5120,1536]{1,0:T(8,128)(2,1)} async-done(((bf16[320,1536]{1,0:T(8,128)(2,1)}), bf16[5120,1536]{1,0:T(8,128)(2,1)}) %all-gather.12.cloned.1.call-update) | async-done | bytes 15728656 | tf_op jit(solution)/shard_map/all_gather | solution.py:538
  253.3 72.5 %gather_rows.1 = (bf16[3,1024,1536]{2,1,0:T(8,128)(2,1)}, bf16[3,1024,1536]{2,1,0:T(8,128)(2,1)}, f32[3,1024,1]{2,1,0:T(8,128)}, f32[16,8,320]{2,1,0:T(8,128)}) custom-call(bf16[320,1536]{1,0:T(8,128)(2,1)} %copy-done.7, f32[16,8,320]{2,1,0:T(8,128)} %pad_maximum_fusion.9.table_ref, bf16[16,320,1536]{2,1,0:T(8,128)(2,1)} %bitcast.243), custom_call_target="tpu_custom_call" | custom-call | flops 6039797760 | bytes 62914560 | tf_op jit(solution)/shard_map/gather_rows/pallas_call | solution.py:316
  325.8 23.2 %expert.4 = (bf16[1024,1536]{1,0:T(8,128)(2,1)}, bf16[1024,1536]{1,0:T(8,128)(2,1)}, f32[1024,1]{1,0:T(8,128)}, bf16[8,384,512]{2,1,0:T(8,128)(2,1)}, bf16[512,1536]{1,0:T(8,128)(2,1)}) custom-call(s32[1]{0:T(128)} %bitcast.36.place_ref, bf16[3,1024,1536]{2,1,0:T(8,128)(2,1)} %get-tuple-element.40.x_ref, bf16[3,1024,1536]{2,1,0:T(8,128)(2,1)} %get-tuple-element.41.dm_ref, ...), custom_call_target="tpu_custom_call" | custom-call | flops 14495514624 | bytes 25165824 | tf_op jit(solution)/shard_map/expert/pallas_call | solution.py:370
  349.0 23.7 %expert.3 = (bf16[1024,1536]{1,0:T(8,128)(2,1)}, bf16[1024,1536]{1,0:T(8,128)(2,1)}, f32[1024,1]{1,0:T(8,128)}, bf16[8,384,512]{2,1,0:T(8,128)(2,1)}, bf16[512,1536]{1,0:T(8,128)(2,1)}) custom-call(s32[1]{0:T(128)} %bitcast.9.place_ref, bf16[3,1024,1536]{2,1,0:T(8,128)(2,1)} %get-tuple-element.40.x_ref, bf16[3,1024,1536]{2,1,0:T(8,128)(2,1)} %get-tuple-element.41.dm_ref, ...), custom_call_target="tpu_custom_call" | custom-call | flops 14495514624 | bytes 25165824 | tf_op jit(solution)/shard_map/expert/pallas_call | solution.py:370
  372.7 14.1 %expert.5 = (bf16[1024,1536]{1,0:T(8,128)(2,1)}, bf16[1024,1536]{1,0:T(8,128)(2,1)}, f32[1024,1]{1,0:T(8,128)}, bf16[8,384,256]{2,1,0:T(8,128)(2,1)}, bf16[256,1536]{1,0:T(8,128)(2,1)}) custom-call(s32[1]{0:T(128)} %constant.142.clone.1.place_ref, bf16[3,1024,1536]{2,1,0:T(8,128)(2,1)} %get-tuple-element.40.x_ref, ...), custom_call_target="tpu_custom_call" | custom-call | flops 7247757312 | bytes 25165824 | tf_op jit(solution)/shard_map/expert/pallas_call | solution.py:370
  386.9 66.1 %combine_with_dg.1 = (f32[320,1536]{1,0:T(8,128)}, f32[16,8,320]{2,1,0:T(8,128)}) custom-call(bf16[1024,1536]{1,0:T(8,128)(2,1)} %get-tuple-element.47.refs_0_, bf16[1024,1536]{1,0:T(8,128)(2,1)} %get-tuple-element.48.refs_1_, bf16[1024,1536]{1,0:T(8,128)(2,1)} %get-tuple-element.49.refs_2_, f32[16,8,320]{2,1,0:T(8,128)} %get-tuple-element.46.refs_3_, ...), custom_call_target="tpu_custom_call" | custom-call | flops 3019898880 | bytes 41943040 | tf_op jit(solution)/shard_map/combine_with_dg/pallas_call | solution.py:490
  453.0 2.2 gather_fusion.8
  459.3 2.5 multiply_reduce_fusion
  464.7 4.4 convolution_convert_fusion.2
  469.6 16.9 %all_to_all.89 = bf16[320,4,384]{2,0,1:T(8,128)(2,1)} all-to-all(bf16[320,4,384]{2,0,1:T(8,128)(2,1)S(1)} %bitcast.206), channel_id=1, replica_groups=mesh['q'=2,'r'=4,'expert'=4] {'expert'}, dimensions={1} | all-to-all | bytes 1966080 | tf_op jit(solution)/shard_map/all_to_all | solution.py:660
  486.5 25.0 %all_to_all.90 = bf16[8,32,1536]{2,1,0:T(8,128)(2,1)} all-to-all(bf16[8,32,1536]{2,1,0:T(8,128)(2,1)S(1)} %bitcast.217), channel_id=1, replica_groups=mesh['q'=2,'r'=4,'expert'=4] {'q','r'}, dimensions={0} | all-to-all | bytes 1572864 | tf_op jit(solution)/shard_map/all_to_all | solution.py:613
  511.5 4.3 all-to-all-start.6
  516.4 35.6 %all-to-all-done.6 = bf16[8,384,256]{2,1,0:T(8,128)(2,1)} async-done(((bf16[8,384,256]{2,1,0:T(8,128)(2,1)}), bf16[8,384,256]{2,1,0:T(8,128)(2,1)}, u32[]{:S(2)}, u32[]{:S(2)}) %all-to-all-start.6) | async-done | bytes 1572896 | tf_op jit(solution)/shard_map/all_to_all | solution.py:613
  552.0 4.3 all-to-all-start.8
  556.3 3.0 fusion
  559.7 24.5 %attention_backward.1 = bf16[1280,640]{1,0:T(8,128)(2,1)} custom-call(bf16[6,1280,64]{2,1,0:T(8,128)(2,1)} %get-tuple-element.55.q_ref, bf16[2,1280,64]{2,1,0:T(8,128)(2,1)} %get-tuple-element.56.k_ref, bf16[2,1280,64]{2,1,0:T(8,128)(2,1)} %get-tuple-element.57.v_ref, bf16[1280,384]{1,0:T(8,128)(2,1)} %bitcast.213, f32[8,1280]{1,0:T(8,128)} %get-tuple-element.58.lse_ref, ...), custom_call_target="tpu_custom_call" | custom-call | flops 12582912000 | bytes 10485760 | tf_op jit(solution)/shard_map/attention_backward/pallas_call | solution.py:179
  584.2 8.6 all-to-all-done.8
  592.8 4.3 all-to-all-start.7
  597.2 8.6 fusion.2
  605.8 2.8 convolution_convert_fusion
  610.2 4.3 copy.196
  614.5 35.9 %all-to-all-done.7 = bf16[8,64,1536]{2,1,0:T(8,128)(2,1)} async-done(((bf16[8,64,1536]{2,1,0:T(8,128)(2,1)}), bf16[8,64,1536]{2,1,0:T(8,128)(2,1)}, u32[]{:S(2)}, u32[]{:S(2)}) %all-to-all-start.7) | async-done | bytes 1572896 | tf_op jit(solution)/shard_map/all_to_all | solution.py:613
  650.4 4.4 all-to-all-start.5
  654.9 5.1 convolution_convert_fusion.1
  660.1 71.8 %all-to-all-done.5 = bf16[8,384,512]{2,1,0:T(8,128)(2,1)} async-done(((bf16[8,384,512]{2,1,0:T(8,128)(2,1)}), bf16[8,384,512]{2,1,0:T(8,128)(2,1)}, u32[]{:S(2)}, u32[]{:S(2)}) %all-to-all-start.5) | async-done | bytes 3145760 | tf_op jit(solution)/shard_map/all_to_all | solution.py:613
  731.8 4.4 all-to-all-start.4
  737.3 117.0 %combine_rows.1 = f32[320,1536]{1,0:T(8,128)} custom-call(bf16[1024,1536]{1,0:T(8,128)(2,1)} %get-tuple-element.43.refs_0_, bf16[1024,1536]{1,0:T(8,128)(2,1)} %get-tuple-element.44.refs_1_, bf16[1024,1536]{1,0:T(8,128)(2,1)} %get-tuple-element.45.refs_2_, f32[16,8,320]{2,1,0:T(8,128)} %get-tuple-element.46.refs_3_), custom_call_target="tpu_custom_call" | custom-call | flops 3019898880 | bytes 41943040 | tf_op jit(solution)/shard_map/combine_rows/pallas_call | solution.py:490
  856.7 1.9 convert_reduce_fusion.2
  862.1 2.2 pad_maximum_fusion.2
  864.3 4.5 convert_reduce_fusion
  868.8 3.7 all-to-all-start.3
  872.5 3.0 convert_reduce_fusion.1
  877.3 2.4 pad_maximum_fusion.1
  880.8 2.4 pad_maximum_fusion
  884.1 2.8 collective-permute-start
  893.0 1.9 fusion.8
  894.9 4.9 fusion.11
  (198 shorter events, 51.3 us)
Async XLA Ops:
  7.2 1.1 copy-start
  7.2 14.2 %copy-start.21 = (s32[1280]{0:T(1024)S(1)}, s32[1280]{0:T(1024)}, u32[]{:S(2)}) copy-start(s32[1280]{0:T(1024)} %param.34) | copy-start | bytes 15364
  7.2 66.4 %all-gather.8.cloned.1.call-start = ((), (), s32[]{:S(2)}) async-start(), calls=%async_computation.14 | async-start | bytes 2211840 | tf_op jit(solution)/shard_map/all_gather | solution.py:530
  7.3 14.8 %copy-start.20 = (bf16[48,40]{0,1:T(8,128)(2,1)S(1)}, bf16[48,40]{0,1:T(8,128)(2,1)}, u32[]{:S(2)}) copy-start(bf16[48,40]{0,1:T(8,128)(2,1)} %param.28) | copy-start | bytes 11524
  7.3 14.8 %copy-start.26 = (bf16[48]{0:T(256)(128)(2,1)S(1)}, bf16[48]{0:T(256)(128)(2,1)}, u32[]{:S(2)}) copy-start(bf16[48]{0:T(256)(128)(2,1)} %param.29) | copy-start | bytes 292
  7.3 14.9 %copy-start.27 = (bf16[48]{0:T(256)(128)(2,1)S(1)}, bf16[48]{0:T(256)(128)(2,1)}, u32[]{:S(2)}) copy-start(bf16[48]{0:T(256)(128)(2,1)} %param.30) | copy-start | bytes 292
  7.3 15.0 %copy-start.18 = (s32[320,8]{0,1:T(8,128)S(1)}, s32[320,8]{0,1:T(8,128)}, u32[]{:S(2)}) copy-start(s32[320,8]{0,1:T(8,128)} %param.36) | copy-start | bytes 30724
  7.3 15.0 %copy-start.19 = (s32[320,8]{0,1:T(8,128)S(1)}, s32[320,8]{0,1:T(8,128)}, u32[]{:S(2)}) copy-start(s32[320,8]{0,1:T(8,128)} %param.35) | copy-start | bytes 30724
  19.2 83.0 %all-gather.6.cloned.1.call-start = ((), (), s32[]{:S(2)}) async-start(), calls=%async_computation.13 | async-start | bytes 4915200 | tf_op jit(solution)/shard_map/all_gather | solution.py:531
  19.9 3.2 copy-start.31
  19.9 3.8 copy-start.30
  19.9 4.4 copy-start.29
  20.0 5.0 copy-start.28
  20.0 148.9 %all-gather.10.cloned.1.call-start = ((), (), s32[]{:S(2)}) async-start(), calls=%async_computation.15 | async-start | bytes 4866048 | tf_op jit(solution)/shard_map/all_gather | solution.py:537
  20.7 232.6 %all-gather.12.cloned.1.call-start = ((), (), s32[]{:S(2)}) async-start(), calls=%async_computation.16 | async-start | bytes 16711680 | tf_op jit(solution)/shard_map/all_gather | solution.py:538
  25.0 46.2 %copy-start.24 = (s32[1024]{0:T(1024)}, s32[1024]{0:T(1024)S(1)}, u32[]{:S(2)}) copy-start(s32[1024]{0:T(1024)S(1)} %pad_clamp_fusion.4) | copy-start | bytes 12292
  69.9 2.5 copy-start.14
  73.6 57.2 %copy-start.16 = (s32[2,256]{1,0:T(2,128)}, s32[2,256]{1,0:T(2,128)S(1)}, u32[]{:S(2)}) copy-start(s32[2,256]{1,0:T(2,128)S(1)} %broadcast_add_fusion.2) | copy-start | bytes 6148
  126.8 18.3 %all-to-all-start.1 = ((bf16[4,320,384]{2,1,0:T(8,128)(2,1)}), bf16[4,320,384]{2,1,0:T(8,128)(2,1)S(1)}, u32[]{:S(2)}, u32[]{:S(2)}) async-start(bf16[4,320,384]{2,1,0:T(8,128)(2,1)} %bitcast.212), calls=%async_computation.1 | async-start | bytes 1966080 | tf_op jit(solution)/shard_map/all_to_all | solution.py:567
  136.8 32.1 %copy-start.4 = (bf16[320,1536]{1,0:T(8,128)(2,1)S(1)}, bf16[320,1536]{1,0:T(8,128)(2,1)}, u32[]{:S(2)}) copy-start(bf16[320,1536]{1,0:T(8,128)(2,1)} %param.23) | copy-start | bytes 2949124
  173.5 1.0 copy-start.7
  386.9 68.3 %copy-start.25 = (pred[16]{0:T(512)(128)(4,1)S(1)}, pred[16]{0:T(512)(128)(4,1)}, u32[]{:S(2)}) copy-start(pred[16]{0:T(512)(128)(4,1)} %compare_and_fusion) | copy-start | bytes 52
  459.3 3.8 copy-start.6
  461.8 1.3 copy-start.2
  469.1 17.4 %copy-start.13 = (bf16[256,1536]{1,0:T(8,128)(2,1)S(1)}, bf16[256,1536]{1,0:T(8,128)(2,1)}, u32[]{:S(2)}) copy-start(bf16[256,1536]{1,0:T(8,128)(2,1)} %get-tuple-element.65) | copy-start | bytes 2359300
  511.5 40.5 %all-to-all-start.6 = ((bf16[8,384,256]{2,1,0:T(8,128)(2,1)}), bf16[8,384,256]{2,1,0:T(8,128)(2,1)}, u32[]{:S(2)}, u32[]{:S(2)}) async-start(bf16[8,384,256]{2,1,0:T(8,128)(2,1)} %get-tuple-element.62), calls=%async_computation.8 | async-start | bytes 3145728 | tf_op jit(solution)/shard_map/all_to_all | solution.py:613
  515.8 139.1 %all-gather.14.cloned.1.call-start = ((), (), s32[]{:S(2)}) async-start(), calls=%async_computation.18 | async-start | bytes 4915200 | tf_op jit(solution)/shard_map/all_gather | solution.py:658
  552.0 40.8 %all-to-all-start.8 = ((bf16[8,64,1536]{2,1,0:T(8,128)(2,1)}), bf16[8,64,1536]{2,1,0:T(8,128)(2,1)}, u32[]{:S(2)}, u32[]{:S(2)}) async-start(bf16[8,64,1536]{2,1,0:T(8,128)(2,1)} %bitcast.211), calls=%async_computation.10 | async-start | bytes 3145728 | tf_op jit(solution)/shard_map/all_to_all | solution.py:613
  556.3 3.1 copy-start.8
  592.8 57.5 %all-to-all-start.7 = ((bf16[8,64,1536]{2,1,0:T(8,128)(2,1)}), bf16[8,64,1536]{2,1,0:T(8,128)(2,1)}, u32[]{:S(2)}, u32[]{:S(2)}) async-start(bf16[8,64,1536]{2,1,0:T(8,128)(2,1)} %bitcast.210), calls=%async_computation.9 | async-start | bytes 3145728 | tf_op jit(solution)/shard_map/all_to_all | solution.py:613
  597.1 271.7 %reduce-scatter.10.cloned.1.call-start = ((), (), s32[]{:S(2)}) async-start(), calls=%async_computation.20 | async-start | bytes 2654208 | tf_op jit(solution)/shard_map/reduce_scatter | solution.py:679
  597.2 8.7 copy-start.32
  597.2 8.7 copy-start.33
  650.4 81.5 %all-to-all-start.5 = ((bf16[8,384,512]{2,1,0:T(8,128)(2,1)}), bf16[8,384,512]{2,1,0:T(8,128)(2,1)}, u32[]{:S(2)}, u32[]{:S(2)}) async-start(bf16[8,384,512]{2,1,0:T(8,128)(2,1)} %get-tuple-element.61), calls=%async_computation.7 | async-start | bytes 6291456 | tf_op jit(solution)/shard_map/all_to_all | solution.py:613
  654.8 229.2 %reduce-scatter.8.cloned.1.call-start = ((), (), s32[]{:S(2)}) async-start(), calls=%async_computation.19 | async-start | bytes 1327104 | tf_op jit(solution)/shard_map/reduce_scatter | solution.py:688
  731.8 137.0 %all-to-all-start.4 = ((bf16[8,384,512]{2,1,0:T(8,128)(2,1)}), bf16[8,384,512]{2,1,0:T(8,128)(2,1)}, u32[]{:S(2)}, u32[]{:S(2)}) async-start(bf16[8,384,512]{2,1,0:T(8,128)(2,1)} %get-tuple-element.60), calls=%async_computation.6 | async-start | bytes 6291456 | tf_op jit(solution)/shard_map/all_to_all | solution.py:613
  736.3 156.7 %reduce-scatter.6.cloned.1.call-start = ((), (), s32[]{:S(2)}) async-start(), calls=%async_computation.17 | async-start | bytes 4915200 | tf_op jit(solution)/shard_map/reduce_scatter | solution.py:667
  737.3 117.0 %copy-start.9 = (bf16[8,32,1536]{2,1,0:T(8,128)(2,1)S(1)}, bf16[8,32,1536]{2,1,0:T(8,128)(2,1)}, u32[]{:S(2)}) copy-start(bf16[8,32,1536]{2,1,0:T(8,128)(2,1)} %all_to_all.90) | copy-start | bytes 2359300
  854.3 1.8 copy-start.17
  868.8 14.3 %all-to-all-start.3 = ((bf16[4,48,768]{2,1,0:T(8,128)(2,1)}), bf16[4,48,768]{2,1,0:T(8,128)(2,1)S(1)}, u32[]{:S(2)}, u32[]{:S(2)}) async-start(bf16[4,48,768]{2,1,0:T(8,128)(2,1)} %bitcast.224), calls=%async_computation.4 | async-start | bytes 589824 | tf_op jit(solution)/shard_map/all_to_all | solution.py:680
  872.5 3.0 copy-start.5
  876.1 1.1 copy-start.11
  879.6 1.1 copy-start.10
  883.1 9.8 %copy-start.15 = (f32[1536]{0:T(1024)S(1)}, f32[1536]{0:T(1024)}, u32[]{:S(2)}) copy-start(f32[1536]{0:T(1024)} %copy-done.14) | copy-start | bytes 18436
  883.2 0.8 copy-start.12
  884.1 7.3 collective-permute-start
  893.0 1.9 copy-start.3
  894.8 4.9 copy-start.1
  (2 other events, 1.2 us)
Sparse Core Ops, SparseCore 0:
  19.3 48.8 all-gather.7
  69.7 32.3 all-gather.5
  105.0 63.7 all-gather.9
  170.3 82.9 all-gather.11
  517.9 33.3 all-gather.13
  614.6 109.5 reduce-scatter.9
  728.2 112.1 reduce-scatter.7
  843.0 45.3 reduce-scatter.5

commit v3 on v2

v3 whole, which is shorter than its diff:
```python
import functools

import jax
import jax.numpy as jnp
from jax import lax
from jax.experimental import pallas as pl
from jax.experimental.pallas import tpu as pltpu
from jax.sharding import Mesh
from jax.sharding import PartitionSpec as P

HD = 64
QUAD = 4
F32 = jnp.float32
BF16 = jnp.bfloat16

CHEAP = pl.CostEstimate(flops=1 << 20, bytes_accessed=1 << 16, transcendentals=0)

epsilon = 1e-06
rope_base = 10000.0
masked_score = -1e30


def dot32(spec, a, b):
    return jnp.einsum(spec, a, b, preferred_element_type=F32)


def norm_parts(values, gain_row):
    scaling = lax.rsqrt(jnp.mean(values * values, axis=-1, keepdims=True) + epsilon)
    normed = values * scaling
    return (normed * gain_row, normed, scaling)


def norm_back(grad_rows, normed, scaling, gain_row):
    grad_normed = grad_rows * gain_row
    grad_gain = jnp.sum(grad_rows * normed, axis=0)
    inner_sum = jnp.mean(grad_normed * normed, axis=-1, keepdims=True)
    return (scaling * (grad_normed - normed * inner_sum), grad_gain)


def rope_tables(positions, head_size):
    frequency = rope_base ** (-2.0 * jnp.arange(head_size // 2, dtype=F32) / head_size)
    angles = positions.astype(F32)[:, None] * frequency[None, :]
    return (jnp.cos(angles), jnp.sin(angles))


def slot_dense(routes, priority, experts, capacity):
    rows, top_count = routes.shape
    hot = routes[:, :, None] == jnp.arange(experts, dtype=jnp.int32)
    rank = jnp.sum(jnp.where(hot, priority[:, :, None] + 1, 0), axis=1) - 1
    per_rank = rank[None] == jnp.arange(top_count, dtype=jnp.int32)[:, None, None]
    flat = jnp.transpose(per_rank.astype(BF16), (1, 0, 2)).reshape(rows, top_count * experts)
    index = jnp.arange(rows, dtype=jnp.int32)
    before = (index[None, :] < index[:, None]).astype(BF16)
    within = jnp.dot(before, flat, preferred_element_type=F32).reshape(rows, top_count, experts)
    totals = jnp.sum(per_rank.astype(F32), axis=1)
    base = jnp.cumsum(totals, axis=0) - totals
    slot = jnp.sum(
        jnp.where(jnp.transpose(per_rank, (1, 0, 2)), within + base[None], 0.0), axis=1
    )
    named = rank >= 0
    return named, jnp.where(named & (slot < capacity), slot, -1.0)


NT=(((1,),(1,)),((),()))
NN=(((1,),(0,)),((),()))
TN=(((0,),(0,)),((),()))

def mm(a,b,dims=NN):
    return lax.dot_general(a,b,dims,preferred_element_type=F32)

def swap_halves(x):
    lane=lax.broadcasted_iota(jnp.int32,(x.shape[0],128),1)
    low=(lane%HD)<HD//2
    parts=[]
    for c in range(x.shape[1]//128):
        g=x[:,c*128:(c+1)*128]
        parts.append(jnp.where(low,pltpu.roll(g,128-HD//2,1),pltpu.roll(g,HD//2,1)))
    return jnp.concatenate(parts,axis=1)

def bias_block(seg_row, keys, first):
    n=seg_row.shape[1]
    s=lax.broadcasted_iota(jnp.int32,(keys,n),0)
    t=lax.broadcasted_iota(jnp.int32,(keys,n),1)+first
    return jnp.where((s<=t)&(s>=seg_row),0.0,masked_score)

MESH=pl.DeviceIdType.MESH
CORE = 1
GATHER_ORDERS = ((2, 4, 8), (4, 8, 2), (8, 2, 4))
SUM_ORDERS = ((4, 2, 8), (2, 4, 8))

def member_r():
    return lax.axis_index("rh") * 2 + lax.axis_index("rl")

def device_at(q, r, e):
    return (q, r // 2, r % 2, e)

def place_at(q, r):
    return q * QUAD + r

def flip(value, mask):
    low, high = value % 2, value // 2
    if mask & 1:
        low = 1 - low
    if mask & 2:
        high = 1 - high
    return high * 2 + low

def group_device(mask):
    return device_at(lax.axis_index("q"), flip(member_r(), mask >> 2), flip(lax.axis_index("expert"), mask & 3))

def group_member(mask):
    return flip(member_r(), mask >> 2) * 4 + flip(lax.axis_index("expert"), mask & 3)

def greet(masks):
    barrier = pltpu.get_barrier_semaphore()
    for mask in masks:
        pl.semaphore_signal(barrier, inc=1, device_id=group_device(mask), device_id_type=MESH)
    pl.semaphore_wait(barrier, len(masks))

def last_hop(part, mask):
    if mask & CORE:
        return CORE
    return [bit for bit in GATHER_ORDERS[part] if mask & bit][-1]

def gather_order():
    free = {2: 0.0, 4: 0.0, 8: 0.0}
    arrived, todo = {(p, 0): 0.0 for p in range(len(GATHER_ORDERS))}, [(p, m) for p in range(len(GATHER_ORDERS)) for m in range(2, 16, 2)]
    order = []
    while todo:
        best = None
        for p, m in todo:
            hop = last_hop(p, m)
            if (p, m ^ hop) in arrived:
                key = (max(free[hop], arrived[p, m ^ hop]), GATHER_ORDERS[p].index(hop), p, m)
                if best is None or key < best:
                    best = key
        start, _, p, m = best
        hop = last_hop(p, m)
        free[hop] = start + 1
        arrived[p, m] = start + 1
        todo.remove((p, m))
        order.append((start + 1, p, m))
    return [(p, m) for _, p, m in sorted(order)]

def one_hot(table, capacity, slots):
    place = lax.broadcasted_iota(jnp.int32, (capacity, table.shape[1]), 0).astype(F32)
    return [table[k:k + 1, :] == place for k in range(slots)]

def gather_kernel(slots, capacity, h2_ref, table_ref, dm_ref, rows_ref, dm_rows_ref, weight_ref, tables_ref,
                  held, arrived, dm_held, send, recv, table_send, table_recv, dm_sem):
    width = h2_ref.shape[1]
    part_width = width // len(GATHER_ORDERS)
    greet(range(1, 16))
    tables = []
    for mask in range(1, 16):
        copy = pltpu.make_async_remote_copy(table_ref.at[group_member(mask)], arrived.at[mask],
            table_send.at[mask], table_recv.at[mask], device_id=group_device(mask), device_id_type=MESH)
        copy.start()
        tables.append(copy)
    arrived[0] = table_ref[group_member(0)]
    copies = {}
    for p in range(len(GATHER_ORDERS)):
        for mask in range(1, 16):
            hop = last_hop(p, mask)
            source = mask ^ hop
            src = h2_ref.at[:, pl.ds(p * part_width, part_width)] if source == 0 else held.at[p, source]
            copies[p, mask] = pltpu.make_async_remote_copy(src, held.at[p, mask], send.at[p, mask], recv.at[p, mask],
                device_id=group_device(hop), device_id_type=MESH)
    order = gather_order()
    for p, mask in order + [(p, CORE) for p in range(len(GATHER_ORDERS))]:
        if mask ^ last_hop(p, mask) == 0:
            copies[p, mask].start()
    def dm_copy(mask):
        return pltpu.make_async_copy(dm_ref.at[group_member(mask)], dm_held.at[mask % 2], dm_sem.at[mask % 2])
    dm_copy(0).start()
    for copy in tables:
        copy.wait_recv()
    def hots(mask):
        return one_hot(arrived[mask], capacity, slots)
    def place(target, mask, hot, block, columns):
        got = mm(jnp.concatenate([h.astype(BF16) for h in hot], axis=0), block).astype(BF16)
        for k in range(slots):
            target[k, pl.ds(mask * capacity, capacity), columns] = got[k * capacity:(k + 1) * capacity]
    def dm_step(mask):
        if mask + 1 < 16:
            dm_copy(mask + 1).start()
        dm_copy(mask).wait()
        hot = hots(mask)
        place(dm_rows_ref, mask, hot, dm_held[mask % 2], slice(None))
        if mask == 0:
            place(rows_ref, 0, hot, h2_ref[...], slice(None))
        table = arrived[mask]
        for k in range(slots):
            weight_ref[k, pl.ds(mask * capacity, capacity), :] = jnp.sum(
                jnp.where(hot[k], table[4 + k:5 + k, :], 0.0), axis=1, keepdims=True)
        tables_ref[mask] = table
    todo = list(range(16))
    dm_step(todo.pop(0))
    dm_step(todo.pop(0))
    def arrive(p, mask):
        copies[p, mask].wait_recv()
        for nxt in range(1, 16):
            if nxt != mask and (nxt ^ last_hop(p, nxt)) == mask:
                copies[p, nxt].start()
        place(rows_ref, mask, hots(mask), held[p, mask], pl.ds(p * part_width, part_width))
    for step, (p, mask) in enumerate(order):
        arrive(p, mask)
        if todo:
            dm_step(todo.pop(0))
    for p in range(len(GATHER_ORDERS)):
        arrive(p, CORE)
    for p, mask in order:
        arrive(p, mask | CORE)
    for copy in tables:
        copy.wait_send()
    for key in copies:
        copies[key].wait_send()

def gather_rows(h2, table, dm_all, slots, capacity, collective_id):
    tokens, width = h2.shape
    V = pl.BlockSpec(memory_space=pltpu.VMEM)
    rows = jax.ShapeDtypeStruct((slots, 16 * capacity, width), BF16)
    return pl.pallas_call(functools.partial(gather_kernel, slots, capacity),
        out_shape=(rows, rows, jax.ShapeDtypeStruct((slots, 16 * capacity, 1), F32), jax.ShapeDtypeStruct(table.shape, F32)),
        in_specs=[V, V, pl.BlockSpec(memory_space=pl.ANY)], out_specs=(V,) * 4,
        scratch_shapes=[pltpu.VMEM((len(GATHER_ORDERS), 16, tokens, width // len(GATHER_ORDERS)), BF16), pltpu.VMEM(table.shape, F32),
            pltpu.VMEM((2, tokens, width), BF16), pltpu.SemaphoreType.DMA((len(GATHER_ORDERS), 16)), pltpu.SemaphoreType.DMA((len(GATHER_ORDERS), 16)),
            pltpu.SemaphoreType.DMA((16,)), pltpu.SemaphoreType.DMA((16,)), pltpu.SemaphoreType.DMA((2,))],
        compiler_params=pltpu.CompilerParams(vmem_limit_bytes=58 << 20, collective_id=collective_id, has_side_effects=True),
        cost_estimate=CHEAP,
        name="gather_rows")(h2, table, dm_all)

def expert_kernel(chunks, dp, ways, s_ref, x_ref, dm_ref, weight_ref, wg_ref, wu_ref, wd_ref,
                  y_ref, dr_ref, dg_ref, grads, xs, dms, mgs, das, *banks):
    i = pl.program_id(1)
    block = x_ref.shape[1]
    if ways > 1:
        wg, wu, wd = banks
        ff = wg.shape[1]
        part = ff // dp
        @pl.when(i == 0)
        def _():
            shape = (ff * ways, ff)
            row, col = lax.broadcasted_iota(jnp.int32, shape, 0), lax.broadcasted_iota(jnp.int32, shape, 1)
            pick = (row == (col // part * ways + s_ref[s_ref.shape[0] - 1]) * part + col % part).astype(F32).astype(BF16)
            wg[...] = mm(wg_ref[0], pick).astype(BF16)
            wu[...] = mm(wu_ref[0], pick).astype(BF16)
            wd[...] = mm(pick, wd_ref[0], TN).astype(BF16)
    else:
        wg, wu, wd = wg_ref.at[0], wu_ref.at[0], wd_ref.at[0]
        ff = wg.shape[1]
    @pl.when(i < chunks)
    def _():
        x, dmr, w = x_ref[0], dm_ref[0], weight_ref[0]
        rows = pl.ds(pl.multiple_of(i * block, block), block)
        xs[rows, :] = x
        dms[rows, :] = dmr
        ga = mm(x, wg[...])
        ua = mm(x, wu[...])
        u = mm(dmr, wd[...], NT)
        sig = 1.0 / (1.0 + jnp.exp(-ga))
        silu = ga * sig
        m = silu * ua
        mg = (m * w).astype(BF16)
        dg_ref[0] = jnp.sum(m * u, axis=1, keepdims=True)
        dmh = u * w
        da = (dmh * ua * (sig * (1.0 + ga * (1.0 - sig)))).astype(BF16)
        du = (dmh * silu).astype(BF16)
        mgs[rows, :] = mg
        das[rows, :ff] = da
        das[rows, ff:] = du
        y_ref[0] = mm(mg, wd[...]).astype(BF16)
        dr_ref[0] = (mm(da, wg[...], NT) + mm(du, wu[...], NT)).astype(BF16)
    @pl.when(i == chunks)
    def _():
        width = xs.shape[1]
        share, down_share = width // dp, ff // dp
        for half in range(2):
            grad = mm(xs[...], das[:, half * ff:(half + 1) * ff], TN).astype(BF16)
            for d in range(dp):
                grads[d, 0, half * share:(half + 1) * share, :] = grad[d * share:(d + 1) * share]
        down = mm(mgs[...], dms[...], TN).astype(BF16)
        for d in range(dp):
            for c in range(width // ff):
                first = 2 * share + c * down_share
                grads[d, 0, first:first + down_share, :] = down[d * down_share:(d + 1) * down_share, c * ff:(c + 1) * ff]

def expert_call(rows, dm_rows, weight, first, count, w_gate, w_up, w_down, scalars, dp, ways, block=512):
    _, total, width = rows.shape
    ff = w_gate.shape[2] // ways
    chunks = total // block
    row = lambda n, i, s: (first + n, jnp.minimum(i, chunks - 1), 0)
    out = lambda n, i, s: (n, jnp.minimum(i, chunks - 1), 0)
    bank = lambda a: pl.BlockSpec((1,) + a.shape[1:], lambda n, i, s: (s[n], 0, 0))
    share = width // dp
    S, M = jax.ShapeDtypeStruct, pltpu.VMEM
    return pl.pallas_call(functools.partial(expert_kernel, chunks, dp, ways),
        grid_spec=pltpu.PrefetchScalarGridSpec(num_scalar_prefetch=1, grid=(count, chunks + 1),
            in_specs=[pl.BlockSpec((1, block, width), row), pl.BlockSpec((1, block, width), row), pl.BlockSpec((1, block, 1), row),
                bank(w_gate), bank(w_up), bank(w_down)],
            out_specs=(pl.BlockSpec((1, block, width), out), pl.BlockSpec((1, block, width), out), pl.BlockSpec((1, block, 1), out),
                pl.BlockSpec((dp, 1, 3 * share, ff), lambda n, i, s: (0, n, 0, 0))),
            scratch_shapes=[M((total, width), BF16), M((total, width), BF16), M((total, ff), BF16), M((total, 2 * ff), BF16)]
                + ([M((width, ff), BF16), M((width, ff), BF16), M((ff, width), BF16)] if ways > 1 else [])),
        out_shape=(S((count, total, width), BF16), S((count, total, width), BF16), S((count, total, 1), F32),
            S((dp, count, 3 * share, ff), BF16)),
        compiler_params=pltpu.CompilerParams(vmem_limit_bytes=58 << 20, dimension_semantics=("arbitrary", "arbitrary")),
        cost_estimate=CHEAP,
        name="expert_part" if ways > 1 else "experts")(scalars, rows, dm_rows, weight, w_gate, w_up, w_down)

def place_kernel(whole, rest, ways, *refs):
    moved, (gate_ref, up_ref, down_ref) = refs[:-3], refs[-3:]
    i = pl.program_id(0)
    share, down_share = gate_ref.shape[1], down_ref.shape[1]
    width, ff = down_ref.shape[2], gate_ref.shape[2]
    quads = moved[0].shape[0]
    @pl.when(i < QUAD)
    def _():
        for s in range(whole):
            block = sum(moved[0][k, 0, s].astype(F32) for k in range(quads))
            gate_ref[s] = block[:share]
            up_ref[s] = block[share:2 * share]
            for c in range(width // ff):
                first = 2 * share + c * down_share
                down_ref[s, :, c * ff:(c + 1) * ff] = block[first:first + down_share]
    if rest:
        @pl.when(i == QUAD)
        def _():
            cols = ff // ways
            part = down_share // ways
            for x in range(rest):
                gate = jnp.zeros((2 * share, ff), F32)
                for h in range(ways):
                    col = lax.broadcasted_iota(jnp.int32, (cols, ff), 0)
                    spot = (col // part * ways + h) * part + col % part
                    pick = (lax.broadcasted_iota(jnp.int32, (cols, ff), 1) == spot).astype(F32).astype(BF16)
                    down = jnp.zeros((share, cols), F32)
                    for k in range(quads):
                        block = moved[1][k, x * ways + h, 0]
                        gate = gate + mm(block[:2 * share], pick)
                        down = down + block[2 * share:].astype(F32)
                    for c in range(width // cols):
                        down_ref[x, h * part:(h + 1) * part, c * cols:(c + 1) * cols] = down[c * part:(c + 1) * part]
                gate_ref[x] = gate[:share]
                up_ref[x] = gate[share:]

def place_call(moved, local, ffn, width):
    whole = local // QUAD
    rest = local - whole * QUAD
    ways = QUAD // rest if rest else 1
    share = moved[0].shape[2] // 3
    down_share = ffn * share // width
    quads = moved[0].shape[0] // QUAD
    steps = QUAD + (1 if rest else 0)
    moved = [a.reshape((quads, QUAD) + a.shape[1:]) for a in moved]
    one = lambda a: pl.BlockSpec((quads, 1) + a.shape[2:], lambda i: (0, jnp.minimum(i, QUAD - 1), 0, 0, 0))
    full = lambda a: pl.BlockSpec(a.shape, lambda i: (0, 0, 0, 0, 0))
    out = lambda a, b: pl.BlockSpec((whole, a, b), lambda i: (i, 0, 0))
    S = jax.ShapeDtypeStruct
    return pl.pallas_call(functools.partial(place_kernel, whole, rest, ways), grid=(steps,),
        in_specs=[one(moved[0])] + [full(a) for a in moved[1:]],
        out_specs=(out(share, ffn), out(share, ffn), out(down_share, width)),
        out_shape=(S((local, share, ffn), F32), S((local, share, ffn), F32), S((local, down_share, width), F32)),
        compiler_params=pltpu.CompilerParams(vmem_limit_bytes=58 << 20, dimension_semantics=("arbitrary",)),
        cost_estimate=CHEAP, name="place_gradients")(*moved)

def first_hop(part, mask):
    return [bit for bit in SUM_ORDERS[part] if mask & bit][0]

def combine_kernel(banks, slots, capacity, with_dg, *refs):
    rows = refs[:banks]
    refs = refs[banks:]
    tables_ref = refs[0]
    refs = refs[1:]
    if with_dg:
        dg_refs, refs = refs[:banks], refs[banks:]
        out_ref, dg_out = refs[:2]
        refs = refs[2:]
    else:
        out_ref, refs = refs[0], refs[1:]
    core_out, core_in, held, got, core_send, core_recv, send, recv = refs[:8]
    if with_dg:
        dg_hold, dg_in, dg_send, dg_recv = refs[8:]
    width = out_ref.shape[1]
    part_width = width // len(SUM_ORDERS)
    greet(range(1, 16) if with_dg else (1, 2, 4, 8))
    def hots(mask):
        return one_hot(tables_ref[mask], capacity, slots)
    def block_sum(mask, hot):
        return mm(jnp.concatenate([h.astype(BF16) for h in hot], axis=0),
            jnp.concatenate([a[n, pl.ds(mask * capacity, capacity), :] for a in rows for n in range(a.shape[0])], axis=0), TN)
    dg_copies = []
    def dg_step(mask, hot):
        if not with_dg:
            return
        for k in range(slots):
            col = [(a, n) for a in dg_refs for n in range(a.shape[0])][k]
            col = col[0][col[1], pl.ds(mask * capacity, capacity), :]
            dg_hold[mask, k:k + 1, :] = jnp.sum(jnp.where(hot[k], col, 0.0), axis=0, keepdims=True)
        if mask == 0:
            return
        copy = pltpu.make_async_remote_copy(dg_hold.at[mask], dg_in.at[mask], dg_send.at[mask], dg_recv.at[mask],
            device_id=group_device(mask), device_id_type=MESH)
        copy.start()
        dg_copies.append(copy)
    listed = sorted(range(0, 16, 2), key=lambda m: (-bin(m).count("1"), m))
    if with_dg:
        dg_hold[...] = jnp.zeros_like(dg_hold)
    core = {}
    for mask in listed:
        hot = hots(mask | CORE)
        core_out[mask // 2] = block_sum(mask | CORE, hot).astype(BF16)
        core[mask] = pltpu.make_async_remote_copy(core_out.at[mask // 2], core_in.at[mask // 2], core_send.at[mask // 2],
            core_recv.at[mask // 2], device_id=group_device(CORE), device_id_type=MESH)
        core[mask].start()
        dg_step(mask | CORE, hot)
    copies = {}
    for p in range(len(SUM_ORDERS)):
        for mask in range(2, 16, 2):
            copies[p, mask] = pltpu.make_async_remote_copy(held.at[p, mask // 2], got.at[p, mask // 2], send.at[p, mask // 2],
                recv.at[p, mask // 2], device_id=group_device(first_hop(p, mask)), device_id_type=MESH)
    for mask in listed:
        hot = hots(mask)
        own = block_sum(mask, hot)
        core[mask].wait_recv()
        own = (own + core_in[mask // 2].astype(F32)).astype(BF16)
        for p in range(len(SUM_ORDERS)):
            held[p, mask // 2] = own[:, p * part_width:(p + 1) * part_width]
            if mask & SUM_ORDERS[p][0]:
                copies[p, mask].start()
        dg_step(mask, hot)
    def add(p, target, sources):
        total = held[p, target // 2].astype(F32)
        for source in sources:
            copies[p, source].wait_recv()
            total = total + got[p, source // 2].astype(F32)
        return total
    def forward(p, target, sources):
        held[p, target // 2] = add(p, target, sources).astype(BF16)
        copies[p, target].start()
    for both in (True, False):
        for p in range(len(SUM_ORDERS)):
            a, b, c = SUM_ORDERS[p]
            target = b | c if both else b
            forward(p, target, [target | a])
    for p in range(len(SUM_ORDERS)):
        a, b, c = SUM_ORDERS[p]
        forward(p, c, [c | a, c | b])
    for p in range(len(SUM_ORDERS)):
        a, b, c = SUM_ORDERS[p]
        out_ref[:, p * part_width:(p + 1) * part_width] = add(p, 0, [a, b, c])
    if with_dg:
        dg_out[0] = dg_hold[0]
        for copy in dg_copies:
            copy.wait_recv()
        for mask in range(1, 16):
            dg_out[mask] = dg_in[mask]
        for copy in dg_copies:
            copy.wait_send()
    for mask in listed:
        core[mask].wait_send()
    for key in copies:
        copies[key].wait_send()

def combine_rows(rows, tables, dgs, capacity, collective_id):
    banks, slots = len(rows), sum(a.shape[0] for a in rows)
    tokens, width = tables.shape[2], rows[0].shape[2]
    V = pl.BlockSpec(memory_space=pltpu.VMEM)
    with_dg = dgs is not None
    out = jax.ShapeDtypeStruct((tokens, width), F32)
    table = pltpu.VMEM(tables.shape, F32)
    sem = pltpu.SemaphoreType.DMA
    return pl.pallas_call(functools.partial(combine_kernel, banks, slots, capacity, with_dg),
        out_shape=(out, jax.ShapeDtypeStruct(tables.shape, F32)) if with_dg else out,
        in_specs=[V] * (banks + 1 + (banks if with_dg else 0)), out_specs=(V, V) if with_dg else V,
        scratch_shapes=[pltpu.VMEM((8, tokens, width), BF16), pltpu.VMEM((8, tokens, width), BF16),
            pltpu.VMEM((len(SUM_ORDERS), 8, tokens, width // len(SUM_ORDERS)), BF16), pltpu.VMEM((len(SUM_ORDERS), 8, tokens, width // len(SUM_ORDERS)), BF16),
            sem((8,)), sem((8,)), sem((len(SUM_ORDERS), 8)), sem((len(SUM_ORDERS), 8))] + ([table, table, sem((16,)), sem((16,))] if with_dg else []),
        compiler_params=pltpu.CompilerParams(vmem_limit_bytes=58 << 20, collective_id=collective_id, has_side_effects=True),
        cost_estimate=CHEAP,
        name="combine_with_dg" if with_dg else "combine_rows")(*rows, tables, *(dgs if with_dg else ()))


DP_ORDERS = (("q", 1, 2), ("q", 2, 1), ("q", 2, 1))


def device_experts(local, r):
    whole = local // QUAD
    rest = local - whole * QUAD
    return [r * whole + s for s in range(whole)] + ([QUAD * whole + r // (QUAD // rest)] if rest else [])


def dp_last(part, k, m):
    return [dim for dim in DP_ORDERS[part] if (k if dim == "q" else m & dim)][-1]

def dp_source(part, k, m):
    dim = dp_last(part, k, m)
    return (0, m) if dim == "q" else (k, m ^ dim)

def dp_origin(k, m):
    return place_at((lax.axis_index("q") + k) % lax.axis_size("q"), flip(member_r(), m))

def dp_copies(ref, rows, first, part_width, send, recv):
    quads = lax.axis_size("q")
    copies = {}
    for p in range(3):
        columns = pl.ds(p * part_width, part_width)
        for k in range(quads):
            for m in range(QUAD):
                if (k, m) == (0, 0):
                    continue
                dim = dp_last(p, k, m)
                block = ref.at[pl.ds(first(dp_origin(*dp_source(p, k, m))), rows), columns]
                q, r, e = lax.axis_index("q"), member_r(), lax.axis_index("expert")
                device = device_at((q + quads - k) % quads, r, e) if dim == "q" else device_at(q, flip(r, dim), e)
                copies[p, k, m] = pltpu.make_async_remote_copy(block, block, send.at[p, k, m], recv.at[p, k, m],
                    device_id=device, device_id_type=MESH)
    return copies

def dp_order(copies):
    def hops(key):
        p, k, m = key
        return (1 if k else 0) + bin(m).count("1")
    return sorted(copies, key=lambda key: (hops(key), DP_ORDERS[key[0]].index(dp_last(*key)), key[0], key))

def dp_start(copies, arrived):
    for key in dp_order(copies):
        if arrived[0] == key[0] and dp_source(*key) == arrived[1:]:
            copies[key].start()

def start_kernel(dims, exchange, *refs):
    (experts, capacity, top_count, q_cols, k_cols, rows_here, shard_rows) = dims
    (tokens_ref, pieces_ref, wout_ref, routes_ref, priority_ref, seg_ref, cos_ref, sin_ref,
     x_out, w_out, wout_out, h1_ref, q_ref, k_ref, v_ref, o_ref, lse_ref, middle_ref, h2_ref, table_ref, probs_ref, gains_ref,
     xs, ws, wouts, vt_ref, h1s, os, own_sem,
     x_send, x_recv, p_send, p_recv, w_send, w_recv, o_send, o_recv, wo_send, wo_recv, wx_send, wx_recv) = refs
    E = lax.axis_size("expert")
    quads = lax.axis_size("q")
    dp = quads * QUAD
    q, r, e = lax.axis_index("q"), member_r(), lax.axis_index("expert")
    place = place_at(q, r)
    length, width = xs.shape
    total = ws.shape[1]
    block_rows = ws.shape[0] // dp
    heads, kv_heads = q_cols // HD, k_cols // HD
    group = heads // kv_heads
    block = 256

    barrier = pltpu.get_barrier_semaphore()
    friends = [device_at(q, r, flip(e, j)) for j in (1, 2, 3)] + [device_at(q, flip(r, m), e) for m in (1, 2)]
    friends += [device_at((q + k) % quads, r, e) for k in range(1, quads)]
    for friend in friends:
        pl.semaphore_signal(barrier, inc=1, device_id=friend, device_id_type=MESH)
    pl.semaphore_wait(barrier, len(friends))

    def token_rows(who):
        return pl.ds(pl.multiple_of(who * rows_here, 16), rows_here)

    x_copies = {}
    for j in (1, 2, 3):
        source = tokens_ref if j < 3 else xs.at[token_rows(flip(e, 2))]
        target = e if j < 3 else flip(e, 2)
        x_copies[j] = pltpu.make_async_remote_copy(source, xs.at[token_rows(target)], x_send.at[j], x_recv.at[j],
            device_id=device_at(q, r, flip(e, j if j < 3 else 1)), device_id_type=MESH)
    p_copies = []
    mine = pl.multiple_of(place * block_rows, 16)
    if exchange:
        for j in (1, 2, 3):
            rows = pl.ds(pl.multiple_of(place * block_rows + e * shard_rows, 16), shard_rows)
            copy = pltpu.make_async_remote_copy(pieces_ref.at[flip(e, j)], ws.at[rows], p_send.at[j], p_recv.at[j],
                device_id=device_at(q, r, flip(e, j)), device_id_type=MESH)
            copy.start()
            p_copies.append(copy)
        ws[pl.ds(pl.multiple_of(place * block_rows + e * shard_rows, 16), shard_rows), :] = pieces_ref[e]
    else:
        ws[pl.ds(mine, block_rows), :] = pieces_ref[...]
    x_copies[2].start()
    x_copies[1].start()
    xs[token_rows(e), :] = tokens_ref[...]
    w_copies = dp_copies(ws, block_rows, lambda d: pl.multiple_of(d * block_rows, 16), total // 3, w_send, w_recv)
    for copy in p_copies:
        copy.wait_recv()
    for p in range(3):
        dp_start(w_copies, (p, 0, 0))
    wo_copies = {}
    if exchange:
        def out_row(d):
            return pl.multiple_of((d * E + e) * shard_rows, 16)
        wouts[pl.ds(out_row(place), shard_rows), :] = wout_ref[...]
        wo_copies = dp_copies(wouts, shard_rows, out_row, width // 3, wo_send, wo_recv)
        for p in range(3):
            dp_start(wo_copies, (p, 0, 0))

    lane = lax.broadcasted_iota(jnp.int32, (rows_here, 128), 1)
    rank = jnp.zeros((rows_here, 128), jnp.int32)
    for j in range(top_count):
        rank = rank + jnp.where(routes_ref[:, j:j + 1] == lane, priority_ref[:, j:j + 1] + 1, 0)
    rank = rank - 1
    before = (lax.broadcasted_iota(jnp.int32, (rows_here, rows_here), 1)
              < lax.broadcasted_iota(jnp.int32, (rows_here, rows_here), 0)).astype(F32).astype(BF16)
    base = jnp.zeros((1, 128), F32)
    slot = jnp.zeros((rows_here, 128), F32)
    for level in range(top_count):
        hot = (rank == level).astype(F32)
        slot = slot + hot * (base + mm(before, hot.astype(BF16)))
        base = base + jnp.sum(hot, axis=0, keepdims=True)
    named = rank >= 0
    slot = jnp.where(named & (slot < capacity), slot, -1.0)

    x_copies[2].wait_recv()
    x_copies[3].start()
    order = dp_order(w_copies)
    wo_order = dp_order(wo_copies)
    for key in order:
        w_copies[key].wait_recv()
        dp_start(w_copies, key)
    x_copies[1].wait_recv()
    x_copies[3].wait_recv()
    x_back = pltpu.make_async_copy(xs, x_out, own_sem.at[0])
    w_back = pltpu.make_async_copy(ws, w_out, own_sem.at[1])
    x_back.start()
    w_back.start()
    wx_copies = {}
    if exchange:
        for d in range(dp):
            for j in (1, 2, 3):
                owner = e if j < 3 else flip(e, 2)
                rows = pl.ds(pl.multiple_of((d * E + owner) * shard_rows, 16), shard_rows)
                wx_copies[d, j] = pltpu.make_async_remote_copy(wouts.at[rows], wouts.at[rows], wx_send.at[d, j], wx_recv.at[d, j],
                    device_id=device_at(q, r, flip(e, j if j < 3 else 1)), device_id_type=MESH)
    def out_step(step):
        if not exchange:
            return
        third = -(-len(wo_order) // 2)
        if step < 2:
            for key in wo_order[step * third:(step + 1) * third]:
                wo_copies[key].wait_recv()
                dp_start(wo_copies, key)
        if step == 1:
            for d in range(dp):
                wx_copies[d, 2].start()
            for d in range(dp):
                wx_copies[d, 1].start()
        if step == 3:
            for d in range(dp):
                wx_copies[d, 2].wait_recv()
                wx_copies[d, 3].start()

    small = ws[:, total - 128:].astype(F32).T
    gain_attn = small[experts:experts + 1, :]
    gain_moe = small[experts + 1:experts + 2, :]
    gains_ref[0:1, :] = gain_attn
    gains_ref[1:2, :] = gain_moe

    def send_block(b):
        rows = pl.ds(b * rows_here, rows_here)
        @pl.when(e == b)
        def _():
            os[b] = o_ref[rows, :]
        @pl.when(e != b)
        def _():
            pltpu.make_async_remote_copy(o_ref.at[rows], os.at[e], o_send.at[b], o_recv.at[e],
                device_id=device_at(q, r, b), device_id_type=MESH).start()
    sent = 0
    for i in range(length // block):
        rows = pl.ds(i * block, block)
        x = xs[rows, :].astype(F32)
        scale = lax.rsqrt(jnp.mean(x * x, axis=1, keepdims=True) + epsilon)
        h1 = (x * scale * gain_attn).astype(BF16)
        h1s[rows, :] = h1
        qkv = mm(h1, ws[:, :total - 128])
        qk = qkv[:, :q_cols + k_cols]
        turns = (q_cols + k_cols) // 128
        cosine = jnp.concatenate([cos_ref[rows, :]] * turns, axis=1)
        sine = jnp.concatenate([sin_ref[rows, :]] * turns, axis=1)
        qk = (qk * cosine + swap_halves(qk) * sine).astype(BF16)
        v = qkv[:, q_cols + k_cols:].astype(BF16)
        for h in range(heads):
            q_ref[h, rows, :] = qk[:, h * HD:(h + 1) * HD]
        vt = v.astype(F32).T.astype(BF16)
        for h in range(kv_heads):
            k_ref[h, rows, :] = qk[:, q_cols + h * HD:q_cols + (h + 1) * HD]
            v_ref[h, rows, :] = v[:, h * HD:(h + 1) * HD]
            vt_ref[h, :, rows] = vt[h * HD:(h + 1) * HD, :]
        keys = (i + 1) * block
        bias = bias_block(seg_ref[:, rows], keys, i * block)
        outs = []
        for h in range(heads):
            g = h // group
            st = mm(k_ref[g, pl.ds(0, keys), :], q_ref[h, rows, :] * BF16(HD ** -0.5), NT) + bias
            top = jnp.max(st, axis=0, keepdims=True)
            p = jnp.exp(st - top)
            sums = jnp.sum(p, axis=0, keepdims=True)
            outs.append(mm(vt_ref[g, :, pl.ds(0, keys)], p.astype(BF16)) / sums)
            lse_ref[pl.ds(h, 1), rows] = top + jnp.log(sums)
        o_ref[rows, :] = jnp.concatenate(outs, axis=0).T.astype(BF16)
        while sent < E and (sent + 1) * rows_here <= keys:
            send_block(sent)
            sent += 1
        out_step(i)
    h1_back = pltpu.make_async_copy(h1s, h1_ref, own_sem.at[2])
    h1_back.start()
    if exchange:
        for d in range(dp):
            wx_copies[d, 1].wait_recv()
            wx_copies[d, 3].wait_recv()
    else:
        fill = pltpu.make_async_copy(wout_ref, wouts, own_sem.at[3])
        fill.start()
        fill.wait()
    wout_back = pltpu.make_async_copy(wouts, wout_out, own_sem.at[3])
    wout_back.start()
    def o_descriptor(b):
        return pltpu.make_async_remote_copy(o_ref.at[pl.ds(0, rows_here)], os.at[b], o_send.at[b], o_recv.at[b],
            device_id=device_at(q, r, flip(e, 1)), device_id_type=MESH)
    middle = xs[token_rows(e), :].astype(F32)
    for b in range(E):
        @pl.when(e != b)
        def _():
            o_descriptor(b).wait_recv()
    for b in range(E):
        middle = middle + mm(os[b], wouts[b * q_cols:(b + 1) * q_cols, :])
    middle_ref[...] = middle
    scale = lax.rsqrt(jnp.mean(middle * middle, axis=1, keepdims=True) + epsilon)
    h2 = (middle * scale * gain_moe).astype(BF16)
    h2_ref[...] = h2
    logits = jnp.where(named, mm(h2, ws[:, total - 128:]), masked_score)
    powers = jnp.where(named, jnp.exp(logits - jnp.max(logits, axis=1, keepdims=True)), 0.0)
    probs = powers / jnp.sum(powers, axis=1, keepdims=True)
    probs_ref[...] = probs
    slot_rows = slot.T
    prob_rows = probs.T
    local = experts // E
    table_ref[...] = jnp.zeros_like(table_ref)
    for dest_r in range(QUAD):
        for dest_e in range(E):
            for at, expert in enumerate(device_experts(local, dest_r)):
                row = dest_e * local + expert
                table_ref[dest_r * E + dest_e, at:at + 1, :] = slot_rows[row:row + 1, :]
                table_ref[dest_r * E + dest_e, 4 + at:5 + at, :] = prob_rows[row:row + 1, :]
    for b in range(E):
        @pl.when(e != b)
        def _():
            o_descriptor(b).wait_send()
    for copy in p_copies + list(x_copies.values()) + list(w_copies.values()) + list(wo_copies.values()) + list(wx_copies.values()):
        copy.wait_send()
    for copy in (x_back, w_back, h1_back, wout_back):
        copy.wait()

def start_call(tokens, pieces, w_out, routes, priority, segments, cosine, sine, experts, capacity, q_cols, k_cols, exchange):
    E, quads = lax.axis_size("expert"), lax.axis_size("q")
    dp = quads * QUAD
    rows_here, width = tokens.shape
    length = rows_here * E
    shard_rows = width // (dp * E)
    total = pieces.shape[-1]
    V, A = pl.BlockSpec(memory_space=pltpu.VMEM), pl.BlockSpec(memory_space=pl.ANY)
    heads, kv_heads = q_cols // HD, k_cols // HD
    S = jax.ShapeDtypeStruct
    sem = pltpu.SemaphoreType.DMA
    dims = (experts, capacity, routes.shape[1], q_cols, k_cols, rows_here, shard_rows)
    kernel = functools.partial(start_kernel, dims, exchange)
    return pl.pallas_call(kernel,
        out_shape=(S((length, width), BF16), S((width, total), BF16), S((width, width), BF16), S((length, width), BF16),
            S((heads, length, HD), BF16), S((kv_heads, length, HD), BF16), S((kv_heads, length, HD), BF16),
            S((length, q_cols), BF16), S((-(-heads // 8) * 8, length), F32), S((rows_here, width), F32), S((rows_here, width), BF16),
            S((QUAD * E, 8, rows_here), F32), S((rows_here, 128), F32), S((8, width), F32)),
        in_specs=[V, V, V if exchange else A, V, V, V, V, V], out_specs=(A, A, A, A) + (V,) * 10,
        scratch_shapes=[pltpu.VMEM((length, width), BF16), pltpu.VMEM((width, total), BF16), pltpu.VMEM((width, width), BF16),
            pltpu.VMEM((kv_heads, HD, length), BF16), pltpu.VMEM((length, width), BF16), pltpu.VMEM((E, rows_here, q_cols), BF16), sem((4,)),
            sem((4,)), sem((4,)), sem((4,)), sem((4,)), sem((3, quads, QUAD)), sem((3, quads, QUAD)), sem((E,)), sem((E,)),
            sem((3, quads, QUAD)), sem((3, quads, QUAD)), sem((dp, 4)), sem((dp, 4))],
        compiler_params=pltpu.CompilerParams(vmem_limit_bytes=58 << 20, collective_id=4, has_side_effects=True),
        cost_estimate=CHEAP,
        name="start")(tokens, pieces, w_out, routes, priority, segments.reshape(1, -1), cosine, sine)


DENSE_ORDERS = ((1, 2, "q"), (2, 1, "q"))

def back_kernel(dims, exchange, *refs):
    (experts, q_cols, k_cols, slots) = dims
    (dr_ref, dg_ref, probs_ref, h2_ref, middle_ref, cot_ref, gains_ref, tokens_ref, wout_ref, q_ref, k_ref, v_ref, lse_ref,
     cos_ref, sin_ref, seg_ref, h1_ref, xall_ref, wall_ref, mixed_ref) = refs[:20]
    refs = refs[20:]
    if exchange:
        (tokens_out, gq_ref, gk_ref, gv_ref, small_ref, gout_ref) = refs[:6]
        refs = refs[6:]
    else:
        (tokens_out, dense_ref, gout_ref) = refs[:3]
        refs = refs[3:]
    (h1s, xs, ws, mixeds, load_sem, dgt, dats, dos, do_out, kt_ref, dk_ref, dv_ref, dqkv, dx1s, small, part, core_in, y_in,
     g1, g2, r1, r2, f1,
     do_send, do_recv, dat_send, dat_recv, part_send, part_recv, g1_send, g1_recv, g2_send, g2_recv, f_send, f_recv) = refs
    E, quads = lax.axis_size("expert"), lax.axis_size("q")
    q, r, e = lax.axis_index("q"), member_r(), lax.axis_index("expert")
    dp = quads * QUAD
    rows_here, width = dr_ref.shape
    length = rows_here * E
    heads, kv_heads = q_cols // HD, k_cols // HD
    group = heads // kv_heads
    total = ws.shape[1]
    qkv_cols = total - 128
    factor = HD ** -0.5
    block = 256
    loads = [pltpu.make_async_copy(a, b, load_sem.at[i])
             for i, (a, b) in enumerate(((wall_ref, ws), (mixed_ref, mixeds), (h1_ref, h1s), (xall_ref, xs.at[pl.ds(0, length)])))]
    load_out = pltpu.make_async_copy(wout_ref, xs, load_sem.at[4])
    load_out.start()
    for load in loads[:3]:
        load.start()
    barrier = pltpu.get_barrier_semaphore()
    friends = [device_at(q, r, flip(e, j)) for j in (1, 2, 3)] + [device_at(q, flip(r, m), e) for m in (1, 2)]
    friends += [device_at((q + k) % quads, r, e) for k in range(1, quads)]
    for friend in friends:
        pl.semaphore_signal(barrier, inc=1, device_id=friend, device_id_type=MESH)
    pl.semaphore_wait(barrier, len(friends))

    dgt[...] = jnp.zeros_like(dgt)
    local = experts // E
    whole = local // QUAD
    for mask in range(QUAD * E):
        from_r, from_e = flip(r, mask >> 2), flip(e, mask & 3)
        for k in range(slots):
            if k < whole:
                row = from_e * local + from_r * whole + k
            else:
                row = from_e * local + QUAD * whole + from_r // (QUAD // (local - QUAD * whole))
            dgt[pl.ds(row, 1), :] += dg_ref[mask, k:k + 1, :]
    dg = dgt[...].T
    probs = probs_ref[...]
    dz = (probs * (dg - jnp.sum(probs * dg, axis=1, keepdims=True))).astype(BF16)
    loads[0].wait()
    dh2 = dr_ref[...] + mm(dz, ws[:, qkv_cols:], NT)
    gain_attn, gain_moe = gains_ref[0:1, :], gains_ref[1:2, :]
    middle = middle_ref[...]
    scale = lax.rsqrt(jnp.mean(middle * middle, axis=1, keepdims=True) + epsilon)
    unit = middle * scale
    grad_moe_gain = jnp.sum(dh2 * unit, axis=0, keepdims=True)
    grad_unit = dh2 * gain_moe
    dx1 = cot_ref[...].astype(F32) + scale * (grad_unit - unit * jnp.mean(grad_unit * unit, axis=1, keepdims=True))
    dx1s[...] = dx1
    dat = dx1.astype(BF16)

    def token_rows(who):
        return pl.ds(pl.multiple_of(who * rows_here, 16), rows_here)
    load_out.wait()
    for b in range(E):
        do = mm(dat, xs[b * q_cols:(b + 1) * q_cols, :], NT).astype(BF16)
        do_out[b] = do
        @pl.when(e == b)
        def _():
            dos[token_rows(e), :] = do_out[b]
        @pl.when(e != b)
        def _():
            pltpu.make_async_remote_copy(do_out.at[b], dos.at[token_rows(e)], do_send.at[b], do_recv.at[e],
                device_id=device_at(q, r, b), device_id_type=MESH).start()
    loads[3].start()
    def do_descriptor(b):
        return pltpu.make_async_remote_copy(do_out.at[b], dos.at[pl.ds(b * rows_here, rows_here)], do_send.at[b], do_recv.at[b],
            device_id=device_at(q, r, flip(e, 1)), device_id_type=MESH)
    dats[token_rows(e), :] = dat
    dat_copies = {}
    for j in (1, 2, 3):
        rows = token_rows(e if j < 3 else flip(e, 2))
        dat_copies[j] = pltpu.make_async_remote_copy(dats.at[rows], dats.at[rows], dat_send.at[j], dat_recv.at[j],
            device_id=device_at(q, r, flip(e, j if j < 3 else 1)), device_id_type=MESH)
    dat_copies[2].start()
    dat_copies[1].start()
    small[...] = mm(h2_ref[...], dz, TN)
    dk_ref[...] = jnp.zeros_like(dk_ref)
    dv_ref[...] = jnp.zeros_like(dv_ref)
    for g in range(kv_heads):
        kt_ref[g] = k_ref[g].astype(F32).T.astype(BF16)

    seen = 0
    for i in range(length // block):
        rows = pl.ds(i * block, block)
        keys = (i + 1) * block
        while seen * rows_here < keys:
            @pl.when(e != seen)
            def _():
                do_descriptor(seen).wait_recv()
            seen += 1
        span = pl.ds(0, keys)
        bias = bias_block(seg_ref[:, rows], keys, i * block)
        dqs = []
        for h in range(heads):
            g = h // group
            qh = q_ref[h, rows, :]
            do = dos[rows, h * HD:(h + 1) * HD]
            st = mm(k_ref[g, span, :], qh * BF16(factor), NT) + bias
            p = jnp.exp(st - lse_ref[pl.ds(h, 1), rows])
            dpt = mm(v_ref[g, span, :], do, NT)
            inner = jnp.sum(p * dpt, axis=0, keepdims=True)
            ds = (p * (dpt - inner)).astype(BF16)
            dv_ref[g, span, :] += mm(p.astype(BF16), do)
            dk_ref[g, span, :] += mm(ds, qh)
            dqs.append(mm(kt_ref[g, :, span], ds))
        dq = jnp.concatenate(dqs, axis=0).T * factor
        cosine = jnp.concatenate([cos_ref[rows, :]] * (q_cols // 128), axis=1)
        sine = jnp.concatenate([sin_ref[rows, :]] * (q_cols // 128), axis=1)
        dqkv[rows, :q_cols] = (dq * cosine - swap_halves(dq) * sine).astype(BF16)
        if i == 1:
            dat_copies[2].wait_recv()
            dat_copies[3].start()
    dk = jnp.concatenate([dk_ref[g] for g in range(kv_heads)], axis=1) * factor
    cosine = jnp.concatenate([cos_ref[...]] * (k_cols // 128), axis=1)
    sine = jnp.concatenate([sin_ref[...]] * (k_cols // 128), axis=1)
    dqkv[:, q_cols:q_cols + k_cols] = (dk * cosine - swap_halves(dk) * sine).astype(BF16)
    dqkv[:, q_cols + k_cols:] = jnp.concatenate([dv_ref[g] for g in range(kv_heads)], axis=1).astype(BF16)

    grad_attn_gain = jnp.zeros((1, width), F32)
    loads[3].wait()
    part_copies = {}
    own = None
    for j in (3, 1, 2, 0):
        rows = token_rows(flip(e, j))
        dh1 = mm(dqkv[rows, :], ws[:, :qkv_cols], NT)
        x = xs[rows, :].astype(F32)
        scale = lax.rsqrt(jnp.mean(x * x, axis=1, keepdims=True) + epsilon)
        grad_attn_gain = grad_attn_gain + jnp.sum(dh1 * (x * scale), axis=0, keepdims=True)
        if j & 1:
            part[j - 1] = dh1.astype(BF16)
            part_copies[j] = pltpu.make_async_remote_copy(part.at[j - 1], core_in.at[j // 2], part_send.at[j], part_recv.at[j],
                device_id=device_at(q, r, flip(e, 1)), device_id_type=MESH)
            part_copies[j].start()
        elif j == 2:
            part_copies[3].wait_recv()
            part[1] = (dh1 + core_in[1].astype(F32)).astype(BF16)
            part_copies[2] = pltpu.make_async_remote_copy(part.at[1], y_in, part_send.at[2], part_recv.at[2],
                device_id=device_at(q, r, flip(e, 2)), device_id_type=MESH)
            part_copies[2].start()
        else:
            own = dh1

    rows_out = lax.broadcasted_iota(jnp.int32, (128, width), 0)
    gains = jnp.where(rows_out == experts, grad_attn_gain, 0.0) + jnp.where(rows_out == experts + 1, grad_moe_gain, 0.0)
    small_all = small[...] + gains.T
    loads[2].wait()
    share = width // dp
    grad = mm(h1s[...], dqkv[...], TN).astype(BF16)
    for d in range(dp):
        g1[d, :, :qkv_cols] = grad[d * share:(d + 1) * share]
        g1[d, :, qkv_cols:] = small_all[d * share:(d + 1) * share].astype(BF16)
    dat_copies[1].wait_recv()
    dat_copies[3].wait_recv()
    loads[1].wait()
    grad = mm(mixeds[...], dats[...], TN)
    out_share = q_cols // dp
    if exchange:
        for d in range(dp):
            g2[d] = grad[d * out_share:(d + 1) * out_share].astype(BF16)
    else:
        gout_ref[...] = grad.astype(BF16)
    arrays = [(g1, r1, g1_send, g1_recv)] + ([(g2, r2, g2_send, g2_recv)] if exchange else [])
    keys = [(k, m) for k in range(quads) for m in range(QUAD)]
    def at(k, m):
        return place_at((q + k) % quads, flip(r, m))
    def has(key, dim):
        return key[0] if dim == "q" else key[1] & dim
    def first(p, key):
        return [n for n, dim in enumerate(DENSE_ORDERS[p]) if has(key, dim)][0]
    def sources(p, key, upto):
        found = []
        for dim in DENSE_ORDERS[p][:upto]:
            found += [(k, key[1]) for k in range(1, quads)] if dim == "q" else [(key[0], key[1] | dim)]
        return found
    copies = {}
    for n, (grad_ref, landing, send, recv) in enumerate(arrays):
        half = grad_ref.shape[2] // 2
        for p in range(2):
            for k, m in keys[1:]:
                dim = DENSE_ORDERS[p][first(p, (k, m))]
                device = device_at((q + k) % quads, r, e) if dim == "q" else device_at(q, flip(r, dim), e)
                copies[n, p, k, m] = pltpu.make_async_remote_copy(grad_ref.at[at(k, m), :, pl.ds(p * half, half)],
                    landing.at[p, k, m], send.at[p, k, m], recv.at[p, k, m], device_id=device, device_id_type=MESH)
    numbers = range(len(arrays))
    def reduced(n, p, key):
        grad_ref, landing = arrays[n][:2]
        half = grad_ref.shape[2] // 2
        sum_now = grad_ref[at(*key), :, p * half:(p + 1) * half].astype(F32)
        for k, m in sources(p, key, 3 if key == (0, 0) else first(p, key)):
            copies[n, p, k, m].wait_recv()
            sum_now = sum_now + landing[p, k, m].astype(F32)
        return sum_now
    def send_on(level):
        for p in range(2):
            now = [key for key in keys[1:] if first(p, key) == level]
            now.sort(key=lambda key: -sum(1 for dim in DENSE_ORDERS[p] if has(key, dim)))
            for k, m in now:
                for n in numbers:
                    if level:
                        half = arrays[n][0].shape[2] // 2
                        arrays[n][0][at(k, m), :, p * half:(p + 1) * half] = reduced(n, p, (k, m)).astype(BF16)
                    copies[n, p, k, m].start()
    send_on(0)
    send_on(1)
    part_copies[1].wait_recv()
    part_copies[2].wait_recv()
    dh1 = own + core_in[0].astype(F32) + y_in[...].astype(F32)
    x = tokens_ref[...].astype(F32)
    scale = lax.rsqrt(jnp.mean(x * x, axis=1, keepdims=True) + epsilon)
    unit = x * scale
    grad_unit = dh1 * gain_attn
    tokens_out[...] = dx1s[...] + scale * (grad_unit - unit * jnp.mean(grad_unit * unit, axis=1, keepdims=True))
    send_on(2)
    final = {(n, p): reduced(n, p, (0, 0)) for n in numbers for p in range(2)}
    dense = jnp.concatenate([final[0, 0], final[0, 1]], axis=1)
    if exchange:
        gout_ref[...] = jnp.concatenate([final[1, 0], final[1, 1]], axis=1).astype(BF16)
        g1[at(0, 0)] = dense.astype(BF16)
        shard = share // E
        f_copies = []
        for j in (1, 2, 3):
            rows = pl.ds(pl.multiple_of(flip(e, j) * shard, 16), shard)
            copy = pltpu.make_async_remote_copy(g1.at[at(0, 0), rows], f1.at[e], f_send.at[j], f_recv.at[j],
                device_id=device_at(q, r, flip(e, j)), device_id_type=MESH)
            copy.start()
            f_copies.append(copy)
        f1[e] = g1[at(0, 0), pl.ds(pl.multiple_of(e * shard, 16), shard), :]
        for copy in f_copies:
            copy.wait_recv()
        tail = jnp.zeros((shard, 128), F32)
        for b in range(E):
            piece = f1[b].astype(F32)
            gq_ref[:, b * q_cols:(b + 1) * q_cols] = piece[:, :q_cols]
            gk_ref[:, b * k_cols:(b + 1) * k_cols] = piece[:, q_cols:q_cols + k_cols]
            gv_ref[:, b * k_cols:(b + 1) * k_cols] = piece[:, q_cols + k_cols:qkv_cols]
            tail = tail + piece[:, qkv_cols:]
        small_ref[...] = tail
        for copy in f_copies:
            copy.wait_send()
    else:
        dense_ref[...] = dense.astype(BF16)
    for b in range(E):
        @pl.when(e != b)
        def _():
            do_descriptor(b).wait_send()
    for copy in list(dat_copies.values()) + list(part_copies.values()) + list(copies.values()):
        copy.wait_send()

def back_call(dr_sum, dg_back, probs, h2, middle, cotangent, gains, tokens, out_full, query, key, value, log_total,
              cosine, sine, segments, h1_all, x_all, w_all, mixed, experts, q_cols, k_cols, slots, exchange):
    E, quads = lax.axis_size("expert"), lax.axis_size("q")
    dp = quads * QUAD
    rows_here, width = tokens.shape
    length = rows_here * E
    total = w_all.shape[1]
    heads, kv_heads = q_cols // HD, k_cols // HD
    share, out_share = width // dp, q_cols // dp
    shard = share // E
    V, A = pl.BlockSpec(memory_space=pltpu.VMEM), pl.BlockSpec(memory_space=pl.ANY)
    S, M, sem = jax.ShapeDtypeStruct, pltpu.VMEM, pltpu.SemaphoreType.DMA
    if exchange:
        outs = (S((rows_here, width), F32), S((shard, q_cols * E), F32), S((shard, k_cols * E), F32), S((shard, k_cols * E), F32),
            S((shard, 128), F32), S((out_share, width), BF16))
        second = [M((dp, out_share, width), BF16), M((2, quads, QUAD, out_share, width // 2), BF16)]
    else:
        outs = (S((rows_here, width), F32), S((share, total), BF16), S((q_cols, width), BF16))
        second = [M((16, 128), BF16)] * 2
    scratch = [M((length, width), BF16), M((width, width), BF16), M((width, total), BF16), M((length, q_cols), BF16), sem((5,)),
        M((128, rows_here), F32), M((length, width), BF16), M((length, q_cols), BF16), M((E, rows_here, q_cols), BF16),
        M((kv_heads, HD, length), BF16), M((kv_heads, length, HD), F32), M((kv_heads, length, HD), F32), M((length, total - 128), BF16),
        M((rows_here, width), F32), M((width, 128), F32), M((3, rows_here, width), BF16), M((2, rows_here, width), BF16),
        M((rows_here, width), BF16),
        M((dp, share, total), BF16), second[0],
        M((2, quads, QUAD, share, total // 2), BF16), second[1], M((E, shard, total), BF16)]
    scratch += [sem((4,))] * 6 + [sem((2, quads, 4))] * 4 + [sem((4,))] * 2
    return pl.pallas_call(functools.partial(back_kernel, (experts, q_cols, k_cols, slots), exchange),
        out_shape=outs, in_specs=[V] * 8 + [A] + [V] * 7 + [A] * 4, out_specs=(V,) * len(outs), scratch_shapes=scratch,
        compiler_params=pltpu.CompilerParams(vmem_limit_bytes=60 << 20, collective_id=5, has_side_effects=True),
        cost_estimate=CHEAP,
        name="backward")(dr_sum, dg_back, probs, h2, middle, cotangent, gains, tokens, out_full, query, key, value, log_total,
            cosine, sine, segments.reshape(1, -1), h1_all, x_all, w_all, mixed)


ALL = ("q", "rh", "rl", "expert")
DP = ("q", "rh", "rl")
GROUP = ("rh", "rl", "expert")


def shards(
    tokens, w_query, w_key, w_value, w_out, w_router, gain_attn, gain_moe,
    w_gate, w_up, w_down, segments, routes, priority, cotangent,
):
    rows_here, width = tokens.shape
    E = lax.axis_size("expert")
    R = QUAD
    Q = lax.axis_size("q")
    e = lax.axis_index("expert")
    r = member_r()
    shard_rows = w_query.shape[0]
    local = w_gate.shape[0]
    experts = local * E
    ffn = w_gate.shape[2]
    capacity = rows_here * routes.shape[1] // experts
    length = rows_here * E
    sources = R * E
    q_cols = w_query.shape[1] // E
    k_cols = w_key.shape[1] // E
    exchange = shard_rows % 16 == 0
    small = jnp.concatenate([w_router, gain_attn[:, None], gain_moe[:, None]], axis=1)
    small = jnp.pad(small, ((0, 0), (0, 128 - small.shape[1])))
    pieces = jnp.concatenate(
        [w.reshape(shard_rows, E, -1) for w in (w_query, w_key, w_value)]
        + [jnp.broadcast_to(small[:, None], (shard_rows, E, 128))],
        axis=2,
    )
    pieces = jnp.transpose(pieces, (1, 0, 2))
    out_part = w_out
    if not exchange:
        pieces = lax.all_to_all(pieces, "expert", split_axis=0, concat_axis=0, tiled=True)
        pieces = pieces.reshape(E * shard_rows, -1)
        out_part = lax.all_gather(w_out, ALL, axis=0, tiled=True)
    dm_all = lax.all_gather(cotangent, GROUP, axis=0, tiled=True).reshape(
        sources, rows_here, width
    )
    cosine, sine = rope_tables(jnp.arange(length, dtype=jnp.int32), HD)
    cosine = jnp.tile(cosine, (1, 4))
    sine = jnp.tile(jnp.concatenate([-sine, sine], axis=1), (1, 2))
    (x_all, w_all, out_full, h1_all, query, key, value, mixed, log_total, middle, h2, table, probs, gains) = start_call(
        tokens, pieces, out_part, routes, priority, segments, cosine, sine, experts, capacity, q_cols, k_cols, exchange
    )
    qkv_cols = q_cols + 2 * k_cols
    dp = Q * R
    whole = local // R
    rest = local - whole * R
    ways = R // rest if rest else 1
    slots = whole + (1 if rest else 0)

    rows, dm_rows, weight, tables = gather_rows(h2, table, dm_all, slots, capacity, 1)
    def scalars(places):
        return jnp.stack(places + [r % ways]).astype(jnp.int32)

    banks = (w_gate, w_up, w_down)
    done = []
    if rest:
        part = expert_call(rows, dm_rows, weight, whole, 1, *banks, scalars([R * whole + r // ways]), dp, ways)
        part_moved = lax.all_to_all(part[3], DP, split_axis=0, concat_axis=0, tiled=True)
    done.append(expert_call(rows, dm_rows, weight, 0, whole, *banks, scalars([r * whole + s for s in range(whole)]), dp, 1))
    moved = [lax.all_to_all(done[0][3], DP, split_axis=0, concat_axis=0, tiled=True)]
    if rest:
        done.append(part)
        moved.append(part_moved)
    y_rows, dr_rows, dg_rows = ([d[n] for d in done] for n in range(3))
    dr_sum, dg_back = combine_rows(dr_rows, tables, dg_rows, capacity, 2)
    out = back_call(
        dr_sum, dg_back, probs, h2, middle, cotangent, gains, tokens, out_full, query, key, value, log_total,
        cosine, sine, segments, h1_all, x_all, w_all, mixed, experts, q_cols, k_cols, slots, exchange
    )
    if exchange:
        grad_tokens, grad_query, grad_key, grad_value, small_own, out_sum = out
    else:
        grad_tokens, qkv_sum, out_sum = out
        qkv_own = lax.all_to_all(
            qkv_sum.reshape(E, shard_rows, -1), "expert", split_axis=0, concat_axis=0, tiled=True
        )
        qkv_own = jnp.transpose(qkv_own, (1, 0, 2)).astype(F32)
        small_own = jnp.sum(qkv_own[:, :, qkv_cols:], axis=1)
        grad_query = qkv_own[:, :, :q_cols].reshape(shard_rows, -1)
        grad_key = qkv_own[:, :, q_cols : q_cols + k_cols].reshape(shard_rows, -1)
        grad_value = qkv_own[:, :, q_cols + k_cols : qkv_cols].reshape(shard_rows, -1)
        out_sum = lax.psum_scatter(out_sum, DP, scatter_dimension=0, tiled=True)
    perm = [(p * E + x, dp * x + p) for p in range(dp) for x in range(E)]
    out_own = lax.ppermute(out_sum, ALL, perm).astype(F32)
    late = lax.optimization_barrier((tuple(y_rows), grad_tokens))
    y_sum = combine_rows(list(late[0]), tables, None, capacity, 3)
    outputs = (middle + y_sum).astype(BF16)
    moved, _ = lax.optimization_barrier((moved, outputs))
    gate_share, up_share, down_share = place_call(moved, local, ffn, width)
    return (
        outputs,
        grad_tokens,
        grad_query,
        grad_key,
        grad_value,
        out_own,
        small_own[:, :experts],
        small_own[:, experts],
        small_own[:, experts + 1],
        gate_share,
        up_share,
        down_share,
    )


def solution(mesh):
    dp, ex = mesh.devices.shape
    fine = Mesh(mesh.devices.reshape(dp // QUAD, 2, 2, ex), ALL)
    row, flat = P(ALL, None), P(ALL)
    bank = P("expert", None, None)
    spread = P("expert", DP, None)
    return jax.shard_map(
        shards,
        mesh=fine,
        in_specs=(row,) * 6 + (flat,) * 2 + (bank,) * 3 + (P(DP),) + (row,) * 3,
        out_specs=(row,) * 7 + (flat,) * 2 + (spread,) * 3,
        check_vma=False,
    )
```

time: 923 us -> 751 us (0.81); the launches traced: 907 us -> 744 us
  Pallas kernels: 366 us -> 683 us
  waiting for transfers between devices: 281 us -> 13.6 us
  blocking collectives: 94.9 us -> 0 us
  matrix products: 38.3 us -> 0 us
  other arithmetic: 44.1 us -> 6.83 us
  local copies, waits for them, and re-layouts: 34.5 us -> 13.7 us
  starting transfers between devices: 32.8 us -> 12.3 us
    pallas_call x7, Pallas kernels: 293 us -> 607 us  [the longest x2 267 us: combine_rows(): pl.pallas_call(functools.partial(combine_kernel, banks, slots, capacity,...]
    all_to_all x7 -> x2, waiting for transfers between devices: 157 us -> 12.9 us  [the longest x1 12.9 us: shards(): lax.all_to_all(part[3], DP, split_axis=0, concat_axis=0, tiled=True)]
    all_gather x1, waiting for transfers between devices: 70.3 us -> 0.01 us  [shards(): lax.all_gather(cotangent, GROUP, axis=0, tiled=True)]
    all_to_all x3 -> x0, blocking collectives: 51.9 us -> none  [the longest x1 25 us: shards(): lax.all_to_all(a, DP, split_axis=0, concat_axis=0, tiled=True)]
    all_gather x4 -> x0, waiting for transfers between devices: 51.2 us -> none  [the longest x1 28.5 us: shards(): x_all = lax.all_gather(tokens, 'expert', axis=0, tiled=True)]
    all_gather x1 -> x0, blocking collectives: 43 us -> none  [shards(): small = lax.all_gather(small, ALL, axis=0, tiled=True)]
    dot_general x13 -> x0, matrix products: 38.3 us -> none  [the longest x10 33.1 us: dot32(): return jnp.einsum(spec, a, b, preferred_element_type=F32)]
    reduce_sum x15 -> x0, other arithmetic: 19.4 us -> none  [the longest x2 7.42 us: shards(): jnp.sum(gu.reshape(Q, R, 2, share_d, ffn).astype(F32), axis=0)]
  transfers between devices with their start and end apart: 16 -> 4, of which waited for: 8 -> 1; matrix products, arithmetic and copies ran while one was open for 10% -> 2% of each run, Pallas kernels for 18% -> 78%
where the time goes in v3:
time: 751 us; the launch traced here: 744 us
  Pallas kernels  683 us (91%)
  between operations  14.4 us (2%)
  local copies, waits for them, and re-layouts  13.7 us (2%)
  waiting for transfers between devices  13.6 us (2%)
  starting transfers between devices  12.3 us (2%)
    pallas_call x2, Pallas kernels, combine_rows(): pl.pallas_call(functools.partial(combine_kernel, banks, slots, capacity,...  267 us
    pallas_call x1, Pallas kernels, start_call(): pl.pallas_call(kernel, out_shape=(S((length, width), BF16), S((width, tot...  149 us
    pallas_call x1, Pallas kernels, back_call(): pl.pallas_call(functools.partial(back_kernel, (experts, q_cols, k_cols, s...  124 us
    pallas_call x1, Pallas kernels, gather_rows(): pl.pallas_call(functools.partial(gather_kernel, slots, capacity), out_sha...  76.3 us
    pallas_call x2, Pallas kernels, expert_call(): pl.pallas_call(functools.partial(expert_kernel, chunks, dp, ways), grid_s...  56.7 us
  transfers between devices with their start and end apart: 4, of which 1 were waited for; matrix products, arithmetic and copies ran while one was open for 2% of the time, Pallas kernels for 78%

profile of v3, /device:TPU:0, one launch (start us, length us, event | category | flops | bytes accessed | tf_op | source)
XLA Modules:
  0.0 744.4 jit_solution(15263445070378730863)
XLA Ops:
  7.2 0.0 copy-start
  7.2 0.0 copy-start.9
  7.2 0.0 all-gather.2.cloned.1.call-start
  7.3 0.7 all-gather.2.cloned.1.call-update
  8.0 1.3 reshape.93.refs_5_.refs_15_
  9.3 0.7 pad_maximum_fusion.1
  10.0 0.1 copy.42
  10.1 0.9 copy.49
  11.0 1.5 copy.35.refs_3_
  12.5 1.5 copy.36.refs_4_
  14.1 0.7 fusion
  14.8 1.1 copy.38.refs_7_.refs_14_
  15.9 1.1 copy.37.refs_6_.refs_13_
  17.0 0.0 copy-done
  17.0 0.0 copy-done.9
  17.1 0.7 maximum_bitcast_fusion.refs_1_
  17.8 149.0 %start.1 = (bf16[1280,1536]{1,0:T(8,128)(2,1)}, bf16[1536,768]{1,0:T(8,128)(2,1)}, bf16[1536,1536]{1,0:T(8,128)(2,1)}, bf16[1280,1536]{1,0:T(8,128)(2,1)}, bf16[...) custom-call(bf16[320,1536]{1,0:T(8,128)(2,1)} %refs_7_.1, ...), custom_call_target="tpu_custom_call" | custom-call | flops 1048576 | bytes 65536 | tf_op jit(solution)/shard_map/start/pallas_call | solution.py:763
  166.9 0.6 pad_add_fusion.1.s_ref
  167.5 76.3 %gather_rows.1 = (bf16[3,1024,1536]{2,1,0:T(8,128)(2,1)}, bf16[3,1024,1536]{2,1,0:T(8,128)(2,1)}, f32[3,1024,1]{2,1,0:T(8,128)}, f32[16,8,320]{2,1,0:T(8,128)}) custom-call(bf16[320,1536]{1,0:T(8,128)(2,1)} %get-tuple-element.54.h2_ref.refs_3_, f32[16,8,320]{2,1,0:T(8,128)} %get-tuple-element.55.table_ref, bf16[16,320,1536]{2,1,0:T(8,128)(2,1)} %bitcast.28), custom_call_target="tpu_custom_call" | custom-call | flops 1048576 | bytes 65536 | tf_op jit(solution)/shard_map/gather_rows/pallas_call | solution.py:223
  243.7 16.8 %expert_part.1 = (bf16[1,1024,1536]{2,1,0:T(8,128)(2,1)}, bf16[1,1024,1536]{2,1,0:T(8,128)(2,1)}, f32[1,1024,1]{2,1,0:T(8,128)}, bf16[8,1,576,256]{3,2,1,0:T(8,128)(2,1)}) custom-call(s32[2]{0:T(128)} %pad_add_fusion.1.s_ref, bf16[3,1024,1536]{2,1,0:T(8,128)(2,1)} %get-tuple-element.56.x_ref, bf16[3,1024,1536]{2,1,0:T(8,128)(2,1)} %get-tuple-element.57.dm_ref, ...), custom_call_target="tpu_custom_call" | custom-call | flops 1048576 | bytes 65536 | tf_op jit(solution)/shard_map/expert_part/pallas_call | solution.py:297
  260.5 4.9 all-to-all-start.1
  265.5 0.6 pad_add_fusion.s_ref
  266.0 40.0 %experts.1 = (bf16[2,1024,1536]{2,1,0:T(8,128)(2,1)}, bf16[2,1024,1536]{2,1,0:T(8,128)(2,1)}, f32[2,1024,1]{2,1,0:T(8,128)}, bf16[8,2,576,512]{3,2,1,0:T(8,128)(2,1)}) custom-call(s32[3]{0:T(128)} %pad_add_fusion.s_ref, bf16[3,1024,1536]{2,1,0:T(8,128)(2,1)} %get-tuple-element.56.x_ref, bf16[3,1024,1536]{2,1,0:T(8,128)(2,1)} %get-tuple-element.57.dm_ref, ...), custom_call_target="tpu_custom_call" | custom-call | flops 1048576 | bytes 65536 | tf_op jit(solution)/shard_map/experts/pallas_call | solution.py:297
  306.0 12.9 %all-to-all-done.1 = bf16[8,1,576,256]{3,2,1,0:T(8,128)(2,1)S(1)} async-done(((bf16[8,1,576,256]{3,2,1,0:T(8,128)(2,1)}), bf16[8,1,576,256]{3,2,1,0:T(8,128)(2,1)S(1)}, u32[]{:S(2)}, u32[]{:S(2)}) %all-to-all-start.1) | async-done | bytes 2359328 | tf_op jit(solution)/shard_map/all_to_all | solution.py:1139
  319.0 1.4 copy-done.2
  320.4 5.5 all-to-all-start
  325.8 176.6 %combine_with_dg.1 = (f32[320,1536]{1,0:T(8,128)}, f32[16,8,320]{2,1,0:T(8,128)}) custom-call(bf16[2,1024,1536]{2,1,0:T(8,128)(2,1)} %get-tuple-element.61.refs_0_, bf16[1,1024,1536]{2,1,0:T(8,128)(2,1)} %get-tuple-element.62.refs_1_, f32[16,8,320]{2,1,0:T(8,128)} %get-tuple-element.63.refs_2_, f32[2,1024,1]{2,1,0:T(8,128)} %get-tuple-element.64.refs_3_, ...), custom_call_target="tpu_custom_call" | custom-call | flops 1048576 | bytes 65536 | tf_op jit(solution)/shard_map/combine_with_dg/pallas_call | solution.py:473
  502.5 124.1 %backward.1 = (f32[320,1536]{1,0:T(8,128)}, f32[48,1536]{1,0:T(8,128)}, f32[48,512]{1,0:T(8,128)}, f32[48,512]{1,0:T(8,128)}, f32[48,128]{1,0:T(8,128)}, /*index=5*/bf16[48,1536]{1,0:T(8,128)(2,1)}) custom-call(f32[320,1536]{1,0:T(8,128)} %get-tuple-element.66.refs_0_, f32[16,8,320]{2,1,0:T(8,128)} %get-tuple-element.67.refs_1_, ...), custom_call_target="tpu_custom_call" | custom-call | flops 1048576 | bytes 65536 | tf_op jit(solution)/shard_map/backward/pallas_call | solution.py:1069
  626.6 0.0 copy-start.3
  626.6 1.8 collective-permute-start
  628.5 90.3 %combine_rows.1 = f32[320,1536]{1,0:T(8,128)} custom-call(bf16[2,1024,1536]{2,1,0:T(8,128)(2,1)} %get-tuple-element.80.refs_0_, bf16[1,1024,1536]{2,1,0:T(8,128)(2,1)} %get-tuple-element.81.refs_1_, f32[16,8,320]{2,1,0:T(8,128)} %get-tuple-element.63.refs_2_), custom_call_target="tpu_custom_call" | custom-call | flops 1048576 | bytes 65536 | tf_op jit(solution)/shard_map/combine_rows/pallas_call | solution.py:473
  718.8 0.0 copy-done.3
  718.8 0.0 copy-start.6
  718.8 2.7 add_convert_fusion
  721.6 0.0 copy-done.6
  721.6 0.7 copy.41
  722.2 0.7 slice_reduce_fusion
  722.9 0.0 collective-permute-done
  722.9 0.7 convert_element_type.23
  723.7 0.0 all-to-all-done
  723.7 10.3 %place_gradients.1 = (f32[10,192,512]{2,1,0:T(8,128)}, f32[10,192,512]{2,1,0:T(8,128)}, f32[10,64,1536]{2,1,0:T(8,128)}) custom-call(bf16[2,4,2,576,512]{4,3,2,1,0:T(8,128)(2,1)} %bitcast.10.refs_0_, bf16[2,4,1,576,256]{4,3,2,1,0:T(8,128)(2,1)} %bitcast.29), custom_call_target="tpu_custom_call" | custom-call | flops 1048576 | bytes 65536 | tf_op jit(solution)/shard_map/place_gradients/pallas_call | solution.py:360
  734.0 0.0 copy-done.4
  734.0 1.3 copy.54
  735.3 0.0 copy-done.5
  735.3 0.7 copy.55
  736.0 0.0 copy-done.8
  736.0 0.6 copy.56
  736.7 0.6 copy.57
  (17 shorter events, 0.2 us)
Async XLA Ops:
  7.2 9.8 %copy-start = (bf16[48,512]{1,0:T(8,128)(2,1)S(1)}, bf16[48,512]{1,0:T(8,128)(2,1)}, u32[]{:S(2)}) copy-start(bf16[48,512]{1,0:T(8,128)(2,1)} %param.17) | copy-start | bytes 147460
  7.2 9.8 %copy-start.9 = (bf16[48,512]{1,0:T(8,128)(2,1)S(1)}, bf16[48,512]{1,0:T(8,128)(2,1)}, u32[]{:S(2)}) copy-start(bf16[48,512]{1,0:T(8,128)(2,1)} %param.18) | copy-start | bytes 147460
  7.2 160.2 %all-gather.2.cloned.1.call-start = ((), (), s32[]{:S(2)}) async-start(), calls=%async_computation.2 | async-start | bytes 16711680 | tf_op jit(solution)/shard_map/all_gather | solution.py:1115
  260.5 58.5 %all-to-all-start.1 = ((bf16[8,1,576,256]{3,2,1,0:T(8,128)(2,1)}), bf16[8,1,576,256]{3,2,1,0:T(8,128)(2,1)S(1)}, u32[]{:S(2)}, u32[]{:S(2)}) async-start(bf16[8,1,576,256]{3,2,1,0:T(8,128)(2,1)} %get-tuple-element.88), calls=%async_computation.1 | async-start | bytes 4718592 | tf_op jit(solution)/shard_map/all_to_all | solution.py:1139
  319.0 1.4 copy-start.2
  320.4 403.3 %all-to-all-start = ((bf16[8,2,576,512]{3,2,1,0:T(8,128)(2,1)}), bf16[8,2,576,512]{3,2,1,0:T(8,128)(2,1)}, u32[]{:S(2)}, u32[]{:S(2)}) async-start(bf16[8,2,576,512]{3,2,1,0:T(8,128)(2,1)} %get-tuple-element.87), calls=%async_computation | async-start | bytes 18874368 | tf_op jit(solution)/shard_map/all_to_all | solution.py:1141
  626.6 92.2 %copy-start.3 = (f32[320,1536]{1,0:T(8,128)S(1)}, f32[320,1536]{1,0:T(8,128)}, u32[]{:S(2)}) copy-start(f32[320,1536]{1,0:T(8,128)} %get-tuple-element.53.refs_4_) | copy-start | bytes 5898244
  626.6 96.3 %collective-permute-start = (bf16[48,1536]{1,0:T(8,128)(2,1)}, bf16[48,1536]{1,0:T(8,128)(2,1)S(1)}, u32[]{:S(2)}, u32[]{:S(2)}) collective-permute-start(bf16[48,1536]{1,0:T(8,128)(2,1)} %get-tuple-element.85), channel_id=1, source_target_pairs={{0,0},{1,8},{2,16},{3,24},{4,1},{5,9},{6,17},{7,25},{8,2},{9,10},{... | collective-permute-start | bytes 442376 | tf_op jit(solution)/shard_map/ppermute | solution.py:1165
  718.8 2.7 copy-start.6
  723.7 10.4 %copy-start.4 = (f32[320,1536]{1,0:T(8,128)S(1)}, f32[320,1536]{1,0:T(8,128)}, u32[]{:S(2)}) copy-start(f32[320,1536]{1,0:T(8,128)} %get-tuple-element.138) | copy-start | bytes 5898244
  723.7 13.6 %copy-start.1 = (bf16[48,512]{1,0:T(8,128)(2,1)S(1)}, bf16[48,512]{1,0:T(8,128)(2,1)}, u32[]{:S(2)}) copy-start(bf16[48,512]{1,0:T(8,128)(2,1)} %param.17) | copy-start | bytes 147460
  734.0 1.3 copy-start.5
  734.0 2.0 copy-start.8
  734.0 2.7 copy-start.7
Sparse Core Ops, SparseCore 0:
  9.6 126.9 all-gather.1

commit v4 on v3

--- a/solution.py
+++ b/solution.py
@@ -2,6 +2,7 @@
 
 import jax
 import jax.numpy as jnp
+import numpy as np
 from jax import lax
 from jax.experimental import pallas as pl
 from jax.experimental.pallas import tpu as pltpu
@@ -20,45 +21,11 @@
 masked_score = -1e30
 
 
-def dot32(spec, a, b):
-    return jnp.einsum(spec, a, b, preferred_element_type=F32)
-
-
-def norm_parts(values, gain_row):
-    scaling = lax.rsqrt(jnp.mean(values * values, axis=-1, keepdims=True) + epsilon)
-    normed = values * scaling
-    return (normed * gain_row, normed, scaling)
-
-
-def norm_back(grad_rows, normed, scaling, gain_row):
-    grad_normed = grad_rows * gain_row
-    grad_gain = jnp.sum(grad_rows * normed, axis=0)
-    inner_sum = jnp.mean(grad_normed * normed, axis=-1, keepdims=True)
-    return (scaling * (grad_normed - normed * inner_sum), grad_gain)
-
-
-def rope_tables(positions, head_size):
-    frequency = rope_base ** (-2.0 * jnp.arange(head_size // 2, dtype=F32) / head_size)
-    angles = positions.astype(F32)[:, None] * frequency[None, :]
-    return (jnp.cos(angles), jnp.sin(angles))
-
-
-def slot_dense(routes, priority, experts, capacity):
-    rows, top_count = routes.shape
-    hot = routes[:, :, None] == jnp.arange(experts, dtype=jnp.int32)
-    rank = jnp.sum(jnp.where(hot, priority[:, :, None] + 1, 0), axis=1) - 1
-    per_rank = rank[None] == jnp.arange(top_count, dtype=jnp.int32)[:, None, None]
-    flat = jnp.transpose(per_rank.astype(BF16), (1, 0, 2)).reshape(rows, top_count * experts)
-    index = jnp.arange(rows, dtype=jnp.int32)
-    before = (index[None, :] < index[:, None]).astype(BF16)
-    within = jnp.dot(before, flat, preferred_element_type=F32).reshape(rows, top_count, experts)
-    totals = jnp.sum(per_rank.astype(F32), axis=1)
-    base = jnp.cumsum(totals, axis=0) - totals
-    slot = jnp.sum(
-        jnp.where(jnp.transpose(per_rank, (1, 0, 2)), within + base[None], 0.0), axis=1
-    )
-    named = rank >= 0
-    return named, jnp.where(named & (slot < capacity), slot, -1.0)
+def rope_tables(length):
+    frequency = np.float32(rope_base) ** (np.float32(-2.0) * np.arange(HD // 2, dtype=np.float32) / np.float32(HD))
+    angles = np.arange(length, dtype=np.float32)[:, None] * frequency[None, :].astype(np.float32)
+    cosine, sine = np.cos(angles).astype(np.float32), np.sin(angles).astype(np.float32)
+    return np.tile(cosine, (1, 4)), np.tile(np.concatenate([-sine, sine], axis=1), (1, 2))
 
 
 NT=(((1,),(1,)),((),()))
@@ -111,31 +78,55 @@
 def group_member(mask):
     return flip(member_r(), mask >> 2) * 4 + flip(lax.axis_index("expert"), mask & 3)
 
+def greet_devices(devices):
+    barrier = pltpu.get_barrier_semaphore()
+    for device in devices:
+        pl.semaphore_signal(barrier, inc=1, device_id=device, device_id_type=MESH)
+    pl.semaphore_wait(barrier, len(devices))
+
 def greet(masks):
-    barrier = pltpu.get_barrier_semaphore()
-    for mask in masks:
-        pl.semaphore_signal(barrier, inc=1, device_id=group_device(mask), device_id_type=MESH)
-    pl.semaphore_wait(barrier, len(masks))
-
-def last_hop(part, mask):
+    greet_devices([group_device(mask) for mask in masks])
+
+DM_ORDERS = ((2, 4, 8), (2, 8, 4))
+
+def last_hop(order, mask):
     if mask & CORE:
         return CORE
-    return [bit for bit in GATHER_ORDERS[part] if mask & bit][-1]
-
-def gather_order():
+    return [bit for bit in order if mask & bit][-1]
+
+def block_copies(own_ref, held_ref, orders, send, recv):
+    part_width = own_ref.shape[1] // len(orders)
+    copies = {}
+    for p, order in enumerate(orders):
+        columns = pl.ds(p * part_width, part_width)
+        for mask in range(1, 16):
+            hop = last_hop(order, mask)
+            source = own_ref.at[:, columns] if mask == hop else held_ref.at[mask ^ hop, :, columns]
+            copies[p, mask] = pltpu.make_async_remote_copy(source, held_ref.at[mask, :, columns], send.at[p, mask], recv.at[p, mask],
+                device_id=group_device(hop), device_id_type=MESH)
+    return copies
+
+def block_start(copies, orders, arrived):
+    p, mask = arrived
+    for nxt in range(1, 16):
+        if nxt != mask and nxt ^ last_hop(orders[p], nxt) == mask:
+            copies[p, nxt].start()
+
+def gather_order(orders):
+    parts = range(len(orders))
     free = {2: 0.0, 4: 0.0, 8: 0.0}
-    arrived, todo = {(p, 0): 0.0 for p in range(len(GATHER_ORDERS))}, [(p, m) for p in range(len(GATHER_ORDERS)) for m in range(2, 16, 2)]
+    arrived, todo = {(p, 0): 0.0 for p in parts}, [(p, m) for p in parts for m in range(2, 16, 2)]
     order = []
     while todo:
         best = None
         for p, m in todo:
-            hop = last_hop(p, m)
+            hop = last_hop(orders[p], m)
             if (p, m ^ hop) in arrived:
-                key = (max(free[hop], arrived[p, m ^ hop]), GATHER_ORDERS[p].index(hop), p, m)
+                key = (max(free[hop], arrived[p, m ^ hop]), orders[p].index(hop), p, m)
                 if best is None or key < best:
                     best = key
         start, _, p, m = best
-        hop = last_hop(p, m)
+        hop = last_hop(orders[p], m)
         free[hop] = start + 1
         arrived[p, m] = start + 1
         todo.remove((p, m))
@@ -158,20 +149,13 @@
         copy.start()
         tables.append(copy)
     arrived[0] = table_ref[group_member(0)]
-    copies = {}
-    for p in range(len(GATHER_ORDERS)):
-        for mask in range(1, 16):
-            hop = last_hop(p, mask)
-            source = mask ^ hop
-            src = h2_ref.at[:, pl.ds(p * part_width, part_width)] if source == 0 else held.at[p, source]
-            copies[p, mask] = pltpu.make_async_remote_copy(src, held.at[p, mask], send.at[p, mask], recv.at[p, mask],
-                device_id=group_device(hop), device_id_type=MESH)
-    order = gather_order()
+    copies = block_copies(h2_ref, held, GATHER_ORDERS, send, recv)
+    order = gather_order(GATHER_ORDERS)
     for p, mask in order + [(p, CORE) for p in range(len(GATHER_ORDERS))]:
-        if mask ^ last_hop(p, mask) == 0:
+        if mask == last_hop(GATHER_ORDERS[p], mask):
             copies[p, mask].start()
     def dm_copy(mask):
-        return pltpu.make_async_copy(dm_ref.at[group_member(mask)], dm_held.at[mask % 2], dm_sem.at[mask % 2])
+        return pltpu.make_async_copy(dm_ref.at[mask], dm_held.at[mask % 2], dm_sem.at[mask % 2])
     dm_copy(0).start()
     for copy in tables:
         copy.wait_recv()
@@ -199,10 +183,9 @@
     dm_step(todo.pop(0))
     def arrive(p, mask):
         copies[p, mask].wait_recv()
-        for nxt in range(1, 16):
-            if nxt != mask and (nxt ^ last_hop(p, nxt)) == mask:
-                copies[p, nxt].start()
-        place(rows_ref, mask, hots(mask), held[p, mask], pl.ds(p * part_width, part_width))
+        block_start(copies, GATHER_ORDERS, (p, mask))
+        columns = pl.ds(p * part_width, part_width)
+        place(rows_ref, mask, hots(mask), held[mask, :, columns], columns)
     for step, (p, mask) in enumerate(order):
         arrive(p, mask)
         if todo:
@@ -223,7 +206,7 @@
     return pl.pallas_call(functools.partial(gather_kernel, slots, capacity),
         out_shape=(rows, rows, jax.ShapeDtypeStruct((slots, 16 * capacity, 1), F32), jax.ShapeDtypeStruct(table.shape, F32)),
         in_specs=[V, V, pl.BlockSpec(memory_space=pl.ANY)], out_specs=(V,) * 4,
-        scratch_shapes=[pltpu.VMEM((len(GATHER_ORDERS), 16, tokens, width // len(GATHER_ORDERS)), BF16), pltpu.VMEM(table.shape, F32),
+        scratch_shapes=[pltpu.VMEM((16, tokens, width), BF16), pltpu.VMEM(table.shape, F32),
             pltpu.VMEM((2, tokens, width), BF16), pltpu.SemaphoreType.DMA((len(GATHER_ORDERS), 16)), pltpu.SemaphoreType.DMA((len(GATHER_ORDERS), 16)),
             pltpu.SemaphoreType.DMA((16,)), pltpu.SemaphoreType.DMA((16,)), pltpu.SemaphoreType.DMA((2,))],
         compiler_params=pltpu.CompilerParams(vmem_limit_bytes=58 << 20, collective_id=collective_id, has_side_effects=True),
@@ -308,16 +291,16 @@
         cost_estimate=CHEAP,
         name="expert_part" if ways > 1 else "experts")(scalars, rows, dm_rows, weight, w_gate, w_up, w_down)
 
-def place_kernel(whole, rest, ways, *refs):
+def place_kernel(whole, rest, ways, order_ref, *refs):
     moved, (gate_ref, up_ref, down_ref) = refs[:-3], refs[-3:]
     i = pl.program_id(0)
     share, down_share = gate_ref.shape[1], down_ref.shape[1]
     width, ff = down_ref.shape[2], gate_ref.shape[2]
-    quads = moved[0].shape[0]
+    quads = moved[0].shape[2]
     @pl.when(i < QUAD)
     def _():
         for s in range(whole):
-            block = sum(moved[0][k, 0, s].astype(F32) for k in range(quads))
+            block = sum(moved[0][s, 0, k].astype(F32) for k in range(quads))
             gate_ref[s] = block[:share]
             up_ref[s] = block[share:2 * share]
             for c in range(width // ff):
@@ -344,46 +327,90 @@
                 gate_ref[x] = gate[:share]
                 up_ref[x] = gate[share:]
 
-def place_call(moved, local, ffn, width):
-    whole = local // QUAD
+def place_call(moved, shared, order, local, ffn, width):
+    whole, _, quads, rows, _ = moved.shape
     rest = local - whole * QUAD
     ways = QUAD // rest if rest else 1
-    share = moved[0].shape[2] // 3
+    share = rows // 3
     down_share = ffn * share // width
-    quads = moved[0].shape[0] // QUAD
-    steps = QUAD + (1 if rest else 0)
-    moved = [a.reshape((quads, QUAD) + a.shape[1:]) for a in moved]
-    one = lambda a: pl.BlockSpec((quads, 1) + a.shape[2:], lambda i: (0, jnp.minimum(i, QUAD - 1), 0, 0, 0))
-    full = lambda a: pl.BlockSpec(a.shape, lambda i: (0, 0, 0, 0, 0))
-    out = lambda a, b: pl.BlockSpec((whole, a, b), lambda i: (i, 0, 0))
+    shared = [a.reshape((quads, QUAD) + a.shape[1:]) for a in shared]
+    full = lambda a: pl.BlockSpec(a.shape, lambda i, s: (0, 0, 0, 0, 0))
+    out = lambda a, b: pl.BlockSpec((whole, a, b), lambda i, s: (i, 0, 0))
     S = jax.ShapeDtypeStruct
-    return pl.pallas_call(functools.partial(place_kernel, whole, rest, ways), grid=(steps,),
-        in_specs=[one(moved[0])] + [full(a) for a in moved[1:]],
-        out_specs=(out(share, ffn), out(share, ffn), out(down_share, width)),
+    return pl.pallas_call(functools.partial(place_kernel, whole, rest, ways),
+        grid_spec=pltpu.PrefetchScalarGridSpec(num_scalar_prefetch=1, grid=(QUAD + (1 if rest else 0),),
+            in_specs=[pl.BlockSpec((whole, 1, quads, rows, ffn), lambda i, s: (0, s[jnp.minimum(i, QUAD - 1)], 0, 0, 0))]
+                + [full(a) for a in shared],
+            out_specs=(out(share, ffn), out(share, ffn), out(down_share, width))),
         out_shape=(S((local, share, ffn), F32), S((local, share, ffn), F32), S((local, down_share, width), F32)),
         compiler_params=pltpu.CompilerParams(vmem_limit_bytes=58 << 20, dimension_semantics=("arbitrary",)),
-        cost_estimate=CHEAP, name="place_gradients")(*moved)
+        cost_estimate=CHEAP, name="place_gradients")(order, moved, *shared)
+
+def relative_device(k, m):
+    return device_at((lax.axis_index("q") + k) % lax.axis_size("q"), flip(member_r(), m), lax.axis_index("expert"))
+
+def carry_keys(quads, slots, with_x):
+    ms = (1, 3) if with_x else (0, 2)
+    return [(s, k, m) for s in slots for m in ms for k in range(quads) if (k, m) != (0, 0)]
+
+def carry_copies(grads_ref, moved_ref, keys, send, recv):
+    quads = lax.axis_size("q")
+    copies = []
+    for s, k, m in keys:
+        q, r = (lax.axis_index("q") + k) % quads, flip(member_r(), m)
+        copies.append(pltpu.make_async_remote_copy(grads_ref.at[place_at(q, r), s], moved_ref.at[s, m, (quads - k) % quads],
+            send.at[s, m, k], recv.at[s, m, (quads - k) % quads], device_id=relative_device(k, m), device_id_type=MESH))
+    return copies
+
+def carry_start(copies, keys, late):
+    outer = lax.axis_index("q") % 2 == lax.axis_index("rh")
+    for copy, (_, k, _m) in zip(copies, keys):
+        if not k:
+            if not late:
+                copy.start()
+        elif late:
+            pl.when(jnp.logical_not(outer))(copy.start)
+        else:
+            pl.when(outer)(copy.start)
+
+def carry_plan(quads, whole):
+    z, x = carry_keys(quads, range(whole), False), carry_keys(quads, range(whole), True)
+    first = [key for key in z if key[0] == 0]
+    second = [key for key in x if key[0] == 0 or key[1] == 0] + [key for key in z if key[0] and (key[1] == 0 or key[2] == 0)]
+    third = [key for key in x + z if key not in first and key not in second]
+    return first, second, third
 
 def first_hop(part, mask):
     return [bit for bit in SUM_ORDERS[part] if mask & bit][0]
 
-def combine_kernel(banks, slots, capacity, with_dg, *refs):
-    rows = refs[:banks]
-    refs = refs[banks:]
-    tables_ref = refs[0]
-    refs = refs[1:]
+def combine_kernel(banks, slots, capacity, with_dg, carried, *refs):
+    rows, refs = refs[:banks], refs[banks:]
+    tables_ref, refs = refs[0], refs[1:]
     if with_dg:
-        dg_refs, refs = refs[:banks], refs[banks:]
-        out_ref, dg_out = refs[:2]
-        refs = refs[2:]
+        dg_refs, grads_ref, refs = refs[:banks], refs[banks], refs[banks + 1:]
+        out_ref, dg_out, moved_ref, refs = refs[0], refs[1], refs[2], refs[3:]
     else:
-        out_ref, refs = refs[0], refs[1:]
-    core_out, core_in, held, got, core_send, core_recv, send, recv = refs[:8]
+        middle_ref, grads_ref, _, out_ref, moved_ref, refs = refs[0], refs[1], refs[2], refs[3], refs[4], refs[5:]
+    core_out, core_in, held, got, core_send, core_recv, send, recv, carry_send, carry_recv, own_sem = refs[:11]
     if with_dg:
-        dg_hold, dg_in, dg_send, dg_recv = refs[8:]
+        dg_hold, dg_in, dg_send, dg_recv = refs[11:]
     width = out_ref.shape[1]
     part_width = width // len(SUM_ORDERS)
-    greet(range(1, 16) if with_dg else (1, 2, 4, 8))
+    masks = list(range(1, 16)) if with_dg else [1, 2, 4, 8]
+    far = sorted({(k, m) for _, k, m in carried if k or m * 4 not in masks})
+    greet_devices([group_device(mask) for mask in masks] + [relative_device(k, m) for k, m in far])
+    carries = carry_copies(grads_ref, moved_ref, carried, carry_send, carry_recv)
+    straight = [n for n, key in enumerate(carried) if not key[2] & 1]
+    turning = [n for n, key in enumerate(carried) if key[2] & 1]
+    def carry(chosen, late):
+        carry_start([carries[n] for n in chosen], [carried[n] for n in chosen], late)
+    carry(straight, False)
+    own_copies = []
+    if with_dg:
+        for s in range(moved_ref.shape[0]):
+            own_copies.append(pltpu.make_async_copy(grads_ref.at[place_at(lax.axis_index("q"), member_r()), s],
+                moved_ref.at[s, 0, 0], own_sem.at[s]))
+            own_copies[-1].start()
     def hots(mask):
         return one_hot(tables_ref[mask], capacity, slots)
     def block_sum(mask, hot):
@@ -429,6 +456,8 @@
             if mask & SUM_ORDERS[p][0]:
                 copies[p, mask].start()
         dg_step(mask, hot)
+    carry(turning, False)
+    carry(straight + turning, True)
     def add(p, target, sources):
         total = held[p, target // 2].astype(F32)
         for source in sources:
@@ -448,7 +477,9 @@
         forward(p, c, [c | a, c | b])
     for p in range(len(SUM_ORDERS)):
         a, b, c = SUM_ORDERS[p]
-        out_ref[:, p * part_width:(p + 1) * part_width] = add(p, 0, [a, b, c])
+        columns = pl.ds(p * part_width, part_width)
+        total = add(p, 0, [a, b, c])
+        out_ref[:, columns] = total if with_dg else (middle_ref[:, columns] + total).astype(BF16)
     if with_dg:
         dg_out[0] = dg_hold[0]
         for copy in dg_copies:
@@ -461,25 +492,35 @@
         core[mask].wait_send()
     for key in copies:
         copies[key].wait_send()
-
-def combine_rows(rows, tables, dgs, capacity, collective_id):
+    for copy in carries:
+        copy.wait()
+    for copy in own_copies:
+        copy.wait()
+
+def combine_rows(rows, tables, dgs, middle, grads, moved, carried, capacity, collective_id):
     banks, slots = len(rows), sum(a.shape[0] for a in rows)
     tokens, width = tables.shape[2], rows[0].shape[2]
-    V = pl.BlockSpec(memory_space=pltpu.VMEM)
+    V, A = pl.BlockSpec(memory_space=pltpu.VMEM), pl.BlockSpec(memory_space=pl.ANY)
     with_dg = dgs is not None
-    out = jax.ShapeDtypeStruct((tokens, width), F32)
+    quads, whole = grads.shape[0] // QUAD, grads.shape[1]
+    out = jax.ShapeDtypeStruct((tokens, width), F32 if with_dg else BF16)
+    moved_shape = jax.ShapeDtypeStruct((whole, QUAD, quads) + grads.shape[2:], grads.dtype)
     table = pltpu.VMEM(tables.shape, F32)
     sem = pltpu.SemaphoreType.DMA
-    return pl.pallas_call(functools.partial(combine_kernel, banks, slots, capacity, with_dg),
-        out_shape=(out, jax.ShapeDtypeStruct(tables.shape, F32)) if with_dg else out,
-        in_specs=[V] * (banks + 1 + (banks if with_dg else 0)), out_specs=(V, V) if with_dg else V,
+    parts = len(SUM_ORDERS)
+    operands = list(rows) + [tables] + (list(dgs) + [grads] if with_dg else [middle, grads, moved])
+    return pl.pallas_call(functools.partial(combine_kernel, banks, slots, capacity, with_dg, carried),
+        out_shape=(out, jax.ShapeDtypeStruct(tables.shape, F32), moved_shape) if with_dg else (out, moved_shape),
+        in_specs=[V] * (banks + 1 + (banks if with_dg else 1)) + [A] * (1 if with_dg else 2),
+        out_specs=(V, V, A) if with_dg else (V, A),
+        input_output_aliases={} if with_dg else {banks + 3: 1},
         scratch_shapes=[pltpu.VMEM((8, tokens, width), BF16), pltpu.VMEM((8, tokens, width), BF16),
-            pltpu.VMEM((len(SUM_ORDERS), 8, tokens, width // len(SUM_ORDERS)), BF16), pltpu.VMEM((len(SUM_ORDERS), 8, tokens, width // len(SUM_ORDERS)), BF16),
-            sem((8,)), sem((8,)), sem((len(SUM_ORDERS), 8)), sem((len(SUM_ORDERS), 8))] + ([table, table, sem((16,)), sem((16,))] if with_dg else []),
+            pltpu.VMEM((parts, 8, tokens, width // parts), BF16), pltpu.VMEM((parts, 8, tokens, width // parts), BF16),
+            sem((8,)), sem((8,)), sem((parts, 8)), sem((parts, 8)), sem((whole, QUAD, quads)), sem((whole, QUAD, quads)), sem((whole,))]
+            + ([table, table, sem((16,)), sem((16,))] if with_dg else []),
         compiler_params=pltpu.CompilerParams(vmem_limit_bytes=58 << 20, collective_id=collective_id, has_side_effects=True),
         cost_estimate=CHEAP,
-        name="combine_with_dg" if with_dg else "combine_rows")(*rows, tables, *(dgs if with_dg else ()))
-
+        name="combine_with_dg" if with_dg else "combine_rows")(*operands)
 
 DP_ORDERS = (("q", 1, 2), ("q", 2, 1), ("q", 2, 1))
 
@@ -530,10 +571,10 @@
 
 def start_kernel(dims, exchange, *refs):
     (experts, capacity, top_count, q_cols, k_cols, rows_here, shard_rows) = dims
-    (tokens_ref, pieces_ref, wout_ref, routes_ref, priority_ref, seg_ref, cos_ref, sin_ref,
-     x_out, w_out, wout_out, h1_ref, q_ref, k_ref, v_ref, o_ref, lse_ref, middle_ref, h2_ref, table_ref, probs_ref, gains_ref,
+    (tokens_ref, pieces_ref, wout_ref, cot_ref, routes_ref, priority_ref, seg_ref, cos_ref, sin_ref,
+     x_out, w_out, wout_out, h1_ref, q_ref, k_ref, v_ref, o_ref, lse_ref, middle_ref, h2_ref, table_ref, probs_ref, gains_ref, dm_ref,
      xs, ws, wouts, vt_ref, h1s, os, own_sem,
-     x_send, x_recv, p_send, p_recv, w_send, w_recv, o_send, o_recv, wo_send, wo_recv, wx_send, wx_recv) = refs
+     x_send, x_recv, p_send, p_recv, w_send, w_recv, o_send, o_recv, wo_send, wo_recv, wx_send, wx_recv, dm_send, dm_recv, dm_sem) = refs
     E = lax.axis_size("expert")
     quads = lax.axis_size("q")
     dp = quads * QUAD
@@ -549,6 +590,12 @@
     barrier = pltpu.get_barrier_semaphore()
     friends = [device_at(q, r, flip(e, j)) for j in (1, 2, 3)] + [device_at(q, flip(r, m), e) for m in (1, 2)]
     friends += [device_at((q + k) % quads, r, e) for k in range(1, quads)]
+    dm_copies = block_copies(cot_ref, dm_ref, DM_ORDERS, dm_send, dm_recv)
+    dm_order = gather_order(DM_ORDERS)
+    def dm_arrive(wanted):
+        for key in wanted:
+            dm_copies[key].wait_recv()
+            block_start(dm_copies, DM_ORDERS, key)
     for friend in friends:
         pl.semaphore_signal(barrier, inc=1, device_id=friend, device_id_type=MESH)
     pl.semaphore_wait(barrier, len(friends))
@@ -576,6 +623,11 @@
         ws[pl.ds(mine, block_rows), :] = pieces_ref[...]
     x_copies[2].start()
     x_copies[1].start()
+    for p in range(len(DM_ORDERS)):
+        dm_copies[p, 2].start()
+        dm_copies[p, CORE].start()
+    dm_own = pltpu.make_async_copy(cot_ref, dm_ref.at[0], dm_sem)
+    dm_own.start()
     xs[token_rows(e), :] = tokens_ref[...]
     w_copies = dp_copies(ws, block_rows, lambda d: pl.multiple_of(d * block_rows, 16), total // 3, w_send, w_recv)
     for copy in p_copies:
@@ -593,8 +645,9 @@
 
     lane = lax.broadcasted_iota(jnp.int32, (rows_here, 128), 1)
     rank = jnp.zeros((rows_here, 128), jnp.int32)
+    routes, priority = routes_ref[...].T, priority_ref[...].T
     for j in range(top_count):
-        rank = rank + jnp.where(routes_ref[:, j:j + 1] == lane, priority_ref[:, j:j + 1] + 1, 0)
+        rank = rank + jnp.where(routes[:, j:j + 1] == lane, priority[:, j:j + 1] + 1, 0)
     rank = rank - 1
     before = (lax.broadcasted_iota(jnp.int32, (rows_here, rows_here), 1)
               < lax.broadcasted_iota(jnp.int32, (rows_here, rows_here), 0)).astype(F32).astype(BF16)
@@ -629,7 +682,15 @@
                 wx_copies[d, j] = pltpu.make_async_remote_copy(wouts.at[rows], wouts.at[rows], wx_send.at[d, j], wx_recv.at[d, j],
                     device_id=device_at(q, r, flip(e, j if j < 3 else 1)), device_id_type=MESH)
     def out_step(step):
+        if step == 2:
+            dm_arrive([key for key in dm_order if key[1] == 2])
+        if step == 4:
+            dm_arrive([key for key in dm_order if key[1] in (4, 8)])
         if not exchange:
+            if step == 1:
+                for p, (_, b, c) in enumerate(DM_ORDERS):
+                    dm_copies[p, b].start()
+                    dm_copies[p, c].start()
             return
         third = -(-len(wo_order) // 2)
         if step < 2:
@@ -637,6 +698,10 @@
                 wo_copies[key].wait_recv()
                 dp_start(wo_copies, key)
         if step == 1:
+            for p, (_, b, c) in enumerate(DM_ORDERS):
+                dm_copies[p, b].start()
+            for p, (_, b, c) in enumerate(DM_ORDERS):
+                dm_copies[p, c].start()
             for d in range(dp):
                 wx_copies[d, 2].start()
             for d in range(dp):
@@ -738,6 +803,13 @@
                 row = dest_e * local + expert
                 table_ref[dest_r * E + dest_e, at:at + 1, :] = slot_rows[row:row + 1, :]
                 table_ref[dest_r * E + dest_e, 4 + at:5 + at, :] = prob_rows[row:row + 1, :]
+    dm_arrive([key for key in dm_order if key[1] not in (2, 4, 8)])
+    for key in dm_copies:
+        if key[1] & CORE:
+            dm_copies[key].wait_recv()
+    for key in dm_copies:
+        dm_copies[key].wait_send()
+    dm_own.wait()
     for b in range(E):
         @pl.when(e != b)
         def _():
@@ -747,7 +819,7 @@
     for copy in (x_back, w_back, h1_back, wout_back):
         copy.wait()
 
-def start_call(tokens, pieces, w_out, routes, priority, segments, cosine, sine, experts, capacity, q_cols, k_cols, exchange):
+def start_call(tokens, pieces, w_out, cotangent, routes, priority, segments, cosine, sine, experts, capacity, q_cols, k_cols, exchange):
     E, quads = lax.axis_size("expert"), lax.axis_size("q")
     dp = quads * QUAD
     rows_here, width = tokens.shape
@@ -758,39 +830,41 @@
     heads, kv_heads = q_cols // HD, k_cols // HD
     S = jax.ShapeDtypeStruct
     sem = pltpu.SemaphoreType.DMA
-    dims = (experts, capacity, routes.shape[1], q_cols, k_cols, rows_here, shard_rows)
+    dims = (experts, capacity, routes.shape[0], q_cols, k_cols, rows_here, shard_rows)
     kernel = functools.partial(start_kernel, dims, exchange)
     return pl.pallas_call(kernel,
         out_shape=(S((length, width), BF16), S((width, total), BF16), S((width, width), BF16), S((length, width), BF16),
             S((heads, length, HD), BF16), S((kv_heads, length, HD), BF16), S((kv_heads, length, HD), BF16),
             S((length, q_cols), BF16), S((-(-heads // 8) * 8, length), F32), S((rows_here, width), F32), S((rows_here, width), BF16),
-            S((QUAD * E, 8, rows_here), F32), S((rows_here, 128), F32), S((8, width), F32)),
-        in_specs=[V, V, V if exchange else A, V, V, V, V, V], out_specs=(A, A, A, A) + (V,) * 10,
+            S((QUAD * E, 8, rows_here), F32), S((rows_here, 128), F32), S((8, width), F32),
+            S((QUAD * E, rows_here, width), BF16)),
+        in_specs=[V, V, V if exchange else A, A, V, V, V, V, V], out_specs=(A, A, A, A) + (V,) * 10 + (A,),
         scratch_shapes=[pltpu.VMEM((length, width), BF16), pltpu.VMEM((width, total), BF16), pltpu.VMEM((width, width), BF16),
             pltpu.VMEM((kv_heads, HD, length), BF16), pltpu.VMEM((length, width), BF16), pltpu.VMEM((E, rows_here, q_cols), BF16), sem((4,)),
             sem((4,)), sem((4,)), sem((4,)), sem((4,)), sem((3, quads, QUAD)), sem((3, quads, QUAD)), sem((E,)), sem((E,)),
-            sem((3, quads, QUAD)), sem((3, quads, QUAD)), sem((dp, 4)), sem((dp, 4))],
+            sem((3, quads, QUAD)), sem((3, quads, QUAD)), sem((dp, 4)), sem((dp, 4)),
+            sem((len(DM_ORDERS), 16)), sem((len(DM_ORDERS), 16)), sem],
         compiler_params=pltpu.CompilerParams(vmem_limit_bytes=58 << 20, collective_id=4, has_side_effects=True),
         cost_estimate=CHEAP,
-        name="start")(tokens, pieces, w_out, routes, priority, segments.reshape(1, -1), cosine, sine)
+        name="start")(tokens, pieces, w_out, cotangent, routes, priority, segments.reshape(1, -1), cosine, sine)
 
 
 DENSE_ORDERS = ((1, 2, "q"), (2, 1, "q"))
 
-def back_kernel(dims, exchange, *refs):
+def back_kernel(dims, exchange, carried, *refs):
     (experts, q_cols, k_cols, slots) = dims
     (dr_ref, dg_ref, probs_ref, h2_ref, middle_ref, cot_ref, gains_ref, tokens_ref, wout_ref, q_ref, k_ref, v_ref, lse_ref,
-     cos_ref, sin_ref, seg_ref, h1_ref, xall_ref, wall_ref, mixed_ref) = refs[:20]
-    refs = refs[20:]
+     cos_ref, sin_ref, seg_ref, h1_ref, xall_ref, wall_ref, mixed_ref, grads_ref, _) = refs[:22]
+    refs = refs[22:]
     if exchange:
-        (tokens_out, gq_ref, gk_ref, gv_ref, small_ref, gout_ref) = refs[:6]
-        refs = refs[6:]
+        (tokens_out, gq_ref, gk_ref, gv_ref, small_ref, gout_ref, moved_ref) = refs[:7]
+        refs = refs[7:]
     else:
-        (tokens_out, dense_ref, gout_ref) = refs[:3]
-        refs = refs[3:]
+        (tokens_out, dense_ref, gout_ref, moved_ref) = refs[:4]
+        refs = refs[4:]
     (h1s, xs, ws, mixeds, load_sem, dgt, dats, dos, do_out, kt_ref, dk_ref, dv_ref, dqkv, dx1s, small, part, core_in, y_in,
      g1, g2, r1, r2, f1,
-     do_send, do_recv, dat_send, dat_recv, part_send, part_recv, g1_send, g1_recv, g2_send, g2_recv, f_send, f_recv) = refs
+     do_send, do_recv, dat_send, dat_recv, part_send, part_recv, g1_send, g1_recv, g2_send, g2_recv, f_send, f_recv, carry_send, carry_recv) = refs
     E, quads = lax.axis_size("expert"), lax.axis_size("q")
     q, r, e = lax.axis_index("q"), member_r(), lax.axis_index("expert")
     dp = quads * QUAD
@@ -808,12 +882,11 @@
     load_out.start()
     for load in loads[:3]:
         load.start()
-    barrier = pltpu.get_barrier_semaphore()
-    friends = [device_at(q, r, flip(e, j)) for j in (1, 2, 3)] + [device_at(q, flip(r, m), e) for m in (1, 2)]
-    friends += [device_at((q + k) % quads, r, e) for k in range(1, quads)]
-    for friend in friends:
-        pl.semaphore_signal(barrier, inc=1, device_id=friend, device_id_type=MESH)
-    pl.semaphore_wait(barrier, len(friends))
+    near = [(0, 1), (0, 2)] + [(k, 0) for k in range(1, quads)]
+    far = sorted({(k, m) for _, k, m in carried} - set(near))
+    greet_devices([device_at(q, r, flip(e, j)) for j in (1, 2, 3)] + [relative_device(k, m) for k, m in near + far])
+    carries = carry_copies(grads_ref, moved_ref, carried, carry_send, carry_recv)
+    carry_start(carries, carried, False)
 
     dgt[...] = jnp.zeros_like(dgt)
     local = experts // E
@@ -903,6 +976,7 @@
         if i == 1:
             dat_copies[2].wait_recv()
             dat_copies[3].start()
+            carry_start(carries, carried, True)
     dk = jnp.concatenate([dk_ref[g] for g in range(kv_heads)], axis=1) * factor
     cosine = jnp.concatenate([cos_ref[...]] * (k_cols // 128), axis=1)
     sine = jnp.concatenate([sin_ref[...]] * (k_cols // 128), axis=1)
@@ -1038,9 +1112,11 @@
             do_descriptor(b).wait_send()
     for copy in list(dat_copies.values()) + list(part_copies.values()) + list(copies.values()):
         copy.wait_send()
+    for copy in carries:
+        copy.wait()
 
 def back_call(dr_sum, dg_back, probs, h2, middle, cotangent, gains, tokens, out_full, query, key, value, log_total,
-              cosine, sine, segments, h1_all, x_all, w_all, mixed, experts, q_cols, k_cols, slots, exchange):
+              cosine, sine, segments, h1_all, x_all, w_all, mixed, grads, moved, carried, experts, q_cols, k_cols, slots, exchange):
     E, quads = lax.axis_size("expert"), lax.axis_size("q")
     dp = quads * QUAD
     rows_here, width = tokens.shape
@@ -1065,13 +1141,15 @@
         M((rows_here, width), BF16),
         M((dp, share, total), BF16), second[0],
         M((2, quads, QUAD, share, total // 2), BF16), second[1], M((E, shard, total), BF16)]
-    scratch += [sem((4,))] * 6 + [sem((2, quads, 4))] * 4 + [sem((4,))] * 2
-    return pl.pallas_call(functools.partial(back_kernel, (experts, q_cols, k_cols, slots), exchange),
-        out_shape=outs, in_specs=[V] * 8 + [A] + [V] * 7 + [A] * 4, out_specs=(V,) * len(outs), scratch_shapes=scratch,
+    scratch += [sem((4,))] * 6 + [sem((2, quads, 4))] * 4 + [sem((4,))] * 2 + [sem(moved.shape[:3])] * 2
+    outs += (S(moved.shape, moved.dtype),)
+    return pl.pallas_call(functools.partial(back_kernel, (experts, q_cols, k_cols, slots), exchange, carried),
+        out_shape=outs, in_specs=[V] * 8 + [A] + [V] * 7 + [A] * 6, out_specs=(V,) * (len(outs) - 1) + (A,), scratch_shapes=scratch,
+        input_output_aliases={21: len(outs) - 1},
         compiler_params=pltpu.CompilerParams(vmem_limit_bytes=60 << 20, collective_id=5, has_side_effects=True),
         cost_estimate=CHEAP,
         name="backward")(dr_sum, dg_back, probs, h2, middle, cotangent, gains, tokens, out_full, query, key, value, log_total,
-            cosine, sine, segments.reshape(1, -1), h1_all, x_all, w_all, mixed)
+            cosine, sine, segments.reshape(1, -1), h1_all, x_all, w_all, mixed, grads, moved)
 
 
 ALL = ("q", "rh", "rl", "expert")
@@ -1112,14 +1190,9 @@
         pieces = lax.all_to_all(pieces, "expert", split_axis=0, concat_axis=0, tiled=True)
         pieces = pieces.reshape(E * shard_rows, -1)
         out_part = lax.all_gather(w_out, ALL, axis=0, tiled=True)
-    dm_all = lax.all_gather(cotangent, GROUP, axis=0, tiled=True).reshape(
-        sources, rows_here, width
-    )
-    cosine, sine = rope_tables(jnp.arange(length, dtype=jnp.int32), HD)
-    cosine = jnp.tile(cosine, (1, 4))
-    sine = jnp.tile(jnp.concatenate([-sine, sine], axis=1), (1, 2))
-    (x_all, w_all, out_full, h1_all, query, key, value, mixed, log_total, middle, h2, table, probs, gains) = start_call(
-        tokens, pieces, out_part, routes, priority, segments, cosine, sine, experts, capacity, q_cols, k_cols, exchange
+    cosine, sine = (jnp.asarray(t) for t in rope_tables(length))
+    (x_all, w_all, out_full, h1_all, query, key, value, mixed, log_total, middle, h2, table, probs, gains, dm_all) = start_call(
+        tokens, pieces, out_part, cotangent, routes.T, priority.T, segments, cosine, sine, experts, capacity, q_cols, k_cols, exchange
     )
     qkv_cols = q_cols + 2 * k_cols
     dp = Q * R
@@ -1138,20 +1211,24 @@
         part = expert_call(rows, dm_rows, weight, whole, 1, *banks, scalars([R * whole + r // ways]), dp, ways)
         part_moved = lax.all_to_all(part[3], DP, split_axis=0, concat_axis=0, tiled=True)
     done.append(expert_call(rows, dm_rows, weight, 0, whole, *banks, scalars([r * whole + s for s in range(whole)]), dp, 1))
-    moved = [lax.all_to_all(done[0][3], DP, split_axis=0, concat_axis=0, tiled=True)]
+    grads = done[0][3]
     if rest:
         done.append(part)
-        moved.append(part_moved)
+    plan = carry_plan(Q, whole)
     y_rows, dr_rows, dg_rows = ([d[n] for d in done] for n in range(3))
-    dr_sum, dg_back = combine_rows(dr_rows, tables, dg_rows, capacity, 2)
+    dr_sum, dg_back, moved = combine_rows(dr_rows, tables, dg_rows, None, grads, None, plan[0], capacity, 2)
+    if rest:
+        (dr_sum, part_moved) = lax.optimization_barrier((dr_sum, part_moved))
     out = back_call(
         dr_sum, dg_back, probs, h2, middle, cotangent, gains, tokens, out_full, query, key, value, log_total,
-        cosine, sine, segments, h1_all, x_all, w_all, mixed, experts, q_cols, k_cols, slots, exchange
+        cosine, sine, segments, h1_all, x_all, w_all, mixed, grads, moved, plan[1],
+        experts, q_cols, k_cols, slots, exchange
     )
+    moved = out[-1]
     if exchange:
-        grad_tokens, grad_query, grad_key, grad_value, small_own, out_sum = out
+        grad_tokens, grad_query, grad_key, grad_value, small_own, out_sum = out[:-1]
     else:
-        grad_tokens, qkv_sum, out_sum = out
+        grad_tokens, qkv_sum, out_sum = out[:-1]
         qkv_own = lax.all_to_all(
             qkv_sum.reshape(E, shard_rows, -1), "expert", split_axis=0, concat_axis=0, tiled=True
         )
@@ -1163,11 +1240,9 @@
         out_sum = lax.psum_scatter(out_sum, DP, scatter_dimension=0, tiled=True)
     perm = [(p * E + x, dp * x + p) for p in range(dp) for x in range(E)]
     out_own = lax.ppermute(out_sum, ALL, perm).astype(F32)
-    late = lax.optimization_barrier((tuple(y_rows), grad_tokens))
-    y_sum = combine_rows(list(late[0]), tables, None, capacity, 3)
-    outputs = (middle + y_sum).astype(BF16)
-    moved, _ = lax.optimization_barrier((moved, outputs))
-    gate_share, up_share, down_share = place_call(moved, local, ffn, width)
+    outputs, moved = combine_rows(y_rows, tables, None, middle, grads, moved, plan[2], capacity, 3)
+    order = jnp.stack([r ^ m for m in range(R)]).astype(jnp.int32)
+    gate_share, up_share, down_share = place_call(moved, [part_moved] if rest else [], order, local, ffn, width)
     return (
         outputs,
         grad_tokens,

time: 751 us -> 636 us (0.85)
  Pallas kernels: 683 us -> 606 us
  waiting for transfers between devices: 13.6 us -> 0.01 us
  between operations: 14.4 us -> 1.01 us
    pallas_call x2, Pallas kernels: 267 us -> 198 us  [combine_rows(): pl.pallas_call(functools.partial(combine_kernel, banks, slots, capacity,...]
    pallas_call x1, Pallas kernels: 149 us -> 131 us  [start_call(): pl.pallas_call(kernel, out_shape=(S((length, width), BF16), S((width, tot...]
    all_to_all x1, waiting for transfers between devices: 12.9 us -> 0.01 us  [shards(): lax.all_to_all(part[3], DP, split_axis=0, concat_axis=0, tiled=True)]
    pallas_call x1, Pallas kernels: 124 us -> 137 us  [back_call(): pl.pallas_call(functools.partial(back_kernel, (experts, q_cols, k_cols, s...]
  transfers between devices with their start and end apart: 4 -> 2, of which waited for: 1 -> 0; matrix products, arithmetic and copies ran while one was open for 2% -> 0% of each run, Pallas kernels for 78% -> 40%
where the time goes in v4:
time: 636 us; the launch traced here: 627 us
  Pallas kernels  606 us (95%)
  local copies, waits for them, and re-layouts  8.79 us (1%)
  starting transfers between devices  7.17 us (1%)
    pallas_call x2, Pallas kernels, combine_rows(): pl.pallas_call(functools.partial(combine_kernel, banks, slots, capacity,...  198 us
    pallas_call x1, Pallas kernels, back_call(): pl.pallas_call(functools.partial(back_kernel, (experts, q_cols, k_cols, s...  137 us
    pallas_call x1, Pallas kernels, start_call(): pl.pallas_call(kernel, out_shape=(S((length, width), BF16), S((width, tot...  131 us
    pallas_call x1, Pallas kernels, gather_rows(): pl.pallas_call(functools.partial(gather_kernel, slots, capacity), out_sha...  72.1 us
    pallas_call x2, Pallas kernels, expert_call(): pl.pallas_call(functools.partial(expert_kernel, chunks, dp, ways), grid_s...  57.2 us
  transfers between devices with their start and end apart: 2, of which 0 were waited for; matrix products, arithmetic and copies ran while one was open for 0% of the time, Pallas kernels for 40%

profile of v4, /device:TPU:0, one launch (start us, length us, event | category | flops | bytes accessed | tf_op | source)
XLA Modules:
  0.0 626.9 jit_solution(16201498858285872288)
XLA Ops:
  0.6 0.0 copy-start
  0.7 1.3 reshape.44.refs_6_.refs_15_
  2.0 0.7 pad_maximum_fusion
  2.7 0.1 copy.38
  2.8 0.9 copy.45
  3.8 0.6 pad_add_fusion.1.s_ref
  4.4 0.0 copy-done
  4.4 0.8 copy_bitcast_fusion.1
  5.2 0.7 maximum_bitcast_fusion.refs_1_
  6.0 131.5 %start.1 = (bf16[1280,1536]{1,0:T(8,128)(2,1)}, bf16[1536,768]{1,0:T(8,128)(2,1)}, bf16[1536,1536]{1,0:T(8,128)(2,1)}, bf16[1280,1536]{1,0:T(8,128)(2,1)}, bf16[...) custom-call(bf16[320,1536]{1,0:T(8,128)(2,1)} %refs_7_.2, ...), custom_call_target="tpu_custom_call" | custom-call | flops 1048576 | bytes 65536 | tf_op jit(solution)/shard_map/start/pallas_call | solution.py:835
  137.4 72.1 %gather_rows.1 = (bf16[3,1024,1536]{2,1,0:T(8,128)(2,1)}, bf16[3,1024,1536]{2,1,0:T(8,128)(2,1)}, f32[3,1024,1]{2,1,0:T(8,128)}, f32[16,8,320]{2,1,0:T(8,128)}) custom-call(bf16[320,1536]{1,0:T(8,128)(2,1)} %get-tuple-element.56.h2_ref.refs_3_, f32[16,8,320]{2,1,0:T(8,128)} %get-tuple-element.57.table_ref, bf16[16,320,1536]{2,1,0:T(8,128)(2,1)} %get-tuple-element.58.dm_ref), custom_call_target="tpu_custom_call" | custom-call | flops 1048576 | bytes 65536 | tf_op jit(solution)/shard_map/gather_rows/pallas_call | solution.py:206
  209.5 16.8 %expert_part.1 = (bf16[1,1024,1536]{2,1,0:T(8,128)(2,1)}, bf16[1,1024,1536]{2,1,0:T(8,128)(2,1)}, f32[1,1024,1]{2,1,0:T(8,128)}, bf16[8,1,576,256]{3,2,1,0:T(8,128)(2,1)}) custom-call(s32[2]{0:T(128)} %pad_add_fusion.1.s_ref, bf16[3,1024,1536]{2,1,0:T(8,128)(2,1)} %get-tuple-element.59.x_ref, bf16[3,1024,1536]{2,1,0:T(8,128)(2,1)} %get-tuple-element.60.dm_ref, ...), custom_call_target="tpu_custom_call" | custom-call | flops 1048576 | bytes 65536 | tf_op jit(solution)/shard_map/expert_part/pallas_call | solution.py:280
  226.3 5.5 all-to-all-start
  231.7 0.6 pad_add_fusion.s_ref
  232.3 40.4 %experts.1 = (bf16[2,1024,1536]{2,1,0:T(8,128)(2,1)}, bf16[2,1024,1536]{2,1,0:T(8,128)(2,1)}, f32[2,1024,1]{2,1,0:T(8,128)}, bf16[8,2,576,512]{3,2,1,0:T(8,128)(2,1)}) custom-call(s32[3]{0:T(128)} %pad_add_fusion.s_ref, bf16[3,1024,1536]{2,1,0:T(8,128)(2,1)} %get-tuple-element.59.x_ref, bf16[3,1024,1536]{2,1,0:T(8,128)(2,1)} %get-tuple-element.60.dm_ref, ...), custom_call_target="tpu_custom_call" | custom-call | flops 1048576 | bytes 65536 | tf_op jit(solution)/shard_map/experts/pallas_call | solution.py:280
  272.7 93.4 %combine_with_dg.1 = (f32[320,1536]{1,0:T(8,128)}, f32[16,8,320]{2,1,0:T(8,128)}, bf16[2,4,2,576,512]{4,3,2,1,0:T(8,128)(2,1)}) custom-call(bf16[2,1024,1536]{2,1,0:T(8,128)(2,1)} %get-tuple-element.67.refs_0_, bf16[1,1024,1536]{2,1,0:T(8,128)(2,1)} %get-tuple-element.68.refs_1_, f32[16,8,320]{2,1,0:T(8,128)} %get-tuple-element.64.refs_2_, ...), custom_call_target="tpu_custom_call" | custom-call | flops 1048576 | bytes 65536 | tf_op jit(solution)/shard_map/combine_with_dg/pallas_call | solution.py:512
  366.1 0.0 all-to-all-done
  366.1 0.0 copy-start.2
  366.1 136.5 %backward.1 = (f32[320,1536]{1,0:T(8,128)}, f32[48,1536]{1,0:T(8,128)}, f32[48,512]{1,0:T(8,128)}, f32[48,512]{1,0:T(8,128)}, f32[48,128]{1,0:T(8,128)}, /*index...) custom-call(f32[320,1536]{1,0:T(8,128)} %get-tuple-element.73.refs_0_, ...), custom_call_target="tpu_custom_call", output_to_operand_aliasing={{6}: (21, {})} | custom-call | flops 1048576 | bytes 65536 | tf_op jit(solution)/shard_map/backward/pallas_call | solution.py:1146
  502.7 0.0 copy-done.2
  502.7 1.7 collective-permute-start
  504.4 0.6 pad_add_fusion.2.order_ref
  505.0 0.0 copy-start.6
  505.0 104.3 %combine_rows.1 = (bf16[320,1536]{1,0:T(8,128)(2,1)}, bf16[2,4,2,576,512]{4,3,2,1,0:T(8,128)(2,1)}) custom-call(bf16[2,1024,1536]{2,1,0:T(8,128)(2,1)} %get-tuple-element.62.refs_0_, bf16[1,1024,1536]{2,1,0:T(8,128)(2,1)} %get-tuple-element.63.refs_1_, f32[16,8,320]{2,1,0:T(8,128)} %get-tuple-element.64.refs_2_, ...), custom_call_target="tpu_custom_call", output_to_operand_aliasing={{1}: (5, {})} | custom-call | flops 1048576 | bytes 65536 | tf_op jit(solution)/shard_map/combine_rows/pallas_call | solution.py:512
  609.3 0.0 copy-done.6
  609.3 0.7 copy.37
  610.0 0.0 copy-start.4
  610.0 0.0 copy-start.3
  610.0 0.0 copy-start.1
  610.0 11.1 %place_gradients.1 = (f32[10,192,512]{2,1,0:T(8,128)}, f32[10,192,512]{2,1,0:T(8,128)}, f32[10,64,1536]{2,1,0:T(8,128)}) custom-call(s32[4]{0:T(128)} %pad_add_fusion.2.order_ref, bf16[2,4,2,576,512]{4,3,2,1,0:T(8,128)(2,1)} %get-tuple-element.95.refs_0_, bf16[2,4,1,576,256]{4,3,2,1,0:T(8,128)(2,1)} %bitcast.30), custom_call_target="tpu_custom_call" | custom-call | flops 1048576 | bytes 65536 | tf_op jit(solution)/shard_map/place_gradients/pallas_call | solution.py:340
  621.1 0.0 copy-start.5
  621.1 0.0 copy-start.8
  621.1 0.0 copy-start.7
  621.1 0.7 slice_reduce_fusion
  621.8 0.0 collective-permute-done
  621.8 0.7 convert_element_type.5
  622.5 0.0 copy-done.4
  622.5 0.9 copy.53
  623.5 0.0 copy-done.3
  623.5 1.3 copy.54
  624.8 0.0 copy-done.5
  624.8 0.7 copy.55
  625.5 0.0 copy-done.8
  625.5 0.6 copy.56
  626.1 0.0 copy-done.7
  626.1 0.6 copy.57
  626.8 0.0 copy-done.1
  (2 shorter events, 0.0 us)
Async XLA Ops:
  0.6 3.7 copy-start
  226.3 139.9 %all-to-all-start = ((bf16[8,1,576,256]{3,2,1,0:T(8,128)(2,1)}), bf16[8,1,576,256]{3,2,1,0:T(8,128)(2,1)S(1)}, u32[]{:S(2)}, u32[]{:S(2)}) async-start(bf16[8,1,576,256]{3,2,1,0:T(8,128)(2,1)} %get-tuple-element.72), calls=%async_computation | async-start | bytes 4718592 | tf_op jit(solution)/shard_map/all_to_all | solution.py:1212
  366.1 136.5 %copy-start.2 = (bf16[8,1,576,256]{3,2,1,0:T(8,128)(2,1)}, bf16[8,1,576,256]{3,2,1,0:T(8,128)(2,1)S(1)}, u32[]{:S(2)}) copy-start(bf16[8,1,576,256]{3,2,1,0:T(8,128)(2,1)S(1)} %all-to-all-done) | copy-start | bytes 7077892
  502.7 119.1 %collective-permute-start = (bf16[48,1536]{1,0:T(8,128)(2,1)}, bf16[48,1536]{1,0:T(8,128)(2,1)S(1)}, u32[]{:S(2)}, u32[]{:S(2)}) collective-permute-start(bf16[48,1536]{1,0:T(8,128)(2,1)} %get-tuple-element.93), channel_id=1, source_target_pairs={{0,0},{1,8},{2,16},{3,24},{4,1},{5,9},{6,17},{7,25},{8,2},{9,10},{... | collective-permute-start | bytes 442376 | tf_op jit(solution)/shard_map/ppermute | solution.py:1242
  505.0 104.3 %copy-start.6 = (f32[48,128]{1,0:T(8,128)S(1)}, f32[48,128]{1,0:T(8,128)}, u32[]{:S(2)}) copy-start(f32[48,128]{1,0:T(8,128)} %get-tuple-element.94) | copy-start | bytes 73732
  610.0 12.5 %copy-start.4 = (bf16[320,1536]{1,0:T(8,128)(2,1)S(1)}, bf16[320,1536]{1,0:T(8,128)(2,1)}, u32[]{:S(2)}) copy-start(bf16[320,1536]{1,0:T(8,128)(2,1)} %get-tuple-element.140) | copy-start | bytes 2949124
  610.0 13.5 %copy-start.3 = (f32[320,1536]{1,0:T(8,128)S(1)}, f32[320,1536]{1,0:T(8,128)}, u32[]{:S(2)}) copy-start(f32[320,1536]{1,0:T(8,128)} %get-tuple-element.141) | copy-start | bytes 5898244
  610.0 16.7 %copy-start.1 = (bf16[48,512]{1,0:T(8,128)(2,1)S(1)}, bf16[48,512]{1,0:T(8,128)(2,1)}, u32[]{:S(2)}) copy-start(bf16[48,512]{1,0:T(8,128)(2,1)} %param.19) | copy-start | bytes 147460
  621.1 3.7 copy-start.5
  621.1 4.4 copy-start.8
  621.1 5.0 copy-start.7

commit v5 on v4

--- a/solution.py
+++ b/solution.py
@@ -53,7 +53,8 @@
 MESH=pl.DeviceIdType.MESH
 CORE = 1
 GATHER_ORDERS = ((2, 4, 8), (4, 8, 2), (8, 2, 4))
-SUM_ORDERS = ((4, 2, 8), (2, 4, 8))
+SUM_ORDERS = ((2, 4, 8), (4, 8, 2), (8, 2, 4))
+LAST_ORDERS = ((4, 2, 8), (2, 4, 8))
 
 def member_r():
     return lax.axis_index("rh") * 2 + lax.axis_index("rl")
@@ -87,21 +88,21 @@
 def greet(masks):
     greet_devices([group_device(mask) for mask in masks])
 
-DM_ORDERS = ((2, 4, 8), (2, 8, 4))
+DM_ORDERS = ((2, 4, 8), (4, 8, 2), (8, 2, 4))
 
 def last_hop(order, mask):
     if mask & CORE:
         return CORE
     return [bit for bit in order if mask & bit][-1]
 
-def block_copies(own_ref, held_ref, orders, send, recv):
-    part_width = own_ref.shape[1] // len(orders)
+def block_copies(own_ref, held_ref, orders, send, recv, first=0, last=None):
+    part_width = ((last or own_ref.shape[1]) - first) // len(orders)
     copies = {}
     for p, order in enumerate(orders):
         columns = pl.ds(p * part_width, part_width)
         for mask in range(1, 16):
             hop = last_hop(order, mask)
-            source = own_ref.at[:, columns] if mask == hop else held_ref.at[mask ^ hop, :, columns]
+            source = own_ref.at[:, pl.ds(first + p * part_width, part_width)] if mask == hop else held_ref.at[mask ^ hop, :, columns]
             copies[p, mask] = pltpu.make_async_remote_copy(source, held_ref.at[mask, :, columns], send.at[p, mask], recv.at[p, mask],
                 device_id=group_device(hop), device_id_type=MESH)
     return copies
@@ -353,37 +354,55 @@
     ms = (1, 3) if with_x else (0, 2)
     return [(s, k, m) for s in slots for m in ms for k in range(quads) if (k, m) != (0, 0)]
 
-def carry_copies(grads_ref, moved_ref, keys, send, recv):
+def carry_copies(grads_ref, moved_ref, carried, send, recv):
     quads = lax.axis_size("q")
     copies = []
-    for s, k, m in keys:
+    for s, k, m, _ in carried:
         q, r = (lax.axis_index("q") + k) % quads, flip(member_r(), m)
         copies.append(pltpu.make_async_remote_copy(grads_ref.at[place_at(q, r), s], moved_ref.at[s, m, (quads - k) % quads],
             send.at[s, m, k], recv.at[s, m, (quads - k) % quads], device_id=relative_device(k, m), device_id_type=MESH))
     return copies
 
-def carry_start(copies, keys, late):
-    outer = lax.axis_index("q") % 2 == lax.axis_index("rh")
-    for copy, (_, k, _m) in zip(copies, keys):
-        if not k:
+def is_outer():
+    return lax.axis_index("q") % 2 == lax.axis_index("rh")
+
+def carry_start(copies, carried, late):
+    for copy, (_, k, _, who) in zip(copies, carried):
+        if who != "all":
+            if not late:
+                pl.when(is_outer() if who == "outer" else jnp.logical_not(is_outer()))(copy.start)
+        elif not k:
             if not late:
                 copy.start()
         elif late:
-            pl.when(jnp.logical_not(outer))(copy.start)
+            pl.when(jnp.logical_not(is_outer()))(copy.start)
         else:
-            pl.when(outer)(copy.start)
+            pl.when(is_outer())(copy.start)
+
+def carry_wait(copies, carried):
+    for copy, (_, _, _, who) in zip(copies, carried):
+        if who == "all":
+            copy.wait()
+        else:
+            pl.when(is_outer() if who == "outer" else jnp.logical_not(is_outer()))(copy.wait)
 
 def carry_plan(quads, whole):
-    z, x = carry_keys(quads, range(whole), False), carry_keys(quads, range(whole), True)
-    first = [key for key in z if key[0] == 0]
-    second = [key for key in x if key[0] == 0 or key[1] == 0] + [key for key in z if key[0] and (key[1] == 0 or key[2] == 0)]
-    third = [key for key in x + z if key not in first and key not in second]
+    first, second, third = [], [], []
+    for key in carry_keys(quads, range(whole), False) + carry_keys(quads, range(whole), True):
+        s, k, m = key
+        rest = third if s and (k or m == 2) else second
+        if m == 2 and k % 2:
+            first.append(key + ("inner",))
+            rest.append(key + ("outer",))
+        else:
+            rest.append(key + ("all",))
     return first, second, third
 
-def first_hop(part, mask):
-    return [bit for bit in SUM_ORDERS[part] if mask & bit][0]
+def first_hop(order, mask):
+    return [bit for bit in order if mask & bit][0]
 
 def combine_kernel(banks, slots, capacity, with_dg, carried, *refs):
+    orders = SUM_ORDERS if with_dg else LAST_ORDERS
     rows, refs = refs[:banks], refs[banks:]
     tables_ref, refs = refs[0], refs[1:]
     if with_dg:
@@ -395,9 +414,9 @@
     if with_dg:
         dg_hold, dg_in, dg_send, dg_recv = refs[11:]
     width = out_ref.shape[1]
-    part_width = width // len(SUM_ORDERS)
+    part_width = width // len(orders)
     masks = list(range(1, 16)) if with_dg else [1, 2, 4, 8]
-    far = sorted({(k, m) for _, k, m in carried if k or m * 4 not in masks})
+    far = sorted({(k, m) for _, k, m, _ in carried if k or m * 4 not in masks})
     greet_devices([group_device(mask) for mask in masks] + [relative_device(k, m) for k, m in far])
     carries = carry_copies(grads_ref, moved_ref, carried, carry_send, carry_recv)
     straight = [n for n, key in enumerate(carried) if not key[2] & 1]
@@ -442,18 +461,18 @@
         core[mask].start()
         dg_step(mask | CORE, hot)
     copies = {}
-    for p in range(len(SUM_ORDERS)):
+    for p in range(len(orders)):
         for mask in range(2, 16, 2):
             copies[p, mask] = pltpu.make_async_remote_copy(held.at[p, mask // 2], got.at[p, mask // 2], send.at[p, mask // 2],
-                recv.at[p, mask // 2], device_id=group_device(first_hop(p, mask)), device_id_type=MESH)
+                recv.at[p, mask // 2], device_id=group_device(first_hop(orders[p], mask)), device_id_type=MESH)
     for mask in listed:
         hot = hots(mask)
         own = block_sum(mask, hot)
         core[mask].wait_recv()
         own = (own + core_in[mask // 2].astype(F32)).astype(BF16)
-        for p in range(len(SUM_ORDERS)):
+        for p in range(len(orders)):
             held[p, mask // 2] = own[:, p * part_width:(p + 1) * part_width]
-            if mask & SUM_ORDERS[p][0]:
+            if mask & orders[p][0]:
                 copies[p, mask].start()
         dg_step(mask, hot)
     carry(turning, False)
@@ -468,15 +487,15 @@
         held[p, target // 2] = add(p, target, sources).astype(BF16)
         copies[p, target].start()
     for both in (True, False):
-        for p in range(len(SUM_ORDERS)):
-            a, b, c = SUM_ORDERS[p]
+        for p in range(len(orders)):
+            a, b, c = orders[p]
             target = b | c if both else b
             forward(p, target, [target | a])
-    for p in range(len(SUM_ORDERS)):
-        a, b, c = SUM_ORDERS[p]
+    for p in range(len(orders)):
+        a, b, c = orders[p]
         forward(p, c, [c | a, c | b])
-    for p in range(len(SUM_ORDERS)):
-        a, b, c = SUM_ORDERS[p]
+    for p in range(len(orders)):
+        a, b, c = orders[p]
         columns = pl.ds(p * part_width, part_width)
         total = add(p, 0, [a, b, c])
         out_ref[:, columns] = total if with_dg else (middle_ref[:, columns] + total).astype(BF16)
@@ -492,8 +511,7 @@
         core[mask].wait_send()
     for key in copies:
         copies[key].wait_send()
-    for copy in carries:
-        copy.wait()
+    carry_wait(carries, carried)
     for copy in own_copies:
         copy.wait()
 
@@ -507,7 +525,7 @@
     moved_shape = jax.ShapeDtypeStruct((whole, QUAD, quads) + grads.shape[2:], grads.dtype)
     table = pltpu.VMEM(tables.shape, F32)
     sem = pltpu.SemaphoreType.DMA
-    parts = len(SUM_ORDERS)
+    parts = len(SUM_ORDERS if with_dg else LAST_ORDERS)
     operands = list(rows) + [tables] + (list(dgs) + [grads] if with_dg else [middle, grads, moved])
     return pl.pallas_call(functools.partial(combine_kernel, banks, slots, capacity, with_dg, carried),
         out_shape=(out, jax.ShapeDtypeStruct(tables.shape, F32), moved_shape) if with_dg else (out, moved_shape),
@@ -621,6 +639,12 @@
         ws[pl.ds(pl.multiple_of(place * block_rows + e * shard_rows, 16), shard_rows), :] = pieces_ref[e]
     else:
         ws[pl.ds(mine, block_rows), :] = pieces_ref[...]
+    def out_rows(d, who):
+        return pl.ds(pl.multiple_of((d * E + who) * shard_rows, 16), shard_rows)
+    if exchange:
+        y_copy = pltpu.make_async_remote_copy(wout_ref, wouts.at[out_rows(place, e)], wx_send.at[0, 3], wx_recv.at[0, 3],
+            device_id=device_at(q, r, flip(e, 2)), device_id_type=MESH)
+        y_copy.start()
     x_copies[2].start()
     x_copies[1].start()
     for p in range(len(DM_ORDERS)):
@@ -634,14 +658,17 @@
         copy.wait_recv()
     for p in range(3):
         dp_start(w_copies, (p, 0, 0))
-    wo_copies = {}
+    wo_copies = []
     if exchange:
-        def out_row(d):
-            return pl.multiple_of((d * E + e) * shard_rows, 16)
-        wouts[pl.ds(out_row(place), shard_rows), :] = wout_ref[...]
-        wo_copies = dp_copies(wouts, shard_rows, out_row, width // 3, wo_send, wo_recv)
+        wouts[out_rows(place, e), :] = wout_ref[...]
+        for n, who in enumerate((e, flip(e, 2))):
+            wo_copies.append(dp_copies(wouts, shard_rows, lambda d, who=who: pl.multiple_of((d * E + who) * shard_rows, 16),
+                width // 3, wo_send.at[n], wo_recv.at[n]))
         for p in range(3):
-            dp_start(wo_copies, (p, 0, 0))
+            dp_start(wo_copies[0], (p, 0, 0))
+        y_copy.wait_recv()
+        for p in range(3):
+            dp_start(wo_copies[1], (p, 0, 0))
 
     lane = lax.broadcasted_iota(jnp.int32, (rows_here, 128), 1)
     rank = jnp.zeros((rows_here, 128), jnp.int32)
@@ -663,7 +690,7 @@
     x_copies[2].wait_recv()
     x_copies[3].start()
     order = dp_order(w_copies)
-    wo_order = dp_order(wo_copies)
+    wo_order = dp_order(wo_copies[0]) if exchange else []
     for key in order:
         w_copies[key].wait_recv()
         dp_start(w_copies, key)
@@ -676,40 +703,26 @@
     wx_copies = {}
     if exchange:
         for d in range(dp):
-            for j in (1, 2, 3):
-                owner = e if j < 3 else flip(e, 2)
-                rows = pl.ds(pl.multiple_of((d * E + owner) * shard_rows, 16), shard_rows)
-                wx_copies[d, j] = pltpu.make_async_remote_copy(wouts.at[rows], wouts.at[rows], wx_send.at[d, j], wx_recv.at[d, j],
-                    device_id=device_at(q, r, flip(e, j if j < 3 else 1)), device_id_type=MESH)
+            for n, who in enumerate((e, flip(e, 2))):
+                block_ref = wouts.at[out_rows(d, who)]
+                wx_copies[d, n] = pltpu.make_async_remote_copy(block_ref, block_ref, wx_send.at[d, n], wx_recv.at[d, n],
+                    device_id=device_at(q, r, flip(e, 1)), device_id_type=MESH)
     def out_step(step):
-        if step == 2:
+        half = -(-len(wo_order) // 2)
+        if step < 2:
+            for key in wo_order[step * half:(step + 1) * half]:
+                for some in wo_copies:
+                    some[key].wait_recv()
+                    dp_start(some, key)
+        if step == 1:
+            for p, mask in dm_order:
+                if mask in (4, 8):
+                    dm_copies[p, mask].start()
+            for key in wx_copies:
+                wx_copies[key].start()
             dm_arrive([key for key in dm_order if key[1] == 2])
-        if step == 4:
+        if step == 3:
             dm_arrive([key for key in dm_order if key[1] in (4, 8)])
-        if not exchange:
-            if step == 1:
-                for p, (_, b, c) in enumerate(DM_ORDERS):
-                    dm_copies[p, b].start()
-                    dm_copies[p, c].start()
-            return
-        third = -(-len(wo_order) // 2)
-        if step < 2:
-            for key in wo_order[step * third:(step + 1) * third]:
-                wo_copies[key].wait_recv()
-                dp_start(wo_copies, key)
-        if step == 1:
-            for p, (_, b, c) in enumerate(DM_ORDERS):
-                dm_copies[p, b].start()
-            for p, (_, b, c) in enumerate(DM_ORDERS):
-                dm_copies[p, c].start()
-            for d in range(dp):
-                wx_copies[d, 2].start()
-            for d in range(dp):
-                wx_copies[d, 1].start()
-        if step == 3:
-            for d in range(dp):
-                wx_copies[d, 2].wait_recv()
-                wx_copies[d, 3].start()
 
     small = ws[:, total - 128:].astype(F32).T
     gain_attn = small[experts:experts + 1, :]
@@ -766,9 +779,8 @@
     h1_back = pltpu.make_async_copy(h1s, h1_ref, own_sem.at[2])
     h1_back.start()
     if exchange:
-        for d in range(dp):
-            wx_copies[d, 1].wait_recv()
-            wx_copies[d, 3].wait_recv()
+        for key in wx_copies:
+            wx_copies[key].wait_recv()
     else:
         fill = pltpu.make_async_copy(wout_ref, wouts, own_sem.at[3])
         fill.start()
@@ -814,8 +826,13 @@
         @pl.when(e != b)
         def _():
             o_descriptor(b).wait_send()
-    for copy in p_copies + list(x_copies.values()) + list(w_copies.values()) + list(wo_copies.values()) + list(wx_copies.values()):
+    for copy in p_copies + list(x_copies.values()) + list(w_copies.values()) + list(wx_copies.values()):
         copy.wait_send()
+    for some in wo_copies:
+        for key in some:
+            some[key].wait_send()
+    if exchange:
+        y_copy.wait_send()
     for copy in (x_back, w_back, h1_back, wout_back):
         copy.wait()
 
@@ -842,7 +859,7 @@
         scratch_shapes=[pltpu.VMEM((length, width), BF16), pltpu.VMEM((width, total), BF16), pltpu.VMEM((width, width), BF16),
             pltpu.VMEM((kv_heads, HD, length), BF16), pltpu.VMEM((length, width), BF16), pltpu.VMEM((E, rows_here, q_cols), BF16), sem((4,)),
             sem((4,)), sem((4,)), sem((4,)), sem((4,)), sem((3, quads, QUAD)), sem((3, quads, QUAD)), sem((E,)), sem((E,)),
-            sem((3, quads, QUAD)), sem((3, quads, QUAD)), sem((dp, 4)), sem((dp, 4)),
+            sem((2, 3, quads, QUAD)), sem((2, 3, quads, QUAD)), sem((dp, 4)), sem((dp, 4)),
             sem((len(DM_ORDERS), 16)), sem((len(DM_ORDERS), 16)), sem],
         compiler_params=pltpu.CompilerParams(vmem_limit_bytes=58 << 20, collective_id=4, has_side_effects=True),
         cost_estimate=CHEAP,
@@ -883,7 +900,7 @@
     for load in loads[:3]:
         load.start()
     near = [(0, 1), (0, 2)] + [(k, 0) for k in range(1, quads)]
-    far = sorted({(k, m) for _, k, m in carried} - set(near))
+    far = sorted({(k, m) for _, k, m, _ in carried} - set(near))
     greet_devices([device_at(q, r, flip(e, j)) for j in (1, 2, 3)] + [relative_device(k, m) for k, m in near + far])
     carries = carry_copies(grads_ref, moved_ref, carried, carry_send, carry_recv)
     carry_start(carries, carried, False)
@@ -1112,8 +1129,7 @@
             do_descriptor(b).wait_send()
     for copy in list(dat_copies.values()) + list(part_copies.values()) + list(copies.values()):
         copy.wait_send()
-    for copy in carries:
-        copy.wait()
+    carry_wait(carries, carried)
 
 def back_call(dr_sum, dg_back, probs, h2, middle, cotangent, gains, tokens, out_full, query, key, value, log_total,
               cosine, sine, segments, h1_all, x_all, w_all, mixed, grads, moved, carried, experts, q_cols, k_cols, slots, exchange):

time: 636 us -> 627 us (0.986)
  Pallas kernels: 606 us -> 597 us
    pallas_call x2, Pallas kernels: 198 us -> 178 us  [combine_rows(): pl.pallas_call(functools.partial(combine_kernel, banks, slots, capacity,...]
    pallas_call x1, Pallas kernels: 137 us -> 148 us  [back_call(): pl.pallas_call(functools.partial(back_kernel, (experts, q_cols, k_cols, s...]
  transfers between devices with their start and end apart: 2 -> 2, of which waited for: 0 -> 0; matrix products, arithmetic and copies ran while one was open for 0% -> 0% of each run, Pallas kernels for 40% -> 37%
where the time goes in v5:
time: 627 us; the launch traced here: 618 us
  Pallas kernels  597 us (95%)
  local copies, waits for them, and re-layouts  8.79 us (1%)
  starting transfers between devices  7.26 us (1%)
    pallas_call x2, Pallas kernels, combine_rows(): pl.pallas_call(functools.partial(combine_kernel, banks, slots, capacity,...  178 us
    pallas_call x1, Pallas kernels, back_call(): pl.pallas_call(functools.partial(back_kernel, (experts, q_cols, k_cols, s...  148 us
    pallas_call x1, Pallas kernels, start_call(): pl.pallas_call(kernel, out_shape=(S((length, width), BF16), S((width, tot...  130 us
    pallas_call x1, Pallas kernels, gather_rows(): pl.pallas_call(functools.partial(gather_kernel, slots, capacity), out_sha...  72.1 us
    pallas_call x2, Pallas kernels, expert_call(): pl.pallas_call(functools.partial(expert_kernel, chunks, dp, ways), grid_s...  57.2 us
  transfers between devices with their start and end apart: 2, of which 0 were waited for; matrix products, arithmetic and copies ran while one was open for 0% of the time, Pallas kernels for 37%

profile of v5, /device:TPU:0, one launch (start us, length us, event | category | flops | bytes accessed | tf_op | source)
XLA Modules:
  0.0 618.0 jit_solution(17862764502210660350)
XLA Ops:
  0.6 0.0 copy-start
  0.7 1.3 reshape.44.refs_6_.refs_15_
  2.0 0.7 pad_maximum_fusion
  2.7 0.1 copy.38
  2.8 0.9 copy.45
  3.8 0.6 pad_add_fusion.1.s_ref
  4.4 0.0 copy-done
  4.4 0.8 copy_bitcast_fusion.1
  5.2 0.7 maximum_bitcast_fusion.refs_1_
  6.0 130.2 %start.1 = (bf16[1280,1536]{1,0:T(8,128)(2,1)}, bf16[1536,768]{1,0:T(8,128)(2,1)}, bf16[1536,1536]{1,0:T(8,128)(2,1)}, bf16[1280,1536]{1,0:T(8,128)(2,1)}, bf16[...) custom-call(bf16[320,1536]{1,0:T(8,128)(2,1)} %refs_7_.2, ...), custom_call_target="tpu_custom_call" | custom-call | flops 1048576 | bytes 65536 | tf_op jit(solution)/shard_map/start/pallas_call | solution.py:852
  136.1 72.1 %gather_rows.1 = (bf16[3,1024,1536]{2,1,0:T(8,128)(2,1)}, bf16[3,1024,1536]{2,1,0:T(8,128)(2,1)}, f32[3,1024,1]{2,1,0:T(8,128)}, f32[16,8,320]{2,1,0:T(8,128)}) custom-call(bf16[320,1536]{1,0:T(8,128)(2,1)} %get-tuple-element.56.h2_ref.refs_3_, f32[16,8,320]{2,1,0:T(8,128)} %get-tuple-element.57.table_ref, bf16[16,320,1536]{2,1,0:T(8,128)(2,1)} %get-tuple-element.58.dm_ref), custom_call_target="tpu_custom_call" | custom-call | flops 1048576 | bytes 65536 | tf_op jit(solution)/shard_map/gather_rows/pallas_call | solution.py:207
  208.2 16.8 %expert_part.1 = (bf16[1,1024,1536]{2,1,0:T(8,128)(2,1)}, bf16[1,1024,1536]{2,1,0:T(8,128)(2,1)}, f32[1,1024,1]{2,1,0:T(8,128)}, bf16[8,1,576,256]{3,2,1,0:T(8,128)(2,1)}) custom-call(s32[2]{0:T(128)} %pad_add_fusion.1.s_ref, bf16[3,1024,1536]{2,1,0:T(8,128)(2,1)} %get-tuple-element.59.x_ref, bf16[3,1024,1536]{2,1,0:T(8,128)(2,1)} %get-tuple-element.60.dm_ref, ...), custom_call_target="tpu_custom_call" | custom-call | flops 1048576 | bytes 65536 | tf_op jit(solution)/shard_map/expert_part/pallas_call | solution.py:281
  225.0 5.5 all-to-all-start
  230.5 0.6 pad_add_fusion.s_ref
  231.1 40.4 %experts.1 = (bf16[2,1024,1536]{2,1,0:T(8,128)(2,1)}, bf16[2,1024,1536]{2,1,0:T(8,128)(2,1)}, f32[2,1024,1]{2,1,0:T(8,128)}, bf16[8,2,576,512]{3,2,1,0:T(8,128)(2,1)}) custom-call(s32[3]{0:T(128)} %pad_add_fusion.s_ref, bf16[3,1024,1536]{2,1,0:T(8,128)(2,1)} %get-tuple-element.59.x_ref, bf16[3,1024,1536]{2,1,0:T(8,128)(2,1)} %get-tuple-element.60.dm_ref, ...), custom_call_target="tpu_custom_call" | custom-call | flops 1048576 | bytes 65536 | tf_op jit(solution)/shard_map/experts/pallas_call | solution.py:281
  271.6 67.5 %combine_with_dg.1 = (f32[320,1536]{1,0:T(8,128)}, f32[16,8,320]{2,1,0:T(8,128)}, bf16[2,4,2,576,512]{4,3,2,1,0:T(8,128)(2,1)}) custom-call(bf16[2,1024,1536]{2,1,0:T(8,128)(2,1)} %get-tuple-element.67.refs_0_, bf16[1,1024,1536]{2,1,0:T(8,128)(2,1)} %get-tuple-element.68.refs_1_, f32[16,8,320]{2,1,0:T(8,128)} %get-tuple-element.64.refs_2_, ...), custom_call_target="tpu_custom_call" | custom-call | flops 1048576 | bytes 65536 | tf_op jit(solution)/shard_map/combine_with_dg/pallas_call | solution.py:530
  339.1 0.0 all-to-all-done
  339.1 0.0 copy-start.2
  339.1 148.3 %backward.1 = (f32[320,1536]{1,0:T(8,128)}, f32[48,1536]{1,0:T(8,128)}, f32[48,512]{1,0:T(8,128)}, f32[48,512]{1,0:T(8,128)}, f32[48,128]{1,0:T(8,128)}, /*index...) custom-call(f32[320,1536]{1,0:T(8,128)} %get-tuple-element.73.refs_0_, ...), custom_call_target="tpu_custom_call", output_to_operand_aliasing={{6}: (21, {})} | custom-call | flops 1048576 | bytes 65536 | tf_op jit(solution)/shard_map/backward/pallas_call | solution.py:1162
  487.4 0.0 copy-done.2
  487.4 1.7 collective-permute-start
  489.2 0.6 pad_add_fusion.2.order_ref
  489.8 0.0 copy-start.6
  489.8 110.6 %combine_rows.1 = (bf16[320,1536]{1,0:T(8,128)(2,1)}, bf16[2,4,2,576,512]{4,3,2,1,0:T(8,128)(2,1)}) custom-call(bf16[2,1024,1536]{2,1,0:T(8,128)(2,1)} %get-tuple-element.62.refs_0_, bf16[1,1024,1536]{2,1,0:T(8,128)(2,1)} %get-tuple-element.63.refs_1_, f32[16,8,320]{2,1,0:T(8,128)} %get-tuple-element.64.refs_2_, ...), custom_call_target="tpu_custom_call", output_to_operand_aliasing={{1}: (5, {})} | custom-call | flops 1048576 | bytes 65536 | tf_op jit(solution)/shard_map/combine_rows/pallas_call | solution.py:530
  600.4 0.0 copy-done.6
  600.4 0.7 copy.37
  601.1 0.0 copy-start.4
  601.1 0.0 copy-start.3
  601.1 0.0 copy-start.1
  601.1 11.1 %place_gradients.1 = (f32[10,192,512]{2,1,0:T(8,128)}, f32[10,192,512]{2,1,0:T(8,128)}, f32[10,64,1536]{2,1,0:T(8,128)}) custom-call(s32[4]{0:T(128)} %pad_add_fusion.2.order_ref, bf16[2,4,2,576,512]{4,3,2,1,0:T(8,128)(2,1)} %get-tuple-element.95.refs_0_, bf16[2,4,1,576,256]{4,3,2,1,0:T(8,128)(2,1)} %bitcast.30), custom_call_target="tpu_custom_call" | custom-call | flops 1048576 | bytes 65536 | tf_op jit(solution)/shard_map/place_gradients/pallas_call | solution.py:341
  612.2 0.0 copy-start.5
  612.2 0.0 copy-start.8
  612.2 0.0 copy-start.7
  612.2 0.7 slice_reduce_fusion
  612.9 0.0 collective-permute-done
  612.9 0.7 convert_element_type.5
  613.6 0.0 copy-done.4
  613.6 0.9 copy.53
  614.6 0.0 copy-done.3
  614.6 1.3 copy.54
  615.8 0.0 copy-done.5
  615.8 0.7 copy.55
  616.6 0.0 copy-done.8
  616.6 0.6 copy.56
  617.2 0.0 copy-done.7
  617.2 0.6 copy.57
  617.8 0.0 copy-done.1
  (2 shorter events, 0.0 us)
Async XLA Ops:
  0.6 3.7 copy-start
  225.0 114.1 %all-to-all-start = ((bf16[8,1,576,256]{3,2,1,0:T(8,128)(2,1)}), bf16[8,1,576,256]{3,2,1,0:T(8,128)(2,1)S(1)}, u32[]{:S(2)}, u32[]{:S(2)}) async-start(bf16[8,1,576,256]{3,2,1,0:T(8,128)(2,1)} %get-tuple-element.72), calls=%async_computation | async-start | bytes 4718592 | tf_op jit(solution)/shard_map/all_to_all | solution.py:1228
  339.1 148.3 %copy-start.2 = (bf16[8,1,576,256]{3,2,1,0:T(8,128)(2,1)}, bf16[8,1,576,256]{3,2,1,0:T(8,128)(2,1)S(1)}, u32[]{:S(2)}) copy-start(bf16[8,1,576,256]{3,2,1,0:T(8,128)(2,1)S(1)} %all-to-all-done) | copy-start | bytes 7077892
  487.4 125.4 %collective-permute-start = (bf16[48,1536]{1,0:T(8,128)(2,1)}, bf16[48,1536]{1,0:T(8,128)(2,1)S(1)}, u32[]{:S(2)}, u32[]{:S(2)}) collective-permute-start(bf16[48,1536]{1,0:T(8,128)(2,1)} %get-tuple-element.93), channel_id=1, source_target_pairs={{0,0},{1,8},{2,16},{3,24},{4,1},{5,9},{6,17},{7,25},{8,2},{9,10},{... | collective-permute-start | bytes 442376 | tf_op jit(solution)/shard_map/ppermute | solution.py:1258
  489.8 110.6 %copy-start.6 = (f32[48,128]{1,0:T(8,128)S(1)}, f32[48,128]{1,0:T(8,128)}, u32[]{:S(2)}) copy-start(f32[48,128]{1,0:T(8,128)} %get-tuple-element.94) | copy-start | bytes 73732
  601.1 12.5 %copy-start.4 = (bf16[320,1536]{1,0:T(8,128)(2,1)S(1)}, bf16[320,1536]{1,0:T(8,128)(2,1)}, u32[]{:S(2)}) copy-start(bf16[320,1536]{1,0:T(8,128)(2,1)} %get-tuple-element.140) | copy-start | bytes 2949124
  601.1 13.5 %copy-start.3 = (f32[320,1536]{1,0:T(8,128)S(1)}, f32[320,1536]{1,0:T(8,128)}, u32[]{:S(2)}) copy-start(f32[320,1536]{1,0:T(8,128)} %get-tuple-element.141) | copy-start | bytes 5898244
  601.1 16.7 %copy-start.1 = (bf16[48,512]{1,0:T(8,128)(2,1)S(1)}, bf16[48,512]{1,0:T(8,128)(2,1)}, u32[]{:S(2)}) copy-start(bf16[48,512]{1,0:T(8,128)(2,1)} %param.19) | copy-start | bytes 147460
  612.2 3.7 copy-start.5
  612.2 4.4 copy-start.8
  612.2 5.0 copy-start.7
